TPU v7x, 512 devices: a whole 4x4x16 slice. The times are simulated.
512 devices in a mesh: col: 64 (over y, z), row: 8 (over x, core).
Axes of the slice: x: 4, y: 4, z: 16, core: 2. Of those that a mesh axis runs over, the one named last changes fastest.
Arguments:
- ground: bfloat16 [512, 16, 4096], P('col'), may hold values from -0.21875 to 0.21875
- response: bfloat16 [512, 16, 4096], P('col'), may hold values from -6 to 6
- pattern: int32 [512, 16], replicated, may hold values from -1 to 511, as said below
Outputs:
- purified: bfloat16 [512, 16, 4096], P(('col', 'row'))
Inputs may be any that keep to these rules, and one draw needn't show every extreme that they name: `pattern`: slots [q * 2, (q + 1) * 2) of block row g list distinct block rows of class q whose column group is within 2 of g's column group, cyclically over 64 groups; live entries come first in each class, the rest are -1; every class of every block row has at least one live entry and some have 2; offsets of 2 occur.
All inputs are finite; a program needn't handle non-finite values.
Results may differ from a plain program's by a relative error of at most 0.017.
Values may be sent and summed in bfloat16 or wider, within the bound.
No kernel may reach another device: no remote copies, remote signals or barrier semaphores. Data moves between devices by JAX's collectives and lax.ppermute only.
A program may use at most 64 MiB of HBM per device.

v0:
```python
import jax
import jax.numpy as jnp
from jax import lax
from jax.sharding import PartitionSpec as P

BLK = 64
RB = 1
K8 = 2
REACH = 2


def from_behind(block, axis, distance):
    devices = range(lax.axis_size(axis))
    route = [((i - distance) % len(devices), i) for i in devices]
    return lax.ppermute(block, axis, route)


def surround(block, mover):
    pieces = []
    for step_off in range(-REACH, REACH + 1):
        if step_off == 0:
            pieces.append(block)
        else:
            pieces.append(mover(block, -step_off))
    return jnp.concatenate(pieces, axis=0)


def local(ground, response, pattern):
    col_size = lax.axis_size("col")
    group_rows = ground.shape[0]
    slot_count = ground.shape[1]
    block_cells = ground.shape[2]
    my_class = lax.axis_index("row")
    column = lax.axis_index("col")
    row_start = column * group_rows
    pat_rows = lax.dynamic_slice_in_dim(pattern, row_start, group_rows, 0)
    pat_left = lax.dynamic_slice_in_dim(pat_rows, my_class * K8, K8, 1)
    active = pat_left >= 0
    target = jnp.where(active, pat_left, 0)
    pat_far = pattern[target]
    hit_table = (pat_far[:, :, None, :] == pat_rows[:, None, :, None]) & (
        pat_far[:, :, None, :] >= 0
    )
    hit_table = hit_table & (pat_rows[:, None, :, None] >= 0) & active[:, :, None, None]
    slot_ids = jnp.arange(slot_count, dtype=jnp.int32)
    found_slot = jnp.sum(hit_table.astype(jnp.int32) * slot_ids, axis=-1)
    present = jnp.any(hit_table, axis=-1)
    far_group = target // group_rows
    rim_index = (far_group - column + REACH) % col_size * RB + target % RB
    flat_index = rim_index[:, :, None] * slot_count + found_slot

    def gather_right(rim_rows):
        picked = rim_rows.reshape(-1, block_cells)[flat_index]
        picked = jnp.where(present[..., None], picked, jnp.zeros((), picked.dtype))
        return picked.reshape(group_rows, K8, slot_count, BLK, BLK)

    def multiply(left_full, right_blocks):
        left_blocks = lax.dynamic_slice_in_dim(left_full, my_class * K8, K8, 1)
        left_blocks = jnp.where(active[..., None], left_blocks, jnp.zeros((), left_blocks.dtype))
        left_blocks = left_blocks.reshape(group_rows, K8, BLK, BLK)
        product = jnp.einsum(
            "gapq,gajqs->gjps", left_blocks, right_blocks, preferred_element_type=jnp.float32
        )
        return product.reshape(group_rows, slot_count, block_cells)

    own_ground = lax.dynamic_slice_in_dim(ground, my_class * RB, RB, 0)
    own_response = lax.dynamic_slice_in_dim(response, my_class * RB, RB, 0)
    ground_rows = surround(own_ground, lambda block, amount: from_behind(block, "col", amount))
    response_rows = surround(own_response, lambda block, amount: from_behind(block, "col", amount))
    ground_right = gather_right(ground_rows)
    mix_terms = multiply(response, ground_right) + multiply(ground, gather_right(response_rows))
    sq_terms = multiply(ground, ground_right)
    mixed, square = (
        lax.psum_scatter(
            mix_terms.astype(jnp.bfloat16), "row", scatter_dimension=0, tiled=True
        ).astype(jnp.float32),
        lax.psum_scatter(
            sq_terms.astype(jnp.bfloat16), "row", scatter_dimension=0, tiled=True
        ).astype(jnp.float32),
    )
    pair_rows = surround(
        jnp.concatenate([mixed.astype(jnp.bfloat16), square.astype(jnp.bfloat16)], axis=1),
        lambda block, amount: from_behind(block, "col", amount),
    )
    mixed_rows = pair_rows[:, :slot_count]
    square_rows = pair_rows[:, slot_count:]
    cubic_terms = multiply(response, gather_right(square_rows)) + multiply(
        ground, gather_right(mixed_rows)
    )
    cubic = lax.psum_scatter(
        cubic_terms.astype(jnp.bfloat16), "row", scatter_dimension=0, tiled=True
    ).astype(jnp.float32)
    return (3.0 * mixed - 2.0 * cubic).astype(jnp.bfloat16)


def solution(mesh):
    in_specs = (P("col", None, None), P("col", None, None), P())
    out_specs = P(("col", "row"), None, None)
    return jax.shard_map(local, mesh=mesh, in_specs=in_specs, out_specs=out_specs, check_vma=False)
```

profile of v0, /device:TPU:1, one launch (start us, length us, event | category | flops | bytes accessed | tf_op | source)
XLA Modules:
  0.0 292.7 jit_solution(8896566523253878533)
XLA Ops:
  7.5 5.7 %collective-permute-start.4 = (bf16[1,16,4096]{2,1,0:T(8,128)(2,1)S(1)}, bf16[1,16,4096]{2,1,0:T(8,128)(2,1)S(1)}, u32[]{:S(2)}, u32[]{:S(2)}) collective-permute-start(bf16[1,16,4096]{2,1,0:T(8,128)(2,1)S(1)} %constant_dynamic-slice_fusion), channel_id=1, source_target_pairs={{496,0},{504,8},{0,16},{8,24},{16,32},{24,40},{32,48},{40,56},{48,... | collective-permute-start | bytes 393224 | tf_op jit(solution)/shard_map/ppermute | solution.py:15
  13.2 3.5 %collective-permute-start.5 = (bf16[1,16,4096]{2,1,0:T(8,128)(2,1)S(1)}, bf16[1,16,4096]{2,1,0:T(8,128)(2,1)S(1)}, u32[]{:S(2)}, u32[]{:S(2)}) collective-permute-start(bf16[1,16,4096]{2,1,0:T(8,128)(2,1)S(1)} %constant_dynamic-slice_fusion), channel_id=1, source_target_pairs={{504,0},{0,8},{8,16},{16,24},{24,32},{32,40},{40,48},{48,56},{56,6... | collective-permute-start | bytes 393224 | tf_op jit(solution)/shard_map/ppermute | solution.py:15
  16.7 9.0 %collective-permute-start.6 = (bf16[1,16,4096]{2,1,0:T(8,128)(2,1)S(1)}, bf16[1,16,4096]{2,1,0:T(8,128)(2,1)S(1)}, u32[]{:S(2)}, u32[]{:S(2)}) collective-permute-start(bf16[1,16,4096]{2,1,0:T(8,128)(2,1)S(1)} %constant_dynamic-slice_fusion), channel_id=1, source_target_pairs={{8,0},{16,8},{24,16},{32,24},{40,32},{48,40},{56,48},{64,56},{72,6... | collective-permute-start | bytes 393224 | tf_op jit(solution)/shard_map/ppermute | solution.py:15
  25.7 4.3 %collective-permute-start.7 = (bf16[1,16,4096]{2,1,0:T(8,128)(2,1)S(1)}, bf16[1,16,4096]{2,1,0:T(8,128)(2,1)S(1)}, u32[]{:S(2)}, u32[]{:S(2)}) collective-permute-start(bf16[1,16,4096]{2,1,0:T(8,128)(2,1)S(1)} %constant_dynamic-slice_fusion), channel_id=1, source_target_pairs={{16,0},{24,8},{32,16},{40,24},{48,32},{56,40},{64,48},{72,56},{80,... | collective-permute-start | bytes 393224 | tf_op jit(solution)/shard_map/ppermute | solution.py:15
  44.1 6.4 %collective-permute-start.2 = (bf16[1,16,4096]{2,1,0:T(8,128)(2,1)}, bf16[1,16,4096]{2,1,0:T(8,128)(2,1)S(1)}, u32[]{:S(2)}, u32[]{:S(2)}) collective-permute-start(bf16[1,16,4096]{2,1,0:T(8,128)(2,1)} %constant_dynamic-slice_fusion.1), channel_id=1, source_target_pairs={{8,0},{16,8},{24,16},{32,24},{40,32},{48,40},{56,48},{64,56},{72,6... | collective-permute-start | bytes 393224 | tf_op jit(solution)/shard_map/ppermute | solution.py:15
  51.5 4.2 %collective-permute-start.3 = (bf16[1,16,4096]{2,1,0:T(8,128)(2,1)}, bf16[1,16,4096]{2,1,0:T(8,128)(2,1)}, u32[]{:S(2)}, u32[]{:S(2)}) collective-permute-start(bf16[1,16,4096]{2,1,0:T(8,128)(2,1)} %constant_dynamic-slice_fusion.1), channel_id=1, source_target_pairs={{16,0},{24,8},{32,16},{40,24},{48,32},{56,40},{64,48},{72,56},{80,... | collective-permute-start | bytes 393224 | tf_op jit(solution)/shard_map/ppermute | solution.py:15
  58.6 5.6 %gather.27 = bf16[8,2,16,64,64]{4,3,2,1,0:T(8,128)(2,1)} reshape(bf16[256,4096]{1,0:T(8,128)(2,1)S(1)} %gather_fusion.2) | data formatting | bytes 4194304 | tf_op jit(solution)/shard_map/gather | solution.py:53
  64.2 6.6 %copy.70 = bf16[8,2,16,64,64]{3,4,1,2,0:T(8,128)(2,1)} copy(bf16[8,2,16,64,64]{4,3,2,1,0:T(8,128)(2,1)} %gather.27) | data formatting | bytes 4194304 | tf_op jit(solution)/shard_map/gather | solution.py:53
  73.5 5.6 %gather.25 = bf16[8,2,16,64,64]{4,3,2,1,0:T(8,128)(2,1)} reshape(bf16[256,4096]{1,0:T(8,128)(2,1)S(1)} %gather_fusion.1) | data formatting | bytes 4194304 | tf_op jit(solution)/shard_map/gather | solution.py:53
  79.1 6.5 %copy.66 = bf16[8,2,16,64,64]{3,4,1,2,0:T(8,128)(2,1)} copy(bf16[8,2,16,64,64]{4,3,2,1,0:T(8,128)(2,1)} %gather.25) | data formatting | bytes 4194304 | tf_op jit(solution)/shard_map/gather | solution.py:53
  85.6 3.3 %fusion.6 = f32[8,16,64,64,1]{3,2,4,1,0:T(8,128)S(1)} fusion(bf16[8,2,16,64,64]{3,4,1,2,0:T(8,128)(2,1)} %copy.70, pred[8,2,16]{1,2,0:T(8,128)(4,1)S(1)} %copy.63, bf16[8,2,64,64]{3,2,0,1:T(8,128)(2,1)S(1)} %copy-done.4), kind=kOutput, calls=%fused_computation.14 | convolution fusion | flops 135266304 | bytes 4325632 | tf_op jit(solution)/shard_map/gapq,gajqs->gjps/dot_general | solution.py:61
  89.1 2.5 fusion.13
  91.6 3.0 %copy.73 = bf16[8,16,64,64]{3,2,1,0:T(8,128)(2,1)S(1)} copy(bf16[8,16,64,64]{2,3,1,0:T(8,128)(2,1)} %fusion.13) | data formatting | bytes 2097152 | tf_op jit(solution)/shard_map/convert_element_type | solution.py:75
  97.4 4.9 %fusion.14 = bf16[8,16,64,64]{2,3,1,0:T(8,128)(2,1)} fusion(bf16[8,2,16,64,64]{3,4,1,2,0:T(8,128)(2,1)} %copy.66, pred[8,2,16]{1,2,0:T(8,128)(4,1)S(1)} %copy.63, bf16[8,2,64,64]{3,2,0,1:T(8,128)(2,1)S(1)} %copy-done.4), kind=kOutput, calls=%fused_computation.23 | convolution fusion | flops 135790592 | bytes 3277056 | tf_op jit(solution)/shard_map/gapq,gajqs->gjps/dot_general | solution.py:61
  102.2 3.0 %copy.75 = bf16[8,16,64,64]{3,2,1,0:T(8,128)(2,1)S(1)} copy(bf16[8,16,64,64]{2,3,1,0:T(8,128)(2,1)} %fusion.14) | data formatting | bytes 2097152 | tf_op jit(solution)/shard_map/convert_element_type | solution.py:78
  105.3 2.5 convert_element_type.46
  107.8 23.1 %reduce-scatter.4.cloned.1.call-done = bf16[1,16,4096]{2,1,0:T(8,128)(2,1)} async-done(((bf16[8,16,4096]{2,1,0:T(8,128)(2,1)}), bf16[1,16,4096]{2,1,0:T(8,128)(2,1)}) %reduce-scatter.4.cloned.1.call-update) | async-done | bytes 131088 | tf_op jit(solution)/shard_map/reduce_scatter | solution.py:74
  131.8 40.4 %reduce-scatter.6.cloned.1.call-done = bf16[1,16,4096]{2,1,0:T(8,128)(2,1)} async-done(((bf16[8,16,4096]{2,1,0:T(8,128)(2,1)}), bf16[1,16,4096]{2,1,0:T(8,128)(2,1)}) %reduce-scatter.6.cloned.1.call-update) | async-done | bytes 131088 | tf_op jit(solution)/shard_map/reduce_scatter | solution.py:77
  173.2 3.2 %collective-permute-start.8 = (bf16[1,32,4096]{2,1,0:T(8,128)(2,1)S(1)}, bf16[1,32,4096]{2,1,0:T(8,128)(2,1)S(1)}, u32[]{:S(2)}, u32[]{:S(2)}) collective-permute-start(bf16[1,32,4096]{2,1,0:T(8,128)(2,1)S(1)} %constant_dynamic-update-slice_fusion.10), channel_id=1, source_target_pairs={{496,0},{504,8},{0,16},{8,24},{16,32},{24,40},{32,48},{40,56},{48,... | collective-permute-start | bytes 786440 | tf_op jit(solution)/shard_map/ppermute | solution.py:15
  176.4 3.2 %collective-permute-start.9 = (bf16[1,32,4096]{2,1,0:T(8,128)(2,1)S(1)}, bf16[1,32,4096]{2,1,0:T(8,128)(2,1)S(1)}, u32[]{:S(2)}, u32[]{:S(2)}) collective-permute-start(bf16[1,32,4096]{2,1,0:T(8,128)(2,1)S(1)} %constant_dynamic-update-slice_fusion.10), channel_id=1, source_target_pairs={{504,0},{0,8},{8,16},{16,24},{24,32},{32,40},{40,48},{48,56},{56,6... | collective-permute-start | bytes 786440 | tf_op jit(solution)/shard_map/ppermute | solution.py:15
  179.6 5.4 %collective-permute-start.10 = (bf16[1,32,4096]{2,1,0:T(8,128)(2,1)S(1)}, bf16[1,32,4096]{2,1,0:T(8,128)(2,1)S(1)}, u32[]{:S(2)}, u32[]{:S(2)}) collective-permute-start(bf16[1,32,4096]{2,1,0:T(8,128)(2,1)S(1)} %constant_dynamic-update-slice_fusion.10), channel_id=1, source_target_pairs={{8,0},{16,8},{24,16},{32,24},{40,32},{48,40},{56,48},{64,56},{72,6... | collective-permute-start | bytes 786440 | tf_op jit(solution)/shard_map/ppermute | solution.py:15
  185.0 3.2 %collective-permute-start.11 = (bf16[1,32,4096]{2,1,0:T(8,128)(2,1)S(1)}, bf16[1,32,4096]{2,1,0:T(8,128)(2,1)S(1)}, u32[]{:S(2)}, u32[]{:S(2)}) collective-permute-start(bf16[1,32,4096]{2,1,0:T(8,128)(2,1)S(1)} %constant_dynamic-update-slice_fusion.10), channel_id=1, source_target_pairs={{16,0},{24,8},{32,16},{40,24},{48,32},{56,40},{64,48},{72,56},{80,... | collective-permute-start | bytes 786440 | tf_op jit(solution)/shard_map/ppermute | solution.py:15
  188.2 8.1 %collective-permute-done.9 = bf16[1,32,4096]{2,1,0:T(8,128)(2,1)S(1)} collective-permute-done((bf16[1,32,4096]{2,1,0:T(8,128)(2,1)S(1)}, bf16[1,32,4096]{2,1,0:T(8,128)(2,1)S(1)}, u32[]{:S(2)}, u32[]{:S(2)}) %collective-permute-start.9) | collective-permute-done | bytes 262176 | tf_op jit(solution)/shard_map/ppermute | solution.py:15
  201.5 5.6 %gather.31 = bf16[8,2,16,64,64]{4,3,2,1,0:T(8,128)(2,1)} reshape(bf16[256,4096]{1,0:T(8,128)(2,1)S(1)} %gather_fusion.4) | data formatting | bytes 4194304 | tf_op jit(solution)/shard_map/gather | solution.py:53
  207.0 6.6 %copy.78 = bf16[8,2,16,64,64]{3,4,1,2,0:T(8,128)(2,1)} copy(bf16[8,2,16,64,64]{4,3,2,1,0:T(8,128)(2,1)} %gather.31) | data formatting | bytes 4194304 | tf_op jit(solution)/shard_map/gather | solution.py:53
  213.7 5.5 %fusion.2 = f32[8,16,64,64,1]{3,2,4,1,0:T(8,128)} fusion(bf16[8,2,16,64,64]{3,4,1,2,0:T(8,128)(2,1)} %copy.78, pred[8,2,16]{1,2,0:T(8,128)(4,1)S(1)} %copy.63, bf16[8,2,64,64]{3,2,0,1:T(8,128)(2,1)S(1)} %copy-done.5), kind=kOutput, calls=%fused_computation.10 | convolution fusion | flops 135266304 | bytes 4325632 | tf_op jit(solution)/shard_map/gapq,gajqs->gjps/dot_general | solution.py:61
  221.0 5.6 %gather.29 = bf16[8,2,16,64,64]{4,3,2,1,0:T(8,128)(2,1)} reshape(bf16[256,4096]{1,0:T(8,128)(2,1)S(1)} %gather_fusion.3) | data formatting | bytes 4194304 | tf_op jit(solution)/shard_map/gather | solution.py:53
  226.6 6.6 %copy.76 = bf16[8,2,16,64,64]{3,4,1,2,0:T(8,128)(2,1)} copy(bf16[8,2,16,64,64]{4,3,2,1,0:T(8,128)(2,1)} %gather.29) | data formatting | bytes 4194304 | tf_op jit(solution)/shard_map/gather | solution.py:53
  233.2 6.1 %fusion.15 = bf16[8,16,64,64]{2,3,1,0:T(8,128)(2,1)} fusion(f32[8,16,64,64,1]{3,2,4,1,0:T(8,128)} %fusion.2, bf16[8,2,16,64,64]{3,4,1,2,0:T(8,128)(2,1)} %copy.76, pred[8,2,16]{1,2,0:T(8,128)(4,1)S(1)} %copy.63, bf16[8,2,64,64]{3,2,0,1:T(8,128)(2,1)S(1)} %copy-done.2), kind=kOutput, calls=%fused_computation.24 | convolution fusion | flops 136314880 | bytes 5374208 | tf_op jit(solution)/shard_map/gapq,gajqs->gjps/dot_general | solution.py:61
  239.3 3.0 %copy.80 = bf16[8,16,64,64]{3,2,1,0:T(8,128)(2,1)S(1)} copy(bf16[8,16,64,64]{2,3,1,0:T(8,128)(2,1)} %fusion.15) | data formatting | bytes 2097152 | tf_op jit(solution)/shard_map/convert_element_type | solution.py:91
  242.4 2.5 convert_element_type.49
  244.9 39.7 %reduce-scatter.8.cloned.1.call-done = bf16[1,16,4096]{2,1,0:T(8,128)(2,1)} async-done(((bf16[8,16,4096]{2,1,0:T(8,128)(2,1)}), bf16[1,16,4096]{2,1,0:T(8,128)(2,1)}) %reduce-scatter.8.cloned.1.call-update) | async-done | bytes 131088 | tf_op jit(solution)/shard_map/reduce_scatter | solution.py:90
  (80 shorter events, 34.8 us)
Async XLA Ops:
  6.5 124.4 %reduce-scatter.4.cloned.1.call-start = ((), (), s32[]{:S(2)}) async-start(), calls=%async_computation.3 | async-start | bytes 1179648 | tf_op jit(solution)/shard_map/reduce_scatter | solution.py:74
  7.5 34.4 %collective-permute-start.4 = (bf16[1,16,4096]{2,1,0:T(8,128)(2,1)S(1)}, bf16[1,16,4096]{2,1,0:T(8,128)(2,1)S(1)}, u32[]{:S(2)}, u32[]{:S(2)}) collective-permute-start(bf16[1,16,4096]{2,1,0:T(8,128)(2,1)S(1)} %constant_dynamic-slice_fusion), channel_id=1, source_target_pairs={{496,0},{504,8},{0,16},{8,24},{16,32},{24,40},{32,48},{40,56},{48,... | collective-permute-start | bytes 393224 | tf_op jit(solution)/shard_map/ppermute | solution.py:15
  13.2 30.9 %collective-permute-start.5 = (bf16[1,16,4096]{2,1,0:T(8,128)(2,1)S(1)}, bf16[1,16,4096]{2,1,0:T(8,128)(2,1)S(1)}, u32[]{:S(2)}, u32[]{:S(2)}) collective-permute-start(bf16[1,16,4096]{2,1,0:T(8,128)(2,1)S(1)} %constant_dynamic-slice_fusion), channel_id=1, source_target_pairs={{504,0},{0,8},{8,16},{16,24},{24,32},{32,40},{40,48},{48,56},{56,6... | collective-permute-start | bytes 393224 | tf_op jit(solution)/shard_map/ppermute | solution.py:15
  16.7 39.9 %collective-permute-start.6 = (bf16[1,16,4096]{2,1,0:T(8,128)(2,1)S(1)}, bf16[1,16,4096]{2,1,0:T(8,128)(2,1)S(1)}, u32[]{:S(2)}, u32[]{:S(2)}) collective-permute-start(bf16[1,16,4096]{2,1,0:T(8,128)(2,1)S(1)} %constant_dynamic-slice_fusion), channel_id=1, source_target_pairs={{8,0},{16,8},{24,16},{32,24},{40,32},{48,40},{56,48},{64,56},{72,6... | collective-permute-start | bytes 393224 | tf_op jit(solution)/shard_map/ppermute | solution.py:15
  25.7 31.0 %collective-permute-start.7 = (bf16[1,16,4096]{2,1,0:T(8,128)(2,1)S(1)}, bf16[1,16,4096]{2,1,0:T(8,128)(2,1)S(1)}, u32[]{:S(2)}, u32[]{:S(2)}) collective-permute-start(bf16[1,16,4096]{2,1,0:T(8,128)(2,1)S(1)} %constant_dynamic-slice_fusion), channel_id=1, source_target_pairs={{16,0},{24,8},{32,16},{40,24},{48,32},{56,40},{64,48},{72,56},{80,... | collective-permute-start | bytes 393224 | tf_op jit(solution)/shard_map/ppermute | solution.py:15
  31.6 19.9 %collective-permute-start = (bf16[1,16,4096]{2,1,0:T(8,128)(2,1)}, bf16[1,16,4096]{2,1,0:T(8,128)(2,1)S(1)}, u32[]{:S(2)}, u32[]{:S(2)}) collective-permute-start(bf16[1,16,4096]{2,1,0:T(8,128)(2,1)} %constant_dynamic-slice_fusion.1), channel_id=1, source_target_pairs={{496,0},{504,8},{0,16},{8,24},{16,32},{24,40},{32,48},{40,56},{48,... | collective-permute-start | bytes 393224 | tf_op jit(solution)/shard_map/ppermute | solution.py:15
  41.9 13.8 %collective-permute-start.1 = (bf16[1,16,4096]{2,1,0:T(8,128)(2,1)}, bf16[1,16,4096]{2,1,0:T(8,128)(2,1)S(1)}, u32[]{:S(2)}, u32[]{:S(2)}) collective-permute-start(bf16[1,16,4096]{2,1,0:T(8,128)(2,1)} %constant_dynamic-slice_fusion.1), channel_id=1, source_target_pairs={{504,0},{0,8},{8,16},{16,24},{24,32},{32,40},{40,48},{48,56},{56,6... | collective-permute-start | bytes 393224 | tf_op jit(solution)/shard_map/ppermute | solution.py:15
  44.1 12.6 %collective-permute-start.2 = (bf16[1,16,4096]{2,1,0:T(8,128)(2,1)}, bf16[1,16,4096]{2,1,0:T(8,128)(2,1)S(1)}, u32[]{:S(2)}, u32[]{:S(2)}) collective-permute-start(bf16[1,16,4096]{2,1,0:T(8,128)(2,1)} %constant_dynamic-slice_fusion.1), channel_id=1, source_target_pairs={{8,0},{16,8},{24,16},{32,24},{40,32},{48,40},{56,48},{64,56},{72,6... | collective-permute-start | bytes 393224 | tf_op jit(solution)/shard_map/ppermute | solution.py:15
  51.5 19.3 %collective-permute-start.3 = (bf16[1,16,4096]{2,1,0:T(8,128)(2,1)}, bf16[1,16,4096]{2,1,0:T(8,128)(2,1)}, u32[]{:S(2)}, u32[]{:S(2)}) collective-permute-start(bf16[1,16,4096]{2,1,0:T(8,128)(2,1)} %constant_dynamic-slice_fusion.1), channel_id=1, source_target_pairs={{16,0},{24,8},{32,16},{40,24},{48,32},{56,40},{64,48},{72,56},{80,... | collective-permute-start | bytes 393224 | tf_op jit(solution)/shard_map/ppermute | solution.py:15
  79.1 6.5 %copy-start.4 = (bf16[8,2,64,64]{3,2,0,1:T(8,128)(2,1)S(1)}, bf16[8,2,64,64]{3,2,0,1:T(8,128)(2,1)}, u32[]{:S(2)}) copy-start(bf16[8,2,64,64]{3,2,0,1:T(8,128)(2,1)} %reshape.71) | copy-start | bytes 393220
  85.6 3.4 %copy-start = (bf16[8,2,16,64,64]{3,4,1,2,0:T(8,128)(2,1)S(1)}, bf16[8,2,16,64,64]{3,4,1,2,0:T(8,128)(2,1)}, u32[]{:S(2)}) copy-start(bf16[8,2,16,64,64]{3,4,1,2,0:T(8,128)(2,1)} %copy.66) | copy-start | bytes 6291460
  85.6 3.5 %copy-start.1 = (bf16[8,2,64,64]{3,2,0,1:T(8,128)(2,1)S(1)}, bf16[8,2,64,64]{3,2,0,1:T(8,128)(2,1)}, u32[]{:S(2)}) copy-start(bf16[8,2,64,64]{3,2,0,1:T(8,128)(2,1)} %reshape.69) | copy-start | bytes 393220
  97.2 75.1 %reduce-scatter.6.cloned.1.call-start = ((), (), s32[]{:S(2)}) async-start(), calls=%async_computation.4 | async-start | bytes 1179648 | tf_op jit(solution)/shard_map/reduce_scatter | solution.py:77
  107.8 176.8 %reduce-scatter.8.cloned.1.call-start = ((), (), s32[]{:S(2)}) async-start(), calls=%async_computation.5 | async-start | bytes 1179648 | tf_op jit(solution)/shard_map/reduce_scatter | solution.py:90
  173.2 15.0 %collective-permute-start.8 = (bf16[1,32,4096]{2,1,0:T(8,128)(2,1)S(1)}, bf16[1,32,4096]{2,1,0:T(8,128)(2,1)S(1)}, u32[]{:S(2)}, u32[]{:S(2)}) collective-permute-start(bf16[1,32,4096]{2,1,0:T(8,128)(2,1)S(1)} %constant_dynamic-update-slice_fusion.10), channel_id=1, source_target_pairs={{496,0},{504,8},{0,16},{8,24},{16,32},{24,40},{32,48},{40,56},{48,... | collective-permute-start | bytes 786440 | tf_op jit(solution)/shard_map/ppermute | solution.py:15
  176.4 20.0 %collective-permute-start.9 = (bf16[1,32,4096]{2,1,0:T(8,128)(2,1)S(1)}, bf16[1,32,4096]{2,1,0:T(8,128)(2,1)S(1)}, u32[]{:S(2)}, u32[]{:S(2)}) collective-permute-start(bf16[1,32,4096]{2,1,0:T(8,128)(2,1)S(1)} %constant_dynamic-update-slice_fusion.10), channel_id=1, source_target_pairs={{504,0},{0,8},{8,16},{16,24},{24,32},{32,40},{40,48},{48,56},{56,6... | collective-permute-start | bytes 786440 | tf_op jit(solution)/shard_map/ppermute | solution.py:15
  179.6 18.6 %collective-permute-start.10 = (bf16[1,32,4096]{2,1,0:T(8,128)(2,1)S(1)}, bf16[1,32,4096]{2,1,0:T(8,128)(2,1)S(1)}, u32[]{:S(2)}, u32[]{:S(2)}) collective-permute-start(bf16[1,32,4096]{2,1,0:T(8,128)(2,1)S(1)} %constant_dynamic-update-slice_fusion.10), channel_id=1, source_target_pairs={{8,0},{16,8},{24,16},{32,24},{40,32},{48,40},{56,48},{64,56},{72,6... | collective-permute-start | bytes 786440 | tf_op jit(solution)/shard_map/ppermute | solution.py:15
  185.0 14.5 %collective-permute-start.11 = (bf16[1,32,4096]{2,1,0:T(8,128)(2,1)S(1)}, bf16[1,32,4096]{2,1,0:T(8,128)(2,1)S(1)}, u32[]{:S(2)}, u32[]{:S(2)}) collective-permute-start(bf16[1,32,4096]{2,1,0:T(8,128)(2,1)S(1)} %constant_dynamic-update-slice_fusion.10), channel_id=1, source_target_pairs={{16,0},{24,8},{32,16},{40,24},{48,32},{56,40},{64,48},{72,56},{80,... | collective-permute-start | bytes 786440 | tf_op jit(solution)/shard_map/ppermute | solution.py:15
  207.0 6.6 %copy-start.5 = (bf16[8,2,64,64]{3,2,0,1:T(8,128)(2,1)S(1)}, bf16[8,2,64,64]{3,2,0,1:T(8,128)(2,1)}, u32[]{:S(2)}) copy-start(bf16[8,2,64,64]{3,2,0,1:T(8,128)(2,1)} %reshape.71) | copy-start | bytes 393220
  226.6 6.6 %copy-start.2 = (bf16[8,2,64,64]{3,2,0,1:T(8,128)(2,1)S(1)}, bf16[8,2,64,64]{3,2,0,1:T(8,128)(2,1)}, u32[]{:S(2)}) copy-start(bf16[8,2,64,64]{3,2,0,1:T(8,128)(2,1)} %reshape.69) | copy-start | bytes 393220
  242.4 42.2 %copy-start.3 = (bf16[1,16,4096]{2,1,0:T(8,128)(2,1)S(1)}, bf16[1,16,4096]{2,1,0:T(8,128)(2,1)}, u32[]{:S(2)}) copy-start(bf16[1,16,4096]{2,1,0:T(8,128)(2,1)} %reduce-scatter.4.cloned.1.call-done) | copy-start | bytes 393220
Sparse Core Ops, SparseCore 0:
  97.3 33.5 reduce-scatter.3
  133.7 38.4 reduce-scatter.5
  245.0 39.4 reduce-scatter.7
where the time goes:
time: 295 us; the launch traced here: 293 us
  waiting for transfers between devices  113 us (38%)
  local copies, waits for them, and re-layouts  85.9 us (29%)
  starting transfers between devices  52.5 us (18%)
  matrix products  22.3 us (8%)
  between operations  13.5 us (5%)
  other arithmetic  5.86 us (2%)
    gather x12, local copies, waits for them, and re-layouts, gather_right(): picked = rim_rows.reshape(-1, block_cells)[flat_index]  56 us
    ppermute x12, starting transfers between devices, from_behind(): return lax.ppermute(block, axis, route)  52.2 us
    reduce_scatter x1, waiting for transfers between devices, local(): lax.psum_scatter(sq_terms.astype(jnp.bfloat16), 'row', scatter_dimension=...  40.4 us
    reduce_scatter x1, waiting for transfers between devices, local(): lax.psum_scatter(cubic_terms.astype(jnp.bfloat16), 'row', scatter_dimensi...  39.7 us
    reduce_scatter x1, waiting for transfers between devices, local(): lax.psum_scatter(mix_terms.astype(jnp.bfloat16), 'row', scatter_dimension...  23.1 us
    dot_general x5, matrix products, multiply(): jnp.einsum('gapq,gajqs->gjps', left_blocks, right_blocks, preferred_eleme...  22.3 us
    ppermute x12, waiting for transfers between devices, from_behind(): return lax.ppermute(block, axis, route)  9.43 us
  transfers between devices with their start and end apart: 15, of which 5 were waited for; matrix products, arithmetic and copies ran while one was open for 13% of the time, Pallas kernels for 0%

commit v1 on v0

v1 whole, which is shorter than its diff:
```python
import jax
import jax.numpy as jnp
from jax import lax
from jax.experimental import pallas as pl
from jax.experimental.pallas import tpu as pltpu
from jax.sharding import PartitionSpec as P

BLK = 64
K8 = 2
REACH = 2
SLOTS = 16
ROWS = 8
WIDE = SLOTS * 8
TILES = BLK * BLK // 128
HALF = TILES
F32, BF16 = jnp.float32, jnp.bfloat16
VMEM_BYTES = 48 * 1024 * 1024


def call(body, name, out_shape, scratch, in_specs, flops, moved):
    del name
    return pl.pallas_call(
        body,
        out_shape=out_shape,
        in_specs=in_specs,
        out_specs=jax.tree.map(lambda _: pl.BlockSpec(memory_space=pltpu.VMEM), out_shape),
        scratch_shapes=scratch,
        compiler_params=pltpu.CompilerParams(vmem_limit_bytes=VMEM_BYTES),
        cost_estimate=pl.CostEstimate(flops=flops, bytes_accessed=moved, transcendentals=0),
    )


def in_vmem(count):
    return [pl.BlockSpec(memory_space=pltpu.VMEM)] * count


def by_slot(rows_ref, g, turned):
    flat = rows_ref[g]
    for t in range(TILES):
        turned[pl.ds(t * SLOTS, SLOTS), :] = flat[:, t * 128 : (t + 1) * 128].astype(F32)
    return [turned[pl.ds(b, TILES, stride=SLOTS), :].astype(BF16) for b in range(SLOTS)]


def slice_body(r_ref, ground_ref, response_ref, out_ref, turned, tiles, pick):
    r = r_ref[0]
    line = lax.broadcasted_iota(jnp.int32, (128, 256), 0)
    lane = lax.broadcasted_iota(jnp.int32, (128, 256), 1)
    half, col = line // BLK, line % BLK - 8 * r
    home = jnp.where((col >= 0) & (col < 8), half * 128 + col, -1024)
    for b in range(SLOTS):
        at = (b % 2) * 64 + (b // 2) * 8
        pick[pl.ds(b * 128, 128), :] = jnp.where(lane - at == home, 1.0, 0.0).astype(BF16)
    for m, rows_ref in enumerate((ground_ref, response_ref)):

        def step(g, _, m=m, rows_ref=rows_ref):
            parts = by_slot(rows_ref, g, turned)
            at = pl.multiple_of((m * ROWS + g) * TILES, TILES)
            for b in range(SLOTS):
                tiles[pl.ds(at, TILES), b * 128 : (b + 1) * 128] = parts[b]
            return 0

        lax.fori_loop(0, ROWS, step, 0)
    cut = jnp.dot(tiles[...], pick[...], preferred_element_type=F32).astype(BF16)
    for m in range(2):
        for g in range(ROWS):
            at = (m * ROWS + g) * TILES
            out_ref[m, g, 0:HALF, :] = cut[at : at + TILES, 0:128]
            out_ref[m, g, HALF:BLK, :] = cut[at : at + TILES, 128:256]


def left_body(ground_ref, response_ref, out_ref, turned):
    src = lax.broadcasted_iota(jnp.int32, (256, 256), 0)
    dst = lax.broadcasted_iota(jnp.int32, (256, 256), 1)
    two, half, col = src // 128, src // BLK % 2, src % BLK
    want = half * 128 + two * BLK + (col % 2) * HALF + col // 2
    turn = jnp.where(dst == want, 1.0, 0.0).astype(BF16)
    for m, rows_ref in enumerate((response_ref, ground_ref)):

        def step(g, _, m=m, rows_ref=rows_ref):
            parts = by_slot(rows_ref, g, turned)
            pairs = [jnp.concatenate(parts[b : b + 2], axis=1) for b in range(0, SLOTS, 2)]
            both = jnp.dot(jnp.concatenate(pairs, axis=0), turn, preferred_element_type=F32).astype(BF16)
            for i in range(SLOTS // 2):
                piece = both[i * TILES : (i + 1) * TILES]
                out_ref[m, g, 0:HALF, i * 128 : (i + 1) * 128] = piece[:, 0:128]
                out_ref[m, g, HALF:BLK, i * 128 : (i + 1) * 128] = piece[:, 128:256]
            return 0

        lax.fori_loop(0, ROWS, step, 0)


def fill_window(window, pieces):
    for o, piece in enumerate(pieces):
        for m in range(2):

            def step(g, _, o=o, m=m, piece=piece):
                block = piece[m, g]
                window[o * ROWS + g, m, :, 0:128] = block
                window[o * ROWS + g, m, :, 128:256] = jnp.concatenate([block[:, 64:128], block[:, 0:64]], axis=1)
                return 0

            lax.fori_loop(0, ROWS, step, 0)


def rights(window, where_ref, same_ref, other_ref, g):
    stacks = ([], [])
    for a in range(SLOTS):
        i = g * SLOTS + a
        k = where_ref[i]
        same = jnp.broadcast_to(same_ref[pl.ds(i, 1), :], (16, 128)).astype(BF16)
        other = jnp.broadcast_to(other_ref[pl.ds(i, 1), :], (16, 128)).astype(BF16)
        same, other = jnp.concatenate([same] * 4, axis=0), jnp.concatenate([other] * 4, axis=0)
        for m in range(2):
            both = window[k, m]
            stacks[m].append(both[:, 0:128] * same + both[:, 128:256] * other)
    return [jnp.concatenate(stack, axis=0) for stack in stacks]


def first_body(where_ref, same_ref, other_ref, x0, x1, x2, x3, x4, left_ref, pair_ref, mixed_ref, window):
    fill_window(window, (x0, x1, x2, x3, x4))

    def step(g, _):
        ground, response = rights(window, where_ref, same_ref, other_ref, g)
        left_response, left_ground = left_ref[0, g], left_ref[1, g]
        mixed = jnp.dot(left_response, ground, preferred_element_type=F32)
        mixed = mixed + jnp.dot(left_ground, response, preferred_element_type=F32)
        square = jnp.dot(left_ground, ground, preferred_element_type=F32)
        mixed_ref[g] = mixed
        pair_ref[0, g] = square.astype(BF16)
        pair_ref[1, g] = mixed.astype(BF16)
        return 0

    lax.fori_loop(0, ROWS, step, 0)


def second_body(where_ref, same_ref, other_ref, x0, x1, x2, x3, x4, left_ref, mixed_ref, out_ref, window):
    fill_window(window, (x0, x1, x2, x3, x4))

    def step(g, _):
        square, mixed = rights(window, where_ref, same_ref, other_ref, g)
        cubic = jnp.dot(left_ref[0, g], square, preferred_element_type=F32)
        cubic = cubic + jnp.dot(left_ref[1, g], mixed, preferred_element_type=F32)
        out_ref[g] = (3.0 * mixed_ref[g] - 2.0 * cubic).astype(BF16)
        return 0

    lax.fori_loop(0, ROWS, step, 0)


def join_body(in_ref, out_ref, turned):
    chunk = lax.broadcasted_iota(jnp.int32, (TILES, 128), 1) // 8
    parts = [in_ref[i % 8, (i // 8) * HALF : (i // 8 + 1) * HALF, :].astype(F32) for i in range(16)]
    for bit in (1, 2, 4, 8):
        low = chunk // bit % 2 == 0
        for i in range(16):
            if i & bit:
                continue
            a, b = parts[i], parts[i | bit]
            parts[i] = jnp.where(low, a, pltpu.roll(b, 8 * bit, 1))
            parts[i | bit] = jnp.where(low, pltpu.roll(a, 128 - 8 * bit, 1), b)
    for i in range(16):
        j = 2 * (i % 8) + i // 8
        turned[pl.ds(j * TILES, TILES), :] = parts[i]
    for t in range(TILES):
        out_ref[0, :, t * 128 : (t + 1) * 128] = turned[pl.ds(t, SLOTS, stride=TILES), :].astype(BF16)


def from_behind(block, distance):
    size = lax.axis_size("col")
    return lax.ppermute(block, "col", [((i - distance) % size, i) for i in range(size)])


def surround(block):
    back, ahead = from_behind(block, 1), from_behind(block, -1)
    return from_behind(back, 1), back, block, ahead, from_behind(ahead, -1)


def lookups(pattern):
    column = lax.axis_index("col")
    size = lax.axis_size("col")
    mine = lax.dynamic_slice_in_dim(pattern, column * ROWS, ROWS, 0)
    live = mine >= 0
    target = jnp.where(live, mine, 0)
    place = (target // ROWS - column + REACH) % size
    place = jnp.where(live, place, REACH) * ROWS + target % ROWS
    far = pattern[target].reshape(ROWS, SLOTS, ROWS, K8)
    near = mine.reshape(ROWS, 1, ROWS, K8)
    valid = (near >= 0) & live[:, :, None, None]

    def lanes(hit):
        hit = (hit & valid).astype(F32).transpose(0, 1, 3, 2)
        return jnp.broadcast_to(hit[..., None], hit.shape + (8,)).reshape(ROWS * SLOTS, WIDE)

    return place.reshape(-1), lanes(far == near), lanes(far[..., ::-1] == near)


def local(ground, response, pattern):
    rows = jax.ShapeDtypeStruct((2, ROWS, BLK, WIDE), BF16)
    smem = pl.BlockSpec(memory_space=pltpu.SMEM)
    turned = pltpu.VMEM((SLOTS * TILES, 128), F32)
    window = pltpu.VMEM((5 * ROWS, 2, BLK, 2 * WIDE), BF16)
    r = lax.axis_index("row").astype(jnp.int32).reshape(1)
    cut = call(
        slice_body,
        "slice",
        rows,
        [turned, pltpu.VMEM((2 * ROWS * TILES, SLOTS * 128), BF16), pltpu.VMEM((SLOTS * 128, 256), BF16)],
        [smem] + in_vmem(2),
        2 * 512 * 2048 * 256,
        5 << 20,
    )(r, ground, response)
    cut, ground, response, pattern = lax.optimization_barrier((cut, ground, response, pattern))
    pieces = surround(cut)
    left = call(
        left_body,
        "left",
        jax.ShapeDtypeStruct((2, ROWS, BLK, SLOTS * BLK), BF16),
        [turned],
        in_vmem(2),
        2 * 4096 * 256 * 256,
        5 << 20,
    )(ground, response)
    place, same, other = lookups(pattern)
    flops = 2 * ROWS * BLK * 1024 * 128
    pair, mixed = call(
        first_body,
        "first",
        (rows, jax.ShapeDtypeStruct((ROWS, BLK, WIDE), F32)),
        [window],
        [smem] + in_vmem(8),
        3 * flops,
        5 << 20,
    )(place, same, other, *pieces, left)
    pieces = surround(pair)
    part = call(
        second_body,
        "second",
        jax.ShapeDtypeStruct((ROWS, BLK, WIDE), BF16),
        [window],
        [smem] + in_vmem(9),
        2 * flops,
        5 << 20,
    )(place, same, other, *pieces, left, mixed)
    part = lax.all_to_all(part, "row", 0, 0, tiled=True)
    return call(
        join_body,
        "join",
        jax.ShapeDtypeStruct((1, SLOTS, BLK * BLK), BF16),
        [turned],
        in_vmem(1),
        0,
        1 << 18,
    )(part)


def solution(mesh):
    in_specs = (P("col", None, None), P("col", None, None), P())
    out_specs = P(("col", "row"), None, None)
    return jax.shard_map(local, mesh=mesh, in_specs=in_specs, out_specs=out_specs, check_vma=False)
```

time: 295 us -> 107 us (0.36)
  waiting for transfers between devices: 113 us -> 11.4 us
  local copies, waits for them, and re-layouts: 85.9 us -> 11 us
  Pallas kernels: 0 us -> 25.7 us
  matrix products: 22.3 us -> 0 us
  blocking collectives: 0 us -> 13.8 us
  between operations: 13.5 us -> 0.25 us
  starting transfers between devices: 52.5 us -> 43.8 us
  other arithmetic: 5.86 us -> 0.22 us
    reduce_scatter x3 -> x0, waiting for transfers between devices: 103 us -> none  [the longest x1 40.4 us: local(): lax.psum_scatter(sq_terms.astype(jnp.bfloat16), 'row', scatter_dimension=...]
    gather x13 -> x2, local copies, waits for them, and re-layouts: 56.5 us -> 0.71 us  [lookups(): far = pattern[target].reshape(ROWS, SLOTS, ROWS, K8)]
    pallas_call x0 -> x5, Pallas kernels: none -> 25.7 us  [the longest x1 9.3 us: local(): call(first_body, 'first', (rows, jax.ShapeDtypeStruct((ROWS, BLK, WIDE),...]
    dot_general x5 -> x0, matrix products: 22.3 us -> none  [multiply(): jnp.einsum('gapq,gajqs->gjps', left_blocks, right_blocks, preferred_eleme...]
    convert_element_type x6 -> x0, local copies, waits for them, and re-layouts: 16.5 us -> none  [the longest x2 5.52 us: local(): sq_terms.astype(jnp.bfloat16)]
    all_to_all x0 -> x1, blocking collectives: none -> 13.8 us  [local(): part = lax.all_to_all(part, 'row', 0, 0, tiled=True)]
    ppermute x12 -> x8, starting transfers between devices: 52.2 us -> 43.8 us  [from_behind(): lax.ppermute(block, 'col', [((i - distance) % size, i) for i in range(siz...]
    reshape x2 -> x6, local copies, waits for them, and re-layouts: 1.97 us -> 5.75 us  [the longest x4 5.56 us: lanes(): jnp.broadcast_to(hit[..., None], hit.shape + (8,))]
  transfers between devices with their start and end apart: 15 -> 8, of which waited for: 5 -> 4; matrix products, arithmetic and copies ran while one was open for 13% -> 8% of each run, Pallas kernels for 0% -> 3%
where the time goes in v1:
time: 107 us; the launch traced here: 106 us
  starting transfers between devices  43.8 us (41%)
  Pallas kernels  25.7 us (24%)
  blocking collectives  13.8 us (13%)
  waiting for transfers between devices  11.4 us (11%)
  local copies, waits for them, and re-layouts  11 us (10%)
    ppermute x8, starting transfers between devices, from_behind(): lax.ppermute(block, 'col', [((i - distance) % size, i) for i in range(siz...  43.8 us
    all_to_all x1, blocking collectives, local(): part = lax.all_to_all(part, 'row', 0, 0, tiled=True)  13.8 us
    ppermute x8, waiting for transfers between devices, from_behind(): lax.ppermute(block, 'col', [((i - distance) % size, i) for i in range(siz...  11.4 us
    pallas_call x1, Pallas kernels, local(): call(first_body, 'first', (rows, jax.ShapeDtypeStruct((ROWS, BLK, WIDE),...  9.3 us
    pallas_call x1, Pallas kernels, local(): call(second_body, 'second', jax.ShapeDtypeStruct((ROWS, BLK, WIDE), BF16)...  8.97 us
    reshape x4, local copies, waits for them, and re-layouts, lanes(): jnp.broadcast_to(hit[..., None], hit.shape + (8,))  5.56 us
    pallas_call x1, Pallas kernels, local(): call(left_body, 'left', jax.ShapeDtypeStruct((2, ROWS, BLK, SLOTS * BLK),...  3.72 us
    pallas_call x1, Pallas kernels, local(): call(slice_body, 'slice', rows, [turned, pltpu.VMEM((2 * ROWS * TILES, SL...  2.59 us
  transfers between devices with their start and end apart: 8, of which 4 were waited for; matrix products, arithmetic and copies ran while one was open for 8% of the time, Pallas kernels for 3%

profile of v1, /device:TPU:1, one launch (start us, length us, event | category | flops | bytes accessed | tf_op | source)
XLA Modules:
  0.0 106.2 jit_solution(11042216664332276586)
XLA Ops:
  0.0 1.2 %copy-done = bf16[8,16,4096]{2,1,0:T(8,128)(2,1)S(1)} copy-done((bf16[8,16,4096]{2,1,0:T(8,128)(2,1)S(1)}, bf16[8,16,4096]{2,1,0:T(8,128)(2,1)}, u32[]{:S(2)}) %copy-start) | copy-done | bytes 1048600
  1.2 1.2 %copy-done.2 = bf16[8,16,4096]{2,1,0:T(8,128)(2,1)S(1)} copy-done((bf16[8,16,4096]{2,1,0:T(8,128)(2,1)S(1)}, bf16[8,16,4096]{2,1,0:T(8,128)(2,1)}, u32[]{:S(2)}) %copy-start.2) | copy-done | bytes 1048600
  2.5 2.6 %shard_map.37.x2 = bf16[2,8,64,128]{3,2,1,0:T(8,128)(2,1)S(1)} custom-call(s32[1]{0:T(128)} %bitcast.r_ref, bf16[8,16,4096]{2,1,0:T(8,128)(2,1)S(1)} %copy-done, bf16[8,16,4096]{2,1,0:T(8,128)(2,1)S(1)} %copy-done.2), custom_call_target="tpu_custom_call" | custom-call | flops 536870912 | bytes 5242880 | tf_op jit(solution)/shard_map/pallas_call | solution.py:202
  5.0 14.4 %collective-permute-start.2 = (bf16[2,8,64,128]{3,2,1,0:T(8,128)(2,1)S(1)}, bf16[2,8,64,128]{3,2,1,0:T(8,128)(2,1)S(1)}, u32[]{:S(2)}, u32[]{:S(2)}) collective-permute-start(bf16[2,8,64,128]{3,2,1,0:T(8,128)(2,1)S(1)} %shard_map.37.x2), channel_id=1, source_target_pairs={{8,0},{16,8},{24,16},{32,24},{40,32},{48,40},{56,48},{64,56},{72,6... | collective-permute-start | bytes 786440 | tf_op jit(solution)/shard_map/ppermute | solution.py:169
  19.5 1.9 %collective-permute-start = (bf16[2,8,64,128]{3,2,1,0:T(8,128)(2,1)S(1)}, bf16[2,8,64,128]{3,2,1,0:T(8,128)(2,1)S(1)}, u32[]{:S(2)}, u32[]{:S(2)}) collective-permute-start(bf16[2,8,64,128]{3,2,1,0:T(8,128)(2,1)S(1)} %shard_map.37.x2), channel_id=1, source_target_pairs={{504,0},{0,8},{8,16},{16,24},{24,32},{32,40},{40,48},{48,56},{56,6... | collective-permute-start | bytes 786440 | tf_op jit(solution)/shard_map/ppermute | solution.py:169
  21.6 0.1 reshape.34
  21.7 0.1 copy.14
  21.8 0.1 copy.16
  22.1 0.7 gather_fusion
  22.8 0.1 reshape.29
  22.9 1.5 %collective-permute-done.2.x3 = bf16[2,8,64,128]{3,2,1,0:T(8,128)(2,1)S(1)} collective-permute-done((bf16[2,8,64,128]{3,2,1,0:T(8,128)(2,1)S(1)}, bf16[2,8,64,128]{3,2,1,0:T(8,128)(2,1)S(1)}, u32[]{:S(2)}, u32[]{:S(2)}) %collective-permute-start.2) | collective-permute-done | bytes 262176 | tf_op jit(solution)/shard_map/ppermute | solution.py:169
  24.4 7.4 %collective-permute-start.3 = (bf16[2,8,64,128]{3,2,1,0:T(8,128)(2,1)S(1)}, bf16[2,8,64,128]{3,2,1,0:T(8,128)(2,1)S(1)}, u32[]{:S(2)}, u32[]{:S(2)}) collective-permute-start(bf16[2,8,64,128]{3,2,1,0:T(8,128)(2,1)S(1)} %collective-permute-done.2.x3), channel_id=1, source_target_pairs={{8,0},{16,8},{24,16},{32,24},{40,32},{48,40},{56,48},{64,56},{72,6... | collective-permute-start | bytes 786440 | tf_op jit(solution)/shard_map/ppermute | solution.py:169
  31.8 1.9 %collective-permute-start.1 = (bf16[2,8,64,128]{3,2,1,0:T(8,128)(2,1)S(1)}, bf16[2,8,64,128]{3,2,1,0:T(8,128)(2,1)S(1)}, u32[]{:S(2)}, u32[]{:S(2)}) collective-permute-start(bf16[2,8,64,128]{3,2,1,0:T(8,128)(2,1)S(1)} %collective-permute-done.x1), channel_id=1, source_target_pairs={{504,0},{0,8},{8,16},{16,24},{24,32},{32,40},{40,48},{48,56},{56,6... | collective-permute-start | bytes 786440 | tf_op jit(solution)/shard_map/ppermute | solution.py:169
  33.8 0.1 convert_bitcast_fusion
  33.9 0.8 broadcast_in_dim.10
  34.7 1.9 %reshape.30 = f32[128,128]{0,1:T(8,128)} reshape(f32[8,16,2,8,8]{1,0,4,3,2:T(8,128)} %broadcast_in_dim.10) | data formatting | bytes 131072 | tf_op jit(solution)/shard_map/reshape | solution.py:191
  36.6 0.9 copy.21.same_ref
  37.5 0.8 broadcast_in_dim.11
  38.4 1.9 %reshape.31 = f32[128,128]{0,1:T(8,128)} reshape(f32[8,16,2,8,8]{1,0,4,3,2:T(8,128)} %broadcast_in_dim.11) | data formatting | bytes 131072 | tf_op jit(solution)/shard_map/reshape | solution.py:191
  40.2 0.9 copy.22.other_ref
  41.2 3.7 %shard_map.38.left_ref = bf16[2,8,64,1024]{3,2,1,0:T(8,128)(2,1)S(1)} custom-call(bf16[8,16,4096]{2,1,0:T(8,128)(2,1)S(1)} %copy-done.1, bf16[8,16,4096]{2,1,0:T(8,128)(2,1)S(1)} %copy-done.3), custom_call_target="tpu_custom_call" | custom-call | flops 536870912 | bytes 5242880 | tf_op jit(solution)/shard_map/pallas_call | solution.py:213
  44.9 9.3 %shard_map.39 = (bf16[2,8,64,128]{3,2,1,0:T(8,128)(2,1)S(1)}, f32[8,64,128]{2,1,0:T(8,128)S(1)}) custom-call(s32[128]{0:T(128)S(1)} %reshape.28.where_ref, f32[128,128]{1,0:T(8,128)S(1)} %copy.21.same_ref, f32[128,128]{1,0:T(8,128)S(1)} %copy.22.other_ref, bf16[2,8,64,128]{3,2,1,0:T(8,128)(2,1)S(1)} %collective-permute-done.1.x0, ...), custom_call_target="tpu_custom_call" | custom-call | flops 402653184 | bytes 5242880 | tf_op jit(solution)/shard_map/pallas_call | solution.py:224
  54.2 6.7 %collective-permute-start.6 = (bf16[2,8,64,128]{3,2,1,0:T(8,128)(2,1)S(1)}, bf16[2,8,64,128]{3,2,1,0:T(8,128)(2,1)S(1)}, u32[]{:S(2)}, u32[]{:S(2)}) collective-permute-start(bf16[2,8,64,128]{3,2,1,0:T(8,128)(2,1)S(1)} %get-tuple-element.15.x2), channel_id=1, source_target_pairs={{8,0},{16,8},{24,16},{32,24},{40,32},{48,40},{56,48},{64,56},{72,6... | collective-permute-start | bytes 786440 | tf_op jit(solution)/shard_map/ppermute | solution.py:169
  60.9 1.9 %collective-permute-start.4 = (bf16[2,8,64,128]{3,2,1,0:T(8,128)(2,1)S(1)}, bf16[2,8,64,128]{3,2,1,0:T(8,128)(2,1)S(1)}, u32[]{:S(2)}, u32[]{:S(2)}) collective-permute-start(bf16[2,8,64,128]{3,2,1,0:T(8,128)(2,1)S(1)} %get-tuple-element.15.x2), channel_id=1, source_target_pairs={{504,0},{0,8},{8,16},{16,24},{24,32},{32,40},{40,48},{48,56},{56,6... | collective-permute-start | bytes 786440 | tf_op jit(solution)/shard_map/ppermute | solution.py:169
  62.8 1.4 %collective-permute-done.6.x3 = bf16[2,8,64,128]{3,2,1,0:T(8,128)(2,1)S(1)} collective-permute-done((bf16[2,8,64,128]{3,2,1,0:T(8,128)(2,1)S(1)}, bf16[2,8,64,128]{3,2,1,0:T(8,128)(2,1)S(1)}, u32[]{:S(2)}, u32[]{:S(2)}) %collective-permute-start.6) | collective-permute-done | bytes 262176 | tf_op jit(solution)/shard_map/ppermute | solution.py:169
  64.2 7.6 %collective-permute-start.7 = (bf16[2,8,64,128]{3,2,1,0:T(8,128)(2,1)S(1)}, bf16[2,8,64,128]{3,2,1,0:T(8,128)(2,1)S(1)}, u32[]{:S(2)}, u32[]{:S(2)}) collective-permute-start(bf16[2,8,64,128]{3,2,1,0:T(8,128)(2,1)S(1)} %collective-permute-done.6.x3), channel_id=1, source_target_pairs={{8,0},{16,8},{24,16},{32,24},{40,32},{48,40},{56,48},{64,56},{72,6... | collective-permute-start | bytes 786440 | tf_op jit(solution)/shard_map/ppermute | solution.py:169
  71.8 1.9 %collective-permute-start.5 = (bf16[2,8,64,128]{3,2,1,0:T(8,128)(2,1)S(1)}, bf16[2,8,64,128]{3,2,1,0:T(8,128)(2,1)S(1)}, u32[]{:S(2)}, u32[]{:S(2)}) collective-permute-start(bf16[2,8,64,128]{3,2,1,0:T(8,128)(2,1)S(1)} %collective-permute-done.4.x1), channel_id=1, source_target_pairs={{504,0},{0,8},{8,16},{16,24},{24,32},{32,40},{40,48},{48,56},{56,6... | collective-permute-start | bytes 786440 | tf_op jit(solution)/shard_map/ppermute | solution.py:169
  73.7 1.4 %collective-permute-done.7.x4 = bf16[2,8,64,128]{3,2,1,0:T(8,128)(2,1)S(1)} collective-permute-done((bf16[2,8,64,128]{3,2,1,0:T(8,128)(2,1)S(1)}, bf16[2,8,64,128]{3,2,1,0:T(8,128)(2,1)S(1)}, u32[]{:S(2)}, u32[]{:S(2)}) %collective-permute-start.7) | collective-permute-done | bytes 262176 | tf_op jit(solution)/shard_map/ppermute | solution.py:169
  75.1 7.2 %collective-permute-done.5.x0 = bf16[2,8,64,128]{3,2,1,0:T(8,128)(2,1)S(1)} collective-permute-done((bf16[2,8,64,128]{3,2,1,0:T(8,128)(2,1)S(1)}, bf16[2,8,64,128]{3,2,1,0:T(8,128)(2,1)S(1)}, u32[]{:S(2)}, u32[]{:S(2)}) %collective-permute-start.5) | collective-permute-done | bytes 262176 | tf_op jit(solution)/shard_map/ppermute | solution.py:169
  82.2 9.0 %shard_map.40 = bf16[8,64,128]{2,1,0:T(8,128)(2,1)S(1)} custom-call(s32[128]{0:T(128)S(1)} %reshape.28.where_ref, f32[128,128]{1,0:T(8,128)S(1)} %copy.21.same_ref, f32[128,128]{1,0:T(8,128)S(1)} %copy.22.other_ref, bf16[2,8,64,128]{3,2,1,0:T(8,128)(2,1)S(1)} %collective-permute-done.5.x0, bf16[2,8,64,128]{3,2,1,0:T(8,128)(2,1)S(1)} %collective-permute-done.4.x1, ...), custom_call_target="tpu_custom_call" | custom-call | flops 268435456 | bytes 5242880 | tf_op jit(solution)/shard_map/pallas_call | solution.py:234
  91.2 13.8 %all_to_all.5.in_ref = bf16[8,64,128]{2,1,0:T(8,128)(2,1)S(1)} all-to-all(bf16[8,64,128]{2,1,0:T(8,128)(2,1)S(1)} %shard_map.40), channel_id=1, replica_groups=mesh['col'=64,'row'=8] {'row'}, dimensions={0} | all-to-all | bytes 262144 | tf_op jit(solution)/shard_map/all_to_all | solution.py:243
  105.1 1.2 %shard_map.41 = bf16[1,16,4096]{2,1,0:T(8,128)(2,1)} custom-call(bf16[8,64,128]{2,1,0:T(8,128)(2,1)S(1)} %all_to_all.5.in_ref), custom_call_target="tpu_custom_call" | custom-call | bytes 262144 | tf_op jit(solution)/shard_map/pallas_call | solution.py:244
  (22 shorter events, 0.4 us)
Async XLA Ops:
  0.0 1.2 %copy-start = (bf16[8,16,4096]{2,1,0:T(8,128)(2,1)S(1)}, bf16[8,16,4096]{2,1,0:T(8,128)(2,1)}, u32[]{:S(2)}) copy-start(bf16[8,16,4096]{2,1,0:T(8,128)(2,1)} %ground_ref.2) | copy-start | bytes 3145732
  1.2 1.2 %copy-start.2 = (bf16[8,16,4096]{2,1,0:T(8,128)(2,1)S(1)}, bf16[8,16,4096]{2,1,0:T(8,128)(2,1)}, u32[]{:S(2)}) copy-start(bf16[8,16,4096]{2,1,0:T(8,128)(2,1)} %response_ref.2) | copy-start | bytes 3145732
  2.5 18.9 %copy-start.4 = (s32[512,16]{0,1:T(8,128)S(1)}, s32[512,16]{0,1:T(8,128)}, u32[]{:S(2)}) copy-start(s32[512,16]{0,1:T(8,128)} %param.5) | copy-start | bytes 98308
  5.0 19.4 %collective-permute-start.2 = (bf16[2,8,64,128]{3,2,1,0:T(8,128)(2,1)S(1)}, bf16[2,8,64,128]{3,2,1,0:T(8,128)(2,1)S(1)}, u32[]{:S(2)}, u32[]{:S(2)}) collective-permute-start(bf16[2,8,64,128]{3,2,1,0:T(8,128)(2,1)S(1)} %shard_map.37.x2), channel_id=1, source_target_pairs={{8,0},{16,8},{24,16},{32,24},{40,32},{48,40},{56,48},{64,56},{72,6... | collective-permute-start | bytes 786440 | tf_op jit(solution)/shard_map/ppermute | solution.py:169
  19.5 12.4 %collective-permute-start = (bf16[2,8,64,128]{3,2,1,0:T(8,128)(2,1)S(1)}, bf16[2,8,64,128]{3,2,1,0:T(8,128)(2,1)S(1)}, u32[]{:S(2)}, u32[]{:S(2)}) collective-permute-start(bf16[2,8,64,128]{3,2,1,0:T(8,128)(2,1)S(1)} %shard_map.37.x2), channel_id=1, source_target_pairs={{504,0},{0,8},{8,16},{16,24},{24,32},{32,40},{40,48},{48,56},{56,6... | collective-permute-start | bytes 786440 | tf_op jit(solution)/shard_map/ppermute | solution.py:169
  21.5 19.6 %copy-start.1 = (bf16[8,16,4096]{2,1,0:T(8,128)(2,1)S(1)}, bf16[8,16,4096]{2,1,0:T(8,128)(2,1)}, u32[]{:S(2)}) copy-start(bf16[8,16,4096]{2,1,0:T(8,128)(2,1)} %ground_ref.2) | copy-start | bytes 3145732
  21.5 19.6 %copy-start.3 = (bf16[8,16,4096]{2,1,0:T(8,128)(2,1)S(1)}, bf16[8,16,4096]{2,1,0:T(8,128)(2,1)}, u32[]{:S(2)}) copy-start(bf16[8,16,4096]{2,1,0:T(8,128)(2,1)} %response_ref.2) | copy-start | bytes 3145732
  24.4 20.5 %collective-permute-start.3 = (bf16[2,8,64,128]{3,2,1,0:T(8,128)(2,1)S(1)}, bf16[2,8,64,128]{3,2,1,0:T(8,128)(2,1)S(1)}, u32[]{:S(2)}, u32[]{:S(2)}) collective-permute-start(bf16[2,8,64,128]{3,2,1,0:T(8,128)(2,1)S(1)} %collective-permute-done.2.x3), channel_id=1, source_target_pairs={{8,0},{16,8},{24,16},{32,24},{40,32},{48,40},{56,48},{64,56},{72,6... | collective-permute-start | bytes 786440 | tf_op jit(solution)/shard_map/ppermute | solution.py:169
  31.8 13.1 %collective-permute-start.1 = (bf16[2,8,64,128]{3,2,1,0:T(8,128)(2,1)S(1)}, bf16[2,8,64,128]{3,2,1,0:T(8,128)(2,1)S(1)}, u32[]{:S(2)}, u32[]{:S(2)}) collective-permute-start(bf16[2,8,64,128]{3,2,1,0:T(8,128)(2,1)S(1)} %collective-permute-done.x1), channel_id=1, source_target_pairs={{504,0},{0,8},{8,16},{16,24},{24,32},{32,40},{40,48},{48,56},{56,6... | collective-permute-start | bytes 786440 | tf_op jit(solution)/shard_map/ppermute | solution.py:169
  54.2 10.0 %collective-permute-start.6 = (bf16[2,8,64,128]{3,2,1,0:T(8,128)(2,1)S(1)}, bf16[2,8,64,128]{3,2,1,0:T(8,128)(2,1)S(1)}, u32[]{:S(2)}, u32[]{:S(2)}) collective-permute-start(bf16[2,8,64,128]{3,2,1,0:T(8,128)(2,1)S(1)} %get-tuple-element.15.x2), channel_id=1, source_target_pairs={{8,0},{16,8},{24,16},{32,24},{40,32},{48,40},{56,48},{64,56},{72,6... | collective-permute-start | bytes 786440 | tf_op jit(solution)/shard_map/ppermute | solution.py:169
  60.9 10.9 %collective-permute-start.4 = (bf16[2,8,64,128]{3,2,1,0:T(8,128)(2,1)S(1)}, bf16[2,8,64,128]{3,2,1,0:T(8,128)(2,1)S(1)}, u32[]{:S(2)}, u32[]{:S(2)}) collective-permute-start(bf16[2,8,64,128]{3,2,1,0:T(8,128)(2,1)S(1)} %get-tuple-element.15.x2), channel_id=1, source_target_pairs={{504,0},{0,8},{8,16},{16,24},{24,32},{32,40},{40,48},{48,56},{56,6... | collective-permute-start | bytes 786440 | tf_op jit(solution)/shard_map/ppermute | solution.py:169
  64.2 10.9 %collective-permute-start.7 = (bf16[2,8,64,128]{3,2,1,0:T(8,128)(2,1)S(1)}, bf16[2,8,64,128]{3,2,1,0:T(8,128)(2,1)S(1)}, u32[]{:S(2)}, u32[]{:S(2)}) collective-permute-start(bf16[2,8,64,128]{3,2,1,0:T(8,128)(2,1)S(1)} %collective-permute-done.6.x3), channel_id=1, source_target_pairs={{8,0},{16,8},{24,16},{32,24},{40,32},{48,40},{56,48},{64,56},{72,6... | collective-permute-start | bytes 786440 | tf_op jit(solution)/shard_map/ppermute | solution.py:169
  71.8 10.4 %collective-permute-start.5 = (bf16[2,8,64,128]{3,2,1,0:T(8,128)(2,1)S(1)}, bf16[2,8,64,128]{3,2,1,0:T(8,128)(2,1)S(1)}, u32[]{:S(2)}, u32[]{:S(2)}) collective-permute-start(bf16[2,8,64,128]{3,2,1,0:T(8,128)(2,1)S(1)} %collective-permute-done.4.x1), channel_id=1, source_target_pairs={{504,0},{0,8},{8,16},{16,24},{24,32},{32,40},{40,48},{48,56},{56,6... | collective-permute-start | bytes 786440 | tf_op jit(solution)/shard_map/ppermute | solution.py:169

commit v2 on v1

v2 whole, which is shorter than its diff:
```python
import jax
import jax.numpy as jnp
from jax import lax
from jax.experimental import pallas as pl
from jax.experimental.pallas import tpu as pltpu
from jax.sharding import PartitionSpec as P

BLK = 64
K8 = 2
REACH = 2
NB = 512
SLOTS = 16
ROWS = 8
WIDE = SLOTS * 8
TILES = BLK * BLK // 128
HALF = TILES
F32, BF16 = jnp.float32, jnp.bfloat16
PIECES = 2
VMEM_BYTES = 16 * 1024 * 1024


def call(body, name, out_shape, scratch, in_specs, flops, moved):
    del name
    return pl.pallas_call(
        body,
        out_shape=out_shape,
        in_specs=in_specs,
        out_specs=jax.tree.map(lambda _: pl.BlockSpec(memory_space=pltpu.VMEM), out_shape),
        scratch_shapes=scratch,
        compiler_params=pltpu.CompilerParams(vmem_limit_bytes=VMEM_BYTES),
        cost_estimate=pl.CostEstimate(flops=flops, bytes_accessed=moved, transcendentals=0),
    )


def in_vmem(count):
    return [pl.BlockSpec(memory_space=pltpu.VMEM)] * count


def by_slot(rows_ref, g, turned):
    flat = rows_ref[g]
    for t in range(TILES):
        turned[pl.ds(t * SLOTS, SLOTS), :] = flat[:, t * 128 : (t + 1) * 128].astype(F32)
    return [turned[pl.ds(b, TILES, stride=SLOTS), :].astype(BF16) for b in range(SLOTS)]


def exchange(parts):
    parts = list(parts)
    chunk = lax.broadcasted_iota(jnp.int32, parts[0].shape, 1) // 8
    for bit in (1, 2, 4, 8):
        low = chunk // bit % 2 == 0
        for i in range(16):
            if i & bit:
                continue
            a, b = parts[i], parts[i | bit]
            parts[i] = jnp.where(low, a, pltpu.roll(b, 8 * bit, 1))
            parts[i | bit] = jnp.where(low, pltpu.roll(a, 128 - 8 * bit, 1), b)
    return parts


def slice_body(at_ref, ground_hbm, response_hbm, out_ref, held, picked, placed, arrived):
    copies = []
    for m, rows_hbm in enumerate((ground_hbm, response_hbm)):
        for i in range(PIECES):
            part = pl.ds(i * (ROWS // PIECES), ROWS // PIECES)
            copies.append(pltpu.make_async_copy(rows_hbm.at[part], held.at[m, part], arrived.at[m, i]))
    for copy in copies:
        copy.start()
    line = lax.broadcasted_iota(jnp.int32, (1024, 128), 0)
    lane = lax.broadcasted_iota(jnp.int32, (1024, 128), 1)
    col = line % BLK - 8 * at_ref[1]
    pick = jnp.where((col >= 0) & (col < 8) & (lane == line // BLK * 8 + col), 1.0, 0.0).astype(BF16)
    for m in range(2):
        for copy in copies[m * PIECES : (m + 1) * PIECES]:
            copy.wait()
        flat = held[m].reshape(ROWS * SLOTS, BLK * BLK)
        for n in range(4):
            picked[m, n] = jnp.dot(flat[:, n * 1024 : (n + 1) * 1024], pick, preferred_element_type=F32)
            by = [2 * (i % 8) + i // 8 for i in range(16)]
            parts = exchange(picked[m, n, pl.ds(b, ROWS, stride=SLOTS), :] for b in by)
            for i, part in enumerate(parts):
                placed[m, i % 2, pl.ds(n * 8 + i // 2, ROWS, stride=HALF), :] = part
        for half in range(2):
            lines = placed[m, half].astype(BF16).reshape(ROWS, HALF, 128)
            out_ref[m, :, half * HALF : (half + 1) * HALF, :] = lines


def lookup(at_ref, groups_ref, place_ref, same_ref, other_ref):
    column, odd = at_ref[0], at_ref[1] % 2
    groups = groups_ref[...].astype(F32).astype(BF16)
    line = lax.broadcasted_iota(jnp.int32, (NB, WIDE), 0)
    lane = lax.broadcasted_iota(jnp.int32, (NB, WIDE), 1)
    mine = jnp.where(line == column * ROWS + lane // SLOTS, 1.0, 0.0).astype(BF16)
    near = jnp.dot(groups, mine, preferred_element_type=F32)
    slot = lax.broadcasted_iota(jnp.int32, (SLOTS, WIDE), 0)
    pair = lax.broadcasted_iota(jnp.int32, (SLOTS, WIDE), 1)
    home = jnp.sum(jnp.where(slot == pair % SLOTS, near, 0.0), axis=0, keepdims=True)
    live = home >= 0.0
    group = jnp.where(live, home, 0.0).astype(jnp.int32)
    kind = pair[0:1] % SLOTS // K8
    behind = column - group
    size = NB // ROWS
    behind = jnp.where(behind > REACH, behind - size, jnp.where(behind < -REACH, behind + size, behind))
    behind = jnp.where(odd == 1, -behind, behind)
    piece = jnp.where(behind > 0, behind - 1, jnp.where(behind < 0, 1 - behind, 4))
    place_ref[...] = jnp.where(live, piece, 4) * ROWS + kind
    theirs = jnp.where(line == group * ROWS + kind, 1.0, 0.0).astype(BF16)
    far = jnp.dot(groups, theirs, preferred_element_type=F32)
    i = lax.broadcasted_iota(jnp.int32, (SLOTS, SLOTS), 0)
    j = lax.broadcasted_iota(jnp.int32, (SLOTS, SLOTS), 1)
    swap = jnp.where(i // K8 * K8 + 1 - i % K8 == j, 1.0, 0.0).astype(BF16)
    crossed = jnp.dot(swap, far.astype(BF16), preferred_element_type=F32)
    spread = jnp.where(pair // 8 == slot % K8 * ROWS + slot // K8, 1.0, 0.0).astype(BF16)
    for found, out_ref in ((far, same_ref), (crossed, other_ref)):
        hit = jnp.where((found == near) & (near >= 0.0) & live, 1.0, 0.0).astype(BF16)
        out_ref[...] = lax.dot_general(hit, spread, (((0,), (0,)), ((), ())), preferred_element_type=F32)


def left_body(at_ref, groups_ref, ground_ref, response_ref, out_ref, place_ref, same_ref, other_ref, turned):
    lookup(at_ref, groups_ref, place_ref, same_ref, other_ref)
    src = lax.broadcasted_iota(jnp.int32, (256, 256), 0)
    dst = lax.broadcasted_iota(jnp.int32, (256, 256), 1)
    two, half, col = src // 128, src // BLK % 2, src % BLK
    want = half * 128 + two * BLK + (col % 2) * HALF + col // 2
    turn = jnp.where(dst == want, 1.0, 0.0).astype(BF16)
    for m, rows_ref in enumerate((response_ref, ground_ref)):

        def step(g, _, m=m, rows_ref=rows_ref):
            parts = by_slot(rows_ref, g, turned)
            pairs = [jnp.concatenate(parts[b : b + 2], axis=1) for b in range(0, SLOTS, 2)]
            both = jnp.dot(jnp.concatenate(pairs, axis=0), turn, preferred_element_type=F32).astype(BF16)
            for i in range(SLOTS // 2):
                piece = both[i * TILES : (i + 1) * TILES]
                out_ref[g, m * BLK : m * BLK + HALF, i * 128 : (i + 1) * 128] = piece[:, 0:128]
                out_ref[g, m * BLK + HALF : m * BLK + BLK, i * 128 : (i + 1) * 128] = piece[:, 128:256]
            return 0

        lax.fori_loop(0, ROWS, step, 0, unroll=True)


def fill_window(window, pieces):
    for o, piece in enumerate(pieces):
        for m in range(2):
            flat = piece[m].reshape(ROWS * BLK, 128)
            at = o * ROWS * BLK
            window[m, at : at + ROWS * BLK, 0:128] = flat
            window[m, at : at + ROWS * BLK, 128:256] = jnp.concatenate([flat[:, 64:128], flat[:, 0:64]], axis=1)


def rights(window, where_ref, same_ref, other_ref, g):
    stacks = ([], [])
    for a in range(SLOTS):
        i = g * SLOTS + a
        at = pl.multiple_of(where_ref[0, i] * BLK, BLK)
        same = jnp.broadcast_to(same_ref[pl.ds(i, 1), :], (16, 128)).astype(BF16)
        other = jnp.broadcast_to(other_ref[pl.ds(i, 1), :], (16, 128)).astype(BF16)
        same, other = jnp.concatenate([same] * 4, axis=0), jnp.concatenate([other] * 4, axis=0)
        for m in range(2):
            both = window[m, pl.ds(at, BLK), :]
            stacks[m].append(both[:, 0:128] * same + both[:, 128:256] * other)
    return [jnp.concatenate(stack, axis=0) for stack in stacks]


def first_body(where_ref, same_ref, other_ref, x0, x1, x2, x3, x4, left_ref, pair_ref, mixed_ref, window):
    fill_window(window, (x0, x1, x2, x3, x4))

    def step(g, _):
        ground, response = rights(window, where_ref, same_ref, other_ref, g)
        both = jnp.concatenate([ground, response], axis=1)
        product = jnp.dot(left_ref[g], both, preferred_element_type=F32)
        mixed = product[0:BLK, 0:128] + product[BLK:, 128:256]
        mixed_ref[g] = mixed
        pair_ref[0, g] = product[BLK:, 0:128].astype(BF16)
        pair_ref[1, g] = mixed.astype(BF16)
        return 0

    lax.fori_loop(0, ROWS, step, 0, unroll=True)


def second_body(where_ref, same_ref, other_ref, x0, x1, x2, x3, x4, left_ref, mixed_ref, out_ref, window):
    fill_window(window, (x0, x1, x2, x3, x4))

    def step(g, _):
        square, mixed = rights(window, where_ref, same_ref, other_ref, g)
        cubic = jnp.dot(left_ref[g, 0:BLK], square, preferred_element_type=F32)
        cubic = cubic + jnp.dot(left_ref[g, BLK:], mixed, preferred_element_type=F32)
        out_ref[g] = (3.0 * mixed_ref[g] - 2.0 * cubic).astype(BF16)
        return 0

    lax.fori_loop(0, ROWS, step, 0, unroll=True)


def join_body(in_ref, out_ref, turned):
    parts = exchange(in_ref[i % 8, (i // 8) * HALF : (i // 8 + 1) * HALF, :].astype(F32) for i in range(16))
    for i in range(16):
        j = 2 * (i % 8) + i // 8
        turned[pl.ds(j * TILES, TILES), :] = parts[i]
    for t in range(TILES):
        out_ref[0, :, t * 128 : (t + 1) * 128] = turned[pl.ds(t, SLOTS, stride=TILES), :].astype(BF16)


def from_afar(block, distance):
    columns, rows = lax.axis_size("col"), lax.axis_size("row")
    route = []
    for c in range(columns):
        for r in range(rows):
            to = (c + (distance if r % 2 == 0 else -distance)) % columns
            route.append((c * rows + r, to * rows + r))
    return lax.ppermute(block, ("col", "row"), route)


def surround(block):
    return [from_afar(block, distance) for distance in (1, 2, -1, -2)] + [block]


def local(ground, response, pattern):
    rows = jax.ShapeDtypeStruct((2, ROWS, BLK, WIDE), BF16)
    mask = jax.ShapeDtypeStruct((ROWS * SLOTS, WIDE), F32)
    smem = pl.BlockSpec(memory_space=pltpu.SMEM)
    turned = pltpu.VMEM((SLOTS * TILES, 128), F32)
    window = pltpu.VMEM((2, 5 * ROWS * BLK, 2 * WIDE), BF16)
    at = jnp.stack([lax.axis_index("col"), lax.axis_index("row")]).astype(jnp.int32)
    cut = call(
        slice_body,
        "slice",
        rows,
        [
            pltpu.VMEM((2, ROWS, SLOTS, BLK * BLK), BF16),
            pltpu.VMEM((2, 4, ROWS * SLOTS, 128), F32),
            pltpu.VMEM((2, 2, ROWS * HALF, 128), F32),
            pltpu.SemaphoreType.DMA((2, PIECES)),
        ],
        [smem] + [pl.BlockSpec(memory_space=pltpu.HBM)] * 2,
        2 * 1024 * 1024 * 128,
        5 << 20,
    )(at, ground, response)
    cut, ground, response, pattern = lax.optimization_barrier((cut, ground, response, pattern))
    pieces = surround(cut)
    groups = jnp.where(pattern < 0, -1, pattern // ROWS).T
    left, place, same, other = call(
        left_body,
        "left",
        (jax.ShapeDtypeStruct((ROWS, 2 * BLK, SLOTS * BLK), BF16), jax.ShapeDtypeStruct((1, WIDE), jnp.int32), mask, mask),
        [turned],
        [smem] + in_vmem(3),
        2 * 4096 * 256 * 256,
        5 << 20,
    )(at, groups, ground, response)
    flops = 2 * ROWS * BLK * 1024 * 128
    pair, mixed = call(
        first_body,
        "first",
        (rows, jax.ShapeDtypeStruct((ROWS, BLK, WIDE), F32)),
        [window],
        [smem] + in_vmem(8),
        3 * flops,
        5 << 20,
    )(place, same, other, *pieces, left)
    pieces = surround(pair)
    part = call(
        second_body,
        "second",
        jax.ShapeDtypeStruct((ROWS, BLK, WIDE), BF16),
        [window],
        [smem] + in_vmem(9),
        2 * flops,
        5 << 20,
    )(place, same, other, *pieces, left, mixed)
    part = lax.all_to_all(part, "row", 0, 0, tiled=True)
    return call(
        join_body,
        "join",
        jax.ShapeDtypeStruct((1, SLOTS, BLK * BLK), BF16),
        [turned],
        in_vmem(1),
        0,
        1 << 18,
    )(part)


def solution(mesh):
    in_specs = (P("col", None, None), P("col", None, None), P())
    out_specs = P(("col", "row"), None, None)
    return jax.shard_map(local, mesh=mesh, in_specs=in_specs, out_specs=out_specs, check_vma=False)
```

time: 107 us -> 81.7 us (0.76)
  Pallas kernels: 25.7 us -> 12.3 us
  local copies, waits for them, and re-layouts: 11 us -> 2.46 us
  waiting for transfers between devices: 11.4 us -> 17.9 us
  starting transfers between devices: 43.8 us -> 37.7 us
  blocking collectives: 13.8 us -> 10.7 us
    pallas_call x1, Pallas kernels: 9.3 us -> 2.62 us  [local(): call(first_body, 'first', (rows, jax.ShapeDtypeStruct((ROWS, BLK, WIDE),...]
    ppermute x8, waiting for transfers between devices: 11.4 us -> 17.9 us  [from_afar(): return lax.ppermute(block, ('col', 'row'), route)]
    pallas_call x1, Pallas kernels: 8.97 us -> 2.74 us  [local(): call(second_body, 'second', jax.ShapeDtypeStruct((ROWS, BLK, WIDE), BF16)...]
    ppermute x8, starting transfers between devices: 43.8 us -> 37.7 us  [from_afar(): return lax.ppermute(block, ('col', 'row'), route)]
    reshape x6 -> x0, local copies, waits for them, and re-layouts: 5.75 us -> none  [the longest x4 5.56 us: lanes(): jnp.broadcast_to(hit[..., None], hit.shape + (8,))]
    all_to_all x1, blocking collectives: 13.8 us -> 10.7 us  [local(): part = lax.all_to_all(part, 'row', 0, 0, tiled=True)]
    broadcast_in_dim x3 -> x0, local copies, waits for them, and re-layouts: 1.75 us -> none  [the longest x2 1.66 us: lanes(): jnp.broadcast_to(hit[..., None], hit.shape + (8,))]
    unnamed x10 -> x8, local copies, waits for them, and re-layouts: 2.46 us -> 2.46 us
  transfers between devices with their start and end apart: 8 -> 8, of which waited for: 4 -> 5; matrix products, arithmetic and copies ran while one was open for 8% -> 0% of each run, Pallas kernels for 3% -> 4%
where the time goes in v2:
time: 81.7 us; the launch traced here: 81.3 us
  starting transfers between devices  37.7 us (46%)
  waiting for transfers between devices  17.9 us (22%)
  Pallas kernels  12.3 us (15%)
  blocking collectives  10.7 us (13%)
  local copies, waits for them, and re-layouts  2.46 us (3%)
    ppermute x8, starting transfers between devices, from_afar(): return lax.ppermute(block, ('col', 'row'), route)  37.7 us
    ppermute x8, waiting for transfers between devices, from_afar(): return lax.ppermute(block, ('col', 'row'), route)  17.9 us
    all_to_all x1, blocking collectives, local(): part = lax.all_to_all(part, 'row', 0, 0, tiled=True)  10.7 us
    pallas_call x1, Pallas kernels, local(): call(left_body, 'left', (jax.ShapeDtypeStruct((ROWS, 2 * BLK, SLOTS * BLK...  3.1 us
    pallas_call x1, Pallas kernels, local(): call(second_body, 'second', jax.ShapeDtypeStruct((ROWS, BLK, WIDE), BF16)...  2.74 us
    pallas_call x1, Pallas kernels, local(): call(slice_body, 'slice', rows, [pltpu.VMEM((2, ROWS, SLOTS, BLK * BLK),...  2.63 us
    pallas_call x1, Pallas kernels, local(): call(first_body, 'first', (rows, jax.ShapeDtypeStruct((ROWS, BLK, WIDE),...  2.62 us
    unnamed x8, local copies, waits for them, and re-layouts  2.46 us
  transfers between devices with their start and end apart: 8, of which 5 were waited for; matrix products, arithmetic and copies ran while one was open for 0% of the time, Pallas kernels for 4%

profile of v2, /device:TPU:1, one launch (start us, length us, event | category | flops | bytes accessed | tf_op | source)
XLA Modules:
  0.0 81.3 jit_solution(1298744563215599032)
XLA Ops:
  0.0 0.1 pad_add_fusion.at_ref
  0.1 0.0 copy-start
  0.1 1.2 %copy-done = bf16[8,16,4096]{2,1,0:T(8,128)(2,1)S(1)} copy-done((bf16[8,16,4096]{2,1,0:T(8,128)(2,1)S(1)}, bf16[8,16,4096]{2,1,0:T(8,128)(2,1)}, u32[]{:S(2)}) %copy-start) | copy-done | bytes 1048600
  1.3 0.0 copy-start.2
  1.3 1.2 %copy-done.2 = bf16[8,16,4096]{2,1,0:T(8,128)(2,1)S(1)} copy-done((bf16[8,16,4096]{2,1,0:T(8,128)(2,1)S(1)}, bf16[8,16,4096]{2,1,0:T(8,128)(2,1)}, u32[]{:S(2)}) %copy-start.2) | copy-done | bytes 1048600
  2.5 0.0 copy-start.3
  2.5 0.0 copy-start.1
  2.5 2.6 %shard_map.37.x4 = bf16[2,8,64,128]{3,2,1,0:T(8,128)(2,1)S(1)} custom-call(s32[2]{0:T(128)S(1)} %pad_add_fusion.at_ref, bf16[8,16,4096]{2,1,0:T(8,128)(2,1)S(1)} %copy-done, bf16[8,16,4096]{2,1,0:T(8,128)(2,1)S(1)} %copy-done.2), custom_call_target="tpu_custom_call" | custom-call | flops 268435456 | bytes 5242880 | tf_op jit(solution)/shard_map/pallas_call | solution.py:222
  5.2 5.7 %collective-permute-start.3 = (bf16[2,8,64,128]{3,2,1,0:T(8,128)(2,1)S(1)}, bf16[2,8,64,128]{3,2,1,0:T(8,128)(2,1)S(1)}, u32[]{:S(2)}, u32[]{:S(2)}) collective-permute-start(bf16[2,8,64,128]{3,2,1,0:T(8,128)(2,1)S(1)} %shard_map.37.x4), channel_id=1, source_target_pairs={{0,496},{1,17},{2,498},{3,19},{4,500},{5,21},{6,502},{7,23},{8,504... | collective-permute-start | bytes 786440 | tf_op jit(solution)/shard_map/ppermute | solution.py:208
  10.9 3.6 %collective-permute-start.2 = (bf16[2,8,64,128]{3,2,1,0:T(8,128)(2,1)S(1)}, bf16[2,8,64,128]{3,2,1,0:T(8,128)(2,1)S(1)}, u32[]{:S(2)}, u32[]{:S(2)}) collective-permute-start(bf16[2,8,64,128]{3,2,1,0:T(8,128)(2,1)S(1)} %shard_map.37.x4), channel_id=1, source_target_pairs={{0,504},{1,9},{2,506},{3,11},{4,508},{5,13},{6,510},{7,15},{8,0},{... | collective-permute-start | bytes 786440 | tf_op jit(solution)/shard_map/ppermute | solution.py:208
  14.5 10.1 %collective-permute-start.1 = (bf16[2,8,64,128]{3,2,1,0:T(8,128)(2,1)S(1)}, bf16[2,8,64,128]{3,2,1,0:T(8,128)(2,1)S(1)}, u32[]{:S(2)}, u32[]{:S(2)}) collective-permute-start(bf16[2,8,64,128]{3,2,1,0:T(8,128)(2,1)S(1)} %shard_map.37.x4), channel_id=1, source_target_pairs={{0,16},{1,497},{2,18},{3,499},{4,20},{5,501},{6,22},{7,503},{8,24}... | collective-permute-start | bytes 786440 | tf_op jit(solution)/shard_map/ppermute | solution.py:208
  24.6 3.1 %collective-permute-start = (bf16[2,8,64,128]{3,2,1,0:T(8,128)(2,1)S(1)}, bf16[2,8,64,128]{3,2,1,0:T(8,128)(2,1)S(1)}, u32[]{:S(2)}, u32[]{:S(2)}) collective-permute-start(bf16[2,8,64,128]{3,2,1,0:T(8,128)(2,1)S(1)} %shard_map.37.x4), channel_id=1, source_target_pairs={{0,8},{1,505},{2,10},{3,507},{4,12},{5,509},{6,14},{7,511},{8,16},... | collective-permute-start | bytes 786440 | tf_op jit(solution)/shard_map/ppermute | solution.py:208
  27.7 0.0 copy-done.3
  27.7 0.0 copy-done.1
  27.8 3.1 %shard_map.38 = (bf16[8,128,1024]{2,1,0:T(8,128)(2,1)S(1)}, s32[1,128]{1,0:T(1,128)S(1)}, f32[128,128]{1,0:T(8,128)S(1)}, f32[128,128]{1,0:T(8,128)S(1)}) custom-call(s32[2]{0:T(128)S(1)} %pad_add_fusion.at_ref, s32[16,512]{1,0:T(8,128)S(1)} %fusion.2.groups_ref, bf16[8,16,4096]{2,1,0:T(8,128)(2,1)S(1)} %copy-done.1, bf16[8,16,4096]{2,1,0:T(8,128)(2,1)S(1)} %copy-done.2), custom_call_target="tpu_custom_call" | custom-call | flops 536870912 | bytes 5242880 | tf_op jit(solution)/shard_map/pallas_call | solution.py:239
  30.9 0.0 collective-permute-done.3.x3
  30.9 0.0 collective-permute-done.2.x2
  30.9 4.0 %collective-permute-done.1.x1 = bf16[2,8,64,128]{3,2,1,0:T(8,128)(2,1)S(1)} collective-permute-done((bf16[2,8,64,128]{3,2,1,0:T(8,128)(2,1)S(1)}, bf16[2,8,64,128]{3,2,1,0:T(8,128)(2,1)S(1)}, u32[]{:S(2)}, u32[]{:S(2)}) %collective-permute-start.1) | collective-permute-done | bytes 262176 | tf_op jit(solution)/shard_map/ppermute | solution.py:208
  34.9 3.6 %collective-permute-done.x0 = bf16[2,8,64,128]{3,2,1,0:T(8,128)(2,1)S(1)} collective-permute-done((bf16[2,8,64,128]{3,2,1,0:T(8,128)(2,1)S(1)}, bf16[2,8,64,128]{3,2,1,0:T(8,128)(2,1)S(1)}, u32[]{:S(2)}, u32[]{:S(2)}) %collective-permute-start) | collective-permute-done | bytes 262176 | tf_op jit(solution)/shard_map/ppermute | solution.py:208
  38.5 2.6 %shard_map.39 = (bf16[2,8,64,128]{3,2,1,0:T(8,128)(2,1)S(1)}, f32[8,64,128]{2,1,0:T(8,128)S(1)}) custom-call(s32[1,128]{1,0:T(1,128)S(1)} %get-tuple-element.18.where_ref, f32[128,128]{1,0:T(8,128)S(1)} %get-tuple-element.19.same_ref, f32[128,128]{1,0:T(8,128)S(1)} %get-tuple-element.20.other_ref, bf16[2,8,64,128]{3,2,1,0:T(8,128)(2,1)S(1)} %collective-permute-done.x0, ...), custom_call_target="tpu_custom_call" | custom-call | flops 402653184 | bytes 5242880 | tf_op jit(solution)/shard_map/pallas_call | solution.py:249
  41.1 1.9 %collective-permute-start.7 = (bf16[2,8,64,128]{3,2,1,0:T(8,128)(2,1)S(1)}, bf16[2,8,64,128]{3,2,1,0:T(8,128)(2,1)S(1)}, u32[]{:S(2)}, u32[]{:S(2)}) collective-permute-start(bf16[2,8,64,128]{3,2,1,0:T(8,128)(2,1)S(1)} %get-tuple-element.23.x4), channel_id=1, source_target_pairs={{0,496},{1,17},{2,498},{3,19},{4,500},{5,21},{6,502},{7,23},{8,504... | collective-permute-start | bytes 786440 | tf_op jit(solution)/shard_map/ppermute | solution.py:208
  43.1 1.9 %collective-permute-start.6 = (bf16[2,8,64,128]{3,2,1,0:T(8,128)(2,1)S(1)}, bf16[2,8,64,128]{3,2,1,0:T(8,128)(2,1)S(1)}, u32[]{:S(2)}, u32[]{:S(2)}) collective-permute-start(bf16[2,8,64,128]{3,2,1,0:T(8,128)(2,1)S(1)} %get-tuple-element.23.x4), channel_id=1, source_target_pairs={{0,504},{1,9},{2,506},{3,11},{4,508},{5,13},{6,510},{7,15},{8,0},{... | collective-permute-start | bytes 786440 | tf_op jit(solution)/shard_map/ppermute | solution.py:208
  45.0 8.3 %collective-permute-start.5 = (bf16[2,8,64,128]{3,2,1,0:T(8,128)(2,1)S(1)}, bf16[2,8,64,128]{3,2,1,0:T(8,128)(2,1)S(1)}, u32[]{:S(2)}, u32[]{:S(2)}) collective-permute-start(bf16[2,8,64,128]{3,2,1,0:T(8,128)(2,1)S(1)} %get-tuple-element.23.x4), channel_id=1, source_target_pairs={{0,16},{1,497},{2,18},{3,499},{4,20},{5,501},{6,22},{7,503},{8,24}... | collective-permute-start | bytes 786440 | tf_op jit(solution)/shard_map/ppermute | solution.py:208
  53.3 3.1 %collective-permute-start.4 = (bf16[2,8,64,128]{3,2,1,0:T(8,128)(2,1)S(1)}, bf16[2,8,64,128]{3,2,1,0:T(8,128)(2,1)S(1)}, u32[]{:S(2)}, u32[]{:S(2)}) collective-permute-start(bf16[2,8,64,128]{3,2,1,0:T(8,128)(2,1)S(1)} %get-tuple-element.23.x4), channel_id=1, source_target_pairs={{0,8},{1,505},{2,10},{3,507},{4,12},{5,509},{6,14},{7,511},{8,16},... | collective-permute-start | bytes 786440 | tf_op jit(solution)/shard_map/ppermute | solution.py:208
  56.4 0.0 collective-permute-done.7.x3
  56.4 1.2 %collective-permute-done.6.x2 = bf16[2,8,64,128]{3,2,1,0:T(8,128)(2,1)S(1)} collective-permute-done((bf16[2,8,64,128]{3,2,1,0:T(8,128)(2,1)S(1)}, bf16[2,8,64,128]{3,2,1,0:T(8,128)(2,1)S(1)}, u32[]{:S(2)}, u32[]{:S(2)}) %collective-permute-start.6) | collective-permute-done | bytes 262176 | tf_op jit(solution)/shard_map/ppermute | solution.py:208
  57.6 2.9 %collective-permute-done.5.x1 = bf16[2,8,64,128]{3,2,1,0:T(8,128)(2,1)S(1)} collective-permute-done((bf16[2,8,64,128]{3,2,1,0:T(8,128)(2,1)S(1)}, bf16[2,8,64,128]{3,2,1,0:T(8,128)(2,1)S(1)}, u32[]{:S(2)}, u32[]{:S(2)}) %collective-permute-start.5) | collective-permute-done | bytes 262176 | tf_op jit(solution)/shard_map/ppermute | solution.py:208
  60.5 6.2 %collective-permute-done.4.x0 = bf16[2,8,64,128]{3,2,1,0:T(8,128)(2,1)S(1)} collective-permute-done((bf16[2,8,64,128]{3,2,1,0:T(8,128)(2,1)S(1)}, bf16[2,8,64,128]{3,2,1,0:T(8,128)(2,1)S(1)}, u32[]{:S(2)}, u32[]{:S(2)}) %collective-permute-start.4) | collective-permute-done | bytes 262176 | tf_op jit(solution)/shard_map/ppermute | solution.py:208
  66.7 2.7 %shard_map.40 = bf16[8,64,128]{2,1,0:T(8,128)(2,1)S(1)} custom-call(s32[1,128]{1,0:T(1,128)S(1)} %get-tuple-element.18.where_ref, f32[128,128]{1,0:T(8,128)S(1)} %get-tuple-element.19.same_ref, f32[128,128]{1,0:T(8,128)S(1)} %get-tuple-element.20.other_ref, bf16[2,8,64,128]{3,2,1,0:T(8,128)(2,1)S(1)} %collective-permute-done.4.x0, ...), custom_call_target="tpu_custom_call" | custom-call | flops 268435456 | bytes 5242880 | tf_op jit(solution)/shard_map/pallas_call | solution.py:259
  69.4 10.7 %all_to_all.5.in_ref = bf16[8,64,128]{2,1,0:T(8,128)(2,1)S(1)} all-to-all(bf16[8,64,128]{2,1,0:T(8,128)(2,1)S(1)} %shard_map.40), channel_id=1, replica_groups=mesh['col'=64,'row'=8] {'row'}, dimensions={0} | all-to-all | bytes 262144 | tf_op jit(solution)/shard_map/all_to_all | solution.py:268
  80.1 1.2 %shard_map.41 = bf16[1,16,4096]{2,1,0:T(8,128)(2,1)} custom-call(bf16[8,64,128]{2,1,0:T(8,128)(2,1)S(1)} %all_to_all.5.in_ref), custom_call_target="tpu_custom_call" | custom-call | bytes 262144 | tf_op jit(solution)/shard_map/pallas_call | solution.py:269
  (1 shorter events, 0.0 us)
Async XLA Ops:
  0.1 1.2 %copy-start = (bf16[8,16,4096]{2,1,0:T(8,128)(2,1)S(1)}, bf16[8,16,4096]{2,1,0:T(8,128)(2,1)}, u32[]{:S(2)}) copy-start(bf16[8,16,4096]{2,1,0:T(8,128)(2,1)} %ground_ref) | copy-start | bytes 3145732
  1.3 1.2 %copy-start.2 = (bf16[8,16,4096]{2,1,0:T(8,128)(2,1)S(1)}, bf16[8,16,4096]{2,1,0:T(8,128)(2,1)}, u32[]{:S(2)}) copy-start(bf16[8,16,4096]{2,1,0:T(8,128)(2,1)} %response_ref) | copy-start | bytes 3145732
  2.5 25.2 %copy-start.3 = (s32[512,16]{0,1:T(8,128)S(1)}, s32[512,16]{0,1:T(8,128)}, u32[]{:S(2)}) copy-start(s32[512,16]{0,1:T(8,128)} %param.5) | copy-start | bytes 98308
  2.5 25.2 %copy-start.1 = (bf16[8,16,4096]{2,1,0:T(8,128)(2,1)S(1)}, bf16[8,16,4096]{2,1,0:T(8,128)(2,1)}, u32[]{:S(2)}) copy-start(bf16[8,16,4096]{2,1,0:T(8,128)(2,1)} %ground_ref) | copy-start | bytes 3145732
  5.2 25.7 %collective-permute-start.3 = (bf16[2,8,64,128]{3,2,1,0:T(8,128)(2,1)S(1)}, bf16[2,8,64,128]{3,2,1,0:T(8,128)(2,1)S(1)}, u32[]{:S(2)}, u32[]{:S(2)}) collective-permute-start(bf16[2,8,64,128]{3,2,1,0:T(8,128)(2,1)S(1)} %shard_map.37.x4), channel_id=1, source_target_pairs={{0,496},{1,17},{2,498},{3,19},{4,500},{5,21},{6,502},{7,23},{8,504... | collective-permute-start | bytes 786440 | tf_op jit(solution)/shard_map/ppermute | solution.py:208
  10.9 20.0 %collective-permute-start.2 = (bf16[2,8,64,128]{3,2,1,0:T(8,128)(2,1)S(1)}, bf16[2,8,64,128]{3,2,1,0:T(8,128)(2,1)S(1)}, u32[]{:S(2)}, u32[]{:S(2)}) collective-permute-start(bf16[2,8,64,128]{3,2,1,0:T(8,128)(2,1)S(1)} %shard_map.37.x4), channel_id=1, source_target_pairs={{0,504},{1,9},{2,506},{3,11},{4,508},{5,13},{6,510},{7,15},{8,0},{... | collective-permute-start | bytes 786440 | tf_op jit(solution)/shard_map/ppermute | solution.py:208
  14.5 20.4 %collective-permute-start.1 = (bf16[2,8,64,128]{3,2,1,0:T(8,128)(2,1)S(1)}, bf16[2,8,64,128]{3,2,1,0:T(8,128)(2,1)S(1)}, u32[]{:S(2)}, u32[]{:S(2)}) collective-permute-start(bf16[2,8,64,128]{3,2,1,0:T(8,128)(2,1)S(1)} %shard_map.37.x4), channel_id=1, source_target_pairs={{0,16},{1,497},{2,18},{3,499},{4,20},{5,501},{6,22},{7,503},{8,24}... | collective-permute-start | bytes 786440 | tf_op jit(solution)/shard_map/ppermute | solution.py:208
  24.6 13.9 %collective-permute-start = (bf16[2,8,64,128]{3,2,1,0:T(8,128)(2,1)S(1)}, bf16[2,8,64,128]{3,2,1,0:T(8,128)(2,1)S(1)}, u32[]{:S(2)}, u32[]{:S(2)}) collective-permute-start(bf16[2,8,64,128]{3,2,1,0:T(8,128)(2,1)S(1)} %shard_map.37.x4), channel_id=1, source_target_pairs={{0,8},{1,505},{2,10},{3,507},{4,12},{5,509},{6,14},{7,511},{8,16},... | collective-permute-start | bytes 786440 | tf_op jit(solution)/shard_map/ppermute | solution.py:208
  41.1 15.3 %collective-permute-start.7 = (bf16[2,8,64,128]{3,2,1,0:T(8,128)(2,1)S(1)}, bf16[2,8,64,128]{3,2,1,0:T(8,128)(2,1)S(1)}, u32[]{:S(2)}, u32[]{:S(2)}) collective-permute-start(bf16[2,8,64,128]{3,2,1,0:T(8,128)(2,1)S(1)} %get-tuple-element.23.x4), channel_id=1, source_target_pairs={{0,496},{1,17},{2,498},{3,19},{4,500},{5,21},{6,502},{7,23},{8,504... | collective-permute-start | bytes 786440 | tf_op jit(solution)/shard_map/ppermute | solution.py:208
  43.1 14.6 %collective-permute-start.6 = (bf16[2,8,64,128]{3,2,1,0:T(8,128)(2,1)S(1)}, bf16[2,8,64,128]{3,2,1,0:T(8,128)(2,1)S(1)}, u32[]{:S(2)}, u32[]{:S(2)}) collective-permute-start(bf16[2,8,64,128]{3,2,1,0:T(8,128)(2,1)S(1)} %get-tuple-element.23.x4), channel_id=1, source_target_pairs={{0,504},{1,9},{2,506},{3,11},{4,508},{5,13},{6,510},{7,15},{8,0},{... | collective-permute-start | bytes 786440 | tf_op jit(solution)/shard_map/ppermute | solution.py:208
  45.0 15.5 %collective-permute-start.5 = (bf16[2,8,64,128]{3,2,1,0:T(8,128)(2,1)S(1)}, bf16[2,8,64,128]{3,2,1,0:T(8,128)(2,1)S(1)}, u32[]{:S(2)}, u32[]{:S(2)}) collective-permute-start(bf16[2,8,64,128]{3,2,1,0:T(8,128)(2,1)S(1)} %get-tuple-element.23.x4), channel_id=1, source_target_pairs={{0,16},{1,497},{2,18},{3,499},{4,20},{5,501},{6,22},{7,503},{8,24}... | collective-permute-start | bytes 786440 | tf_op jit(solution)/shard_map/ppermute | solution.py:208
  53.3 13.4 %collective-permute-start.4 = (bf16[2,8,64,128]{3,2,1,0:T(8,128)(2,1)S(1)}, bf16[2,8,64,128]{3,2,1,0:T(8,128)(2,1)S(1)}, u32[]{:S(2)}, u32[]{:S(2)}) collective-permute-start(bf16[2,8,64,128]{3,2,1,0:T(8,128)(2,1)S(1)} %get-tuple-element.23.x4), channel_id=1, source_target_pairs={{0,8},{1,505},{2,10},{3,507},{4,12},{5,509},{6,14},{7,511},{8,16},... | collective-permute-start | bytes 786440 | tf_op jit(solution)/shard_map/ppermute | solution.py:208

commit v3 on v2

--- a/solution.py
+++ b/solution.py
@@ -19,7 +19,10 @@
 VMEM_BYTES = 16 * 1024 * 1024
 
 
-def call(body, name, out_shape, scratch, in_specs, flops, moved):
+SLICE_BYTES = int(62.5 * 1024 * 1024)
+
+
+def call(body, name, out_shape, scratch, in_specs, flops, moved, vmem=VMEM_BYTES):
     del name
     return pl.pallas_call(
         body,
@@ -27,7 +30,7 @@
         in_specs=in_specs,
         out_specs=jax.tree.map(lambda _: pl.BlockSpec(memory_space=pltpu.VMEM), out_shape),
         scratch_shapes=scratch,
-        compiler_params=pltpu.CompilerParams(vmem_limit_bytes=VMEM_BYTES),
+        compiler_params=pltpu.CompilerParams(vmem_limit_bytes=vmem),
         cost_estimate=pl.CostEstimate(flops=flops, bytes_accessed=moved, transcendentals=0),
     )
 
@@ -57,7 +60,7 @@
     return parts
 
 
-def slice_body(at_ref, ground_hbm, response_hbm, out_ref, held, picked, placed, arrived):
+def slice_body(ground_hbm, response_hbm, out_ref, held, picked, placed, arrived):
     copies = []
     for m, rows_hbm in enumerate((ground_hbm, response_hbm)):
         for i in range(PIECES):
@@ -67,7 +70,7 @@
         copy.start()
     line = lax.broadcasted_iota(jnp.int32, (1024, 128), 0)
     lane = lax.broadcasted_iota(jnp.int32, (1024, 128), 1)
-    col = line % BLK - 8 * at_ref[1]
+    col = line % BLK - 8 * lax.axis_index("row")
     pick = jnp.where((col >= 0) & (col < 8) & (lane == line // BLK * 8 + col), 1.0, 0.0).astype(BF16)
     for m in range(2):
         for copy in copies[m * PIECES : (m + 1) * PIECES]:
@@ -84,8 +87,8 @@
             out_ref[m, :, half * HALF : (half + 1) * HALF, :] = lines
 
 
-def lookup(at_ref, groups_ref, place_ref, same_ref, other_ref):
-    column, odd = at_ref[0], at_ref[1] % 2
+def lookup(groups_ref, place_ref, same_ref, other_ref):
+    column, odd = lax.axis_index("col"), lax.axis_index("row") % 2
     groups = groups_ref[...].astype(F32).astype(BF16)
     line = lax.broadcasted_iota(jnp.int32, (NB, WIDE), 0)
     lane = lax.broadcasted_iota(jnp.int32, (NB, WIDE), 1)
@@ -115,8 +118,8 @@
         out_ref[...] = lax.dot_general(hit, spread, (((0,), (0,)), ((), ())), preferred_element_type=F32)
 
 
-def left_body(at_ref, groups_ref, ground_ref, response_ref, out_ref, place_ref, same_ref, other_ref, turned):
-    lookup(at_ref, groups_ref, place_ref, same_ref, other_ref)
+def left_body(groups_ref, ground_ref, response_ref, out_ref, place_ref, same_ref, other_ref, turned):
+    lookup(groups_ref, place_ref, same_ref, other_ref)
     src = lax.broadcasted_iota(jnp.int32, (256, 256), 0)
     dst = lax.broadcasted_iota(jnp.int32, (256, 256), 1)
     two, half, col = src // 128, src // BLK % 2, src % BLK
@@ -218,7 +221,6 @@
     smem = pl.BlockSpec(memory_space=pltpu.SMEM)
     turned = pltpu.VMEM((SLOTS * TILES, 128), F32)
     window = pltpu.VMEM((2, 5 * ROWS * BLK, 2 * WIDE), BF16)
-    at = jnp.stack([lax.axis_index("col"), lax.axis_index("row")]).astype(jnp.int32)
     cut = call(
         slice_body,
         "slice",
@@ -229,10 +231,11 @@
             pltpu.VMEM((2, 2, ROWS * HALF, 128), F32),
             pltpu.SemaphoreType.DMA((2, PIECES)),
         ],
-        [smem] + [pl.BlockSpec(memory_space=pltpu.HBM)] * 2,
+        [pl.BlockSpec(memory_space=pltpu.HBM)] * 2,
         2 * 1024 * 1024 * 128,
         5 << 20,
-    )(at, ground, response)
+        SLICE_BYTES,
+    )(ground, response)
     cut, ground, response, pattern = lax.optimization_barrier((cut, ground, response, pattern))
     pieces = surround(cut)
     groups = jnp.where(pattern < 0, -1, pattern // ROWS).T
@@ -241,10 +244,10 @@
         "left",
         (jax.ShapeDtypeStruct((ROWS, 2 * BLK, SLOTS * BLK), BF16), jax.ShapeDtypeStruct((1, WIDE), jnp.int32), mask, mask),
         [turned],
-        [smem] + in_vmem(3),
+        in_vmem(3),
         2 * 4096 * 256 * 256,
         5 << 20,
-    )(at, groups, ground, response)
+    )(groups, ground, response)
     flops = 2 * ROWS * BLK * 1024 * 128
     pair, mixed = call(
         first_body,

time: 81.7 us -> 80.3 us (0.983)
  local copies, waits for them, and re-layouts: 2.46 us -> 1.23 us
    unnamed x8, local copies, waits for them, and re-layouts: 2.46 us -> 1.23 us
    pallas_call x1, Pallas kernels: 2.63 us -> 3.69 us  [local(): call(slice_body, 'slice', rows, [pltpu.VMEM((2, ROWS, SLOTS, BLK * BLK),...]
  transfers between devices with their start and end apart: 8 -> 8, of which waited for: 5 -> 5; matrix products, arithmetic and copies ran while one was open for 0% -> 0% of each run, Pallas kernels for 4% -> 3%
where the time goes in v3:
time: 80.3 us; the launch traced here: 79.9 us
  starting transfers between devices  37.6 us (47%)
  waiting for transfers between devices  17.6 us (22%)
  Pallas kernels  12.5 us (16%)
  blocking collectives  10.7 us (13%)
  local copies, waits for them, and re-layouts  1.23 us (2%)
    ppermute x8, starting transfers between devices, from_afar(): return lax.ppermute(block, ('col', 'row'), route)  37.6 us
    ppermute x8, waiting for transfers between devices, from_afar(): return lax.ppermute(block, ('col', 'row'), route)  17.6 us
    all_to_all x1, blocking collectives, local(): part = lax.all_to_all(part, 'row', 0, 0, tiled=True)  10.7 us
    pallas_call x1, Pallas kernels, local(): call(slice_body, 'slice', rows, [pltpu.VMEM((2, ROWS, SLOTS, BLK * BLK),...  3.69 us
    pallas_call x1, Pallas kernels, local(): call(second_body, 'second', jax.ShapeDtypeStruct((ROWS, BLK, WIDE), BF16)...  2.67 us
    pallas_call x1, Pallas kernels, local(): call(first_body, 'first', (rows, jax.ShapeDtypeStruct((ROWS, BLK, WIDE),...  2.54 us
    pallas_call x1, Pallas kernels, local(): call(left_body, 'left', (jax.ShapeDtypeStruct((ROWS, 2 * BLK, SLOTS * BLK...  2.45 us
  transfers between devices with their start and end apart: 8, of which 5 were waited for; matrix products, arithmetic and copies ran while one was open for 0% of the time, Pallas kernels for 3%

profile of v3, /device:TPU:1, one launch (start us, length us, event | category | flops | bytes accessed | tf_op | source)
XLA Modules:
  0.0 79.9 jit_solution(7979373235497372250)
XLA Ops:
  0.0 0.0 copy-start
  0.0 0.0 copy-start.3
  0.0 3.7 %shard_map.37.x4 = bf16[2,8,64,128]{3,2,1,0:T(8,128)(2,1)} custom-call(bf16[8,16,4096]{2,1,0:T(8,128)(2,1)} %ground_ref, bf16[8,16,4096]{2,1,0:T(8,128)(2,1)} %response_ref), custom_call_target="tpu_custom_call" | custom-call | flops 268435456 | bytes 5242880 | tf_op jit(solution)/shard_map/pallas_call | solution.py:224
  3.7 5.7 %collective-permute-start.3 = (bf16[2,8,64,128]{3,2,1,0:T(8,128)(2,1)}, bf16[2,8,64,128]{3,2,1,0:T(8,128)(2,1)S(1)}, u32[]{:S(2)}, u32[]{:S(2)}) collective-permute-start(bf16[2,8,64,128]{3,2,1,0:T(8,128)(2,1)} %shard_map.37.x4), channel_id=1, source_target_pairs={{0,496},{1,17},{2,498},{3,19},{4,500},{5,21},{6,502},{7,23},{8,504... | collective-permute-start | bytes 786440 | tf_op jit(solution)/shard_map/ppermute | solution.py:211
  9.4 3.5 %collective-permute-start.2 = (bf16[2,8,64,128]{3,2,1,0:T(8,128)(2,1)}, bf16[2,8,64,128]{3,2,1,0:T(8,128)(2,1)S(1)}, u32[]{:S(2)}, u32[]{:S(2)}) collective-permute-start(bf16[2,8,64,128]{3,2,1,0:T(8,128)(2,1)} %shard_map.37.x4), channel_id=1, source_target_pairs={{0,504},{1,9},{2,506},{3,11},{4,508},{5,13},{6,510},{7,15},{8,0},{... | collective-permute-start | bytes 786440 | tf_op jit(solution)/shard_map/ppermute | solution.py:211
  13.0 10.1 %collective-permute-start.1 = (bf16[2,8,64,128]{3,2,1,0:T(8,128)(2,1)}, bf16[2,8,64,128]{3,2,1,0:T(8,128)(2,1)S(1)}, u32[]{:S(2)}, u32[]{:S(2)}) collective-permute-start(bf16[2,8,64,128]{3,2,1,0:T(8,128)(2,1)} %shard_map.37.x4), channel_id=1, source_target_pairs={{0,16},{1,497},{2,18},{3,499},{4,20},{5,501},{6,22},{7,503},{8,24}... | collective-permute-start | bytes 786440 | tf_op jit(solution)/shard_map/ppermute | solution.py:211
  23.1 3.1 %collective-permute-start = (bf16[2,8,64,128]{3,2,1,0:T(8,128)(2,1)}, bf16[2,8,64,128]{3,2,1,0:T(8,128)(2,1)S(1)}, u32[]{:S(2)}, u32[]{:S(2)}) collective-permute-start(bf16[2,8,64,128]{3,2,1,0:T(8,128)(2,1)} %shard_map.37.x4), channel_id=1, source_target_pairs={{0,8},{1,505},{2,10},{3,507},{4,12},{5,509},{6,14},{7,511},{8,16},... | collective-permute-start | bytes 786440 | tf_op jit(solution)/shard_map/ppermute | solution.py:211
  26.2 0.0 copy-done.3
  26.3 0.0 copy-done
  26.3 0.0 copy-start.1
  26.3 1.2 %copy-done.1 = bf16[8,16,4096]{2,1,0:T(8,128)(2,1)S(1)} copy-done((bf16[8,16,4096]{2,1,0:T(8,128)(2,1)S(1)}, bf16[8,16,4096]{2,1,0:T(8,128)(2,1)}, u32[]{:S(2)}) %copy-start.1) | copy-done | bytes 1048600
  27.5 0.0 copy-start.2
  27.5 2.5 %shard_map.38 = (bf16[8,128,1024]{2,1,0:T(8,128)(2,1)S(1)}, s32[1,128]{1,0:T(1,128)S(1)}, f32[128,128]{1,0:T(8,128)S(1)}, f32[128,128]{1,0:T(8,128)S(1)}) custom-call(s32[16,512]{1,0:T(8,128)S(1)} %fusion.2.groups_ref, bf16[8,16,4096]{2,1,0:T(8,128)(2,1)S(1)} %copy-done, bf16[8,16,4096]{2,1,0:T(8,128)(2,1)S(1)} %copy-done.1), custom_call_target="tpu_custom_call" | custom-call | flops 536870912 | bytes 5242880 | tf_op jit(solution)/shard_map/pallas_call | solution.py:242
  30.0 0.0 collective-permute-done.3.x3
  30.0 0.0 collective-permute-done.2.x2
  30.0 3.8 %collective-permute-done.1.x1 = bf16[2,8,64,128]{3,2,1,0:T(8,128)(2,1)S(1)} collective-permute-done((bf16[2,8,64,128]{3,2,1,0:T(8,128)(2,1)}, bf16[2,8,64,128]{3,2,1,0:T(8,128)(2,1)S(1)}, u32[]{:S(2)}, u32[]{:S(2)}) %collective-permute-start.1) | collective-permute-done | bytes 262176 | tf_op jit(solution)/shard_map/ppermute | solution.py:211
  33.8 3.6 %collective-permute-done.x0 = bf16[2,8,64,128]{3,2,1,0:T(8,128)(2,1)S(1)} collective-permute-done((bf16[2,8,64,128]{3,2,1,0:T(8,128)(2,1)}, bf16[2,8,64,128]{3,2,1,0:T(8,128)(2,1)S(1)}, u32[]{:S(2)}, u32[]{:S(2)}) %collective-permute-start) | collective-permute-done | bytes 262176 | tf_op jit(solution)/shard_map/ppermute | solution.py:211
  37.3 0.0 copy-done.2
  37.4 2.5 %shard_map.39 = (bf16[2,8,64,128]{3,2,1,0:T(8,128)(2,1)S(1)}, f32[8,64,128]{2,1,0:T(8,128)S(1)}) custom-call(s32[1,128]{1,0:T(1,128)S(1)} %get-tuple-element.18.where_ref, f32[128,128]{1,0:T(8,128)S(1)} %get-tuple-element.19.same_ref, f32[128,128]{1,0:T(8,128)S(1)} %get-tuple-element.20.other_ref, bf16[2,8,64,128]{3,2,1,0:T(8,128)(2,1)S(1)} %collective-permute-done.x0, ...), custom_call_target="tpu_custom_call" | custom-call | flops 402653184 | bytes 5242880 | tf_op jit(solution)/shard_map/pallas_call | solution.py:252
  39.9 1.9 %collective-permute-start.7 = (bf16[2,8,64,128]{3,2,1,0:T(8,128)(2,1)S(1)}, bf16[2,8,64,128]{3,2,1,0:T(8,128)(2,1)S(1)}, u32[]{:S(2)}, u32[]{:S(2)}) collective-permute-start(bf16[2,8,64,128]{3,2,1,0:T(8,128)(2,1)S(1)} %get-tuple-element.23.x4), channel_id=1, source_target_pairs={{0,496},{1,17},{2,498},{3,19},{4,500},{5,21},{6,502},{7,23},{8,504... | collective-permute-start | bytes 786440 | tf_op jit(solution)/shard_map/ppermute | solution.py:211
  41.8 1.9 %collective-permute-start.6 = (bf16[2,8,64,128]{3,2,1,0:T(8,128)(2,1)S(1)}, bf16[2,8,64,128]{3,2,1,0:T(8,128)(2,1)S(1)}, u32[]{:S(2)}, u32[]{:S(2)}) collective-permute-start(bf16[2,8,64,128]{3,2,1,0:T(8,128)(2,1)S(1)} %get-tuple-element.23.x4), channel_id=1, source_target_pairs={{0,504},{1,9},{2,506},{3,11},{4,508},{5,13},{6,510},{7,15},{8,0},{... | collective-permute-start | bytes 786440 | tf_op jit(solution)/shard_map/ppermute | solution.py:211
  43.8 8.2 %collective-permute-start.5 = (bf16[2,8,64,128]{3,2,1,0:T(8,128)(2,1)S(1)}, bf16[2,8,64,128]{3,2,1,0:T(8,128)(2,1)S(1)}, u32[]{:S(2)}, u32[]{:S(2)}) collective-permute-start(bf16[2,8,64,128]{3,2,1,0:T(8,128)(2,1)S(1)} %get-tuple-element.23.x4), channel_id=1, source_target_pairs={{0,16},{1,497},{2,18},{3,499},{4,20},{5,501},{6,22},{7,503},{8,24}... | collective-permute-start | bytes 786440 | tf_op jit(solution)/shard_map/ppermute | solution.py:211
  52.0 3.1 %collective-permute-start.4 = (bf16[2,8,64,128]{3,2,1,0:T(8,128)(2,1)S(1)}, bf16[2,8,64,128]{3,2,1,0:T(8,128)(2,1)S(1)}, u32[]{:S(2)}, u32[]{:S(2)}) collective-permute-start(bf16[2,8,64,128]{3,2,1,0:T(8,128)(2,1)S(1)} %get-tuple-element.23.x4), channel_id=1, source_target_pairs={{0,8},{1,505},{2,10},{3,507},{4,12},{5,509},{6,14},{7,511},{8,16},... | collective-permute-start | bytes 786440 | tf_op jit(solution)/shard_map/ppermute | solution.py:211
  55.1 0.0 collective-permute-done.7.x3
  55.1 1.2 %collective-permute-done.6.x2 = bf16[2,8,64,128]{3,2,1,0:T(8,128)(2,1)S(1)} collective-permute-done((bf16[2,8,64,128]{3,2,1,0:T(8,128)(2,1)S(1)}, bf16[2,8,64,128]{3,2,1,0:T(8,128)(2,1)S(1)}, u32[]{:S(2)}, u32[]{:S(2)}) %collective-permute-start.6) | collective-permute-done | bytes 262176 | tf_op jit(solution)/shard_map/ppermute | solution.py:211
  56.3 2.9 %collective-permute-done.5.x1 = bf16[2,8,64,128]{3,2,1,0:T(8,128)(2,1)S(1)} collective-permute-done((bf16[2,8,64,128]{3,2,1,0:T(8,128)(2,1)S(1)}, bf16[2,8,64,128]{3,2,1,0:T(8,128)(2,1)S(1)}, u32[]{:S(2)}, u32[]{:S(2)}) %collective-permute-start.5) | collective-permute-done | bytes 262176 | tf_op jit(solution)/shard_map/ppermute | solution.py:211
  59.2 6.1 %collective-permute-done.4.x0 = bf16[2,8,64,128]{3,2,1,0:T(8,128)(2,1)S(1)} collective-permute-done((bf16[2,8,64,128]{3,2,1,0:T(8,128)(2,1)S(1)}, bf16[2,8,64,128]{3,2,1,0:T(8,128)(2,1)S(1)}, u32[]{:S(2)}, u32[]{:S(2)}) %collective-permute-start.4) | collective-permute-done | bytes 262176 | tf_op jit(solution)/shard_map/ppermute | solution.py:211
  65.3 2.7 %shard_map.40 = bf16[8,64,128]{2,1,0:T(8,128)(2,1)S(1)} custom-call(s32[1,128]{1,0:T(1,128)S(1)} %get-tuple-element.18.where_ref, f32[128,128]{1,0:T(8,128)S(1)} %get-tuple-element.19.same_ref, f32[128,128]{1,0:T(8,128)S(1)} %get-tuple-element.20.other_ref, bf16[2,8,64,128]{3,2,1,0:T(8,128)(2,1)S(1)} %collective-permute-done.4.x0, ...), custom_call_target="tpu_custom_call" | custom-call | flops 268435456 | bytes 5242880 | tf_op jit(solution)/shard_map/pallas_call | solution.py:262
  68.0 10.7 %all_to_all.5.in_ref = bf16[8,64,128]{2,1,0:T(8,128)(2,1)S(1)} all-to-all(bf16[8,64,128]{2,1,0:T(8,128)(2,1)S(1)} %shard_map.40), channel_id=1, replica_groups=mesh['col'=64,'row'=8] {'row'}, dimensions={0} | all-to-all | bytes 262144 | tf_op jit(solution)/shard_map/all_to_all | solution.py:271
  78.7 1.2 %shard_map.41 = bf16[1,16,4096]{2,1,0:T(8,128)(2,1)} custom-call(bf16[8,64,128]{2,1,0:T(8,128)(2,1)S(1)} %all_to_all.5.in_ref), custom_call_target="tpu_custom_call" | custom-call | bytes 262144 | tf_op jit(solution)/shard_map/pallas_call | solution.py:272
  (1 shorter events, 0.0 us)
Async XLA Ops:
  0.0 26.3 %copy-start = (bf16[8,16,4096]{2,1,0:T(8,128)(2,1)S(1)}, bf16[8,16,4096]{2,1,0:T(8,128)(2,1)}, u32[]{:S(2)}) copy-start(bf16[8,16,4096]{2,1,0:T(8,128)(2,1)} %ground_ref) | copy-start | bytes 3145732
  0.0 26.2 %copy-start.3 = (s32[512,16]{0,1:T(8,128)S(1)}, s32[512,16]{0,1:T(8,128)}, u32[]{:S(2)}) copy-start(s32[512,16]{0,1:T(8,128)} %param.5) | copy-start | bytes 98308
  3.7 26.3 %collective-permute-start.3 = (bf16[2,8,64,128]{3,2,1,0:T(8,128)(2,1)}, bf16[2,8,64,128]{3,2,1,0:T(8,128)(2,1)S(1)}, u32[]{:S(2)}, u32[]{:S(2)}) collective-permute-start(bf16[2,8,64,128]{3,2,1,0:T(8,128)(2,1)} %shard_map.37.x4), channel_id=1, source_target_pairs={{0,496},{1,17},{2,498},{3,19},{4,500},{5,21},{6,502},{7,23},{8,504... | collective-permute-start | bytes 786440 | tf_op jit(solution)/shard_map/ppermute | solution.py:211
  9.4 20.5 %collective-permute-start.2 = (bf16[2,8,64,128]{3,2,1,0:T(8,128)(2,1)}, bf16[2,8,64,128]{3,2,1,0:T(8,128)(2,1)S(1)}, u32[]{:S(2)}, u32[]{:S(2)}) collective-permute-start(bf16[2,8,64,128]{3,2,1,0:T(8,128)(2,1)} %shard_map.37.x4), channel_id=1, source_target_pairs={{0,504},{1,9},{2,506},{3,11},{4,508},{5,13},{6,510},{7,15},{8,0},{... | collective-permute-start | bytes 786440 | tf_op jit(solution)/shard_map/ppermute | solution.py:211
  13.0 20.8 %collective-permute-start.1 = (bf16[2,8,64,128]{3,2,1,0:T(8,128)(2,1)}, bf16[2,8,64,128]{3,2,1,0:T(8,128)(2,1)S(1)}, u32[]{:S(2)}, u32[]{:S(2)}) collective-permute-start(bf16[2,8,64,128]{3,2,1,0:T(8,128)(2,1)} %shard_map.37.x4), channel_id=1, source_target_pairs={{0,16},{1,497},{2,18},{3,499},{4,20},{5,501},{6,22},{7,503},{8,24}... | collective-permute-start | bytes 786440 | tf_op jit(solution)/shard_map/ppermute | solution.py:211
  23.1 14.2 %collective-permute-start = (bf16[2,8,64,128]{3,2,1,0:T(8,128)(2,1)}, bf16[2,8,64,128]{3,2,1,0:T(8,128)(2,1)S(1)}, u32[]{:S(2)}, u32[]{:S(2)}) collective-permute-start(bf16[2,8,64,128]{3,2,1,0:T(8,128)(2,1)} %shard_map.37.x4), channel_id=1, source_target_pairs={{0,8},{1,505},{2,10},{3,507},{4,12},{5,509},{6,14},{7,511},{8,16},... | collective-permute-start | bytes 786440 | tf_op jit(solution)/shard_map/ppermute | solution.py:211
  26.3 1.2 %copy-start.1 = (bf16[8,16,4096]{2,1,0:T(8,128)(2,1)S(1)}, bf16[8,16,4096]{2,1,0:T(8,128)(2,1)}, u32[]{:S(2)}) copy-start(bf16[8,16,4096]{2,1,0:T(8,128)(2,1)} %response_ref) | copy-start | bytes 3145732
  27.5 9.8 %copy-start.2 = (bf16[2,8,64,128]{3,2,1,0:T(8,128)(2,1)S(1)}, bf16[2,8,64,128]{3,2,1,0:T(8,128)(2,1)}, u32[]{:S(2)}) copy-start(bf16[2,8,64,128]{3,2,1,0:T(8,128)(2,1)} %shard_map.37.x4) | copy-start | bytes 786436
  39.9 15.2 %collective-permute-start.7 = (bf16[2,8,64,128]{3,2,1,0:T(8,128)(2,1)S(1)}, bf16[2,8,64,128]{3,2,1,0:T(8,128)(2,1)S(1)}, u32[]{:S(2)}, u32[]{:S(2)}) collective-permute-start(bf16[2,8,64,128]{3,2,1,0:T(8,128)(2,1)S(1)} %get-tuple-element.23.x4), channel_id=1, source_target_pairs={{0,496},{1,17},{2,498},{3,19},{4,500},{5,21},{6,502},{7,23},{8,504... | collective-permute-start | bytes 786440 | tf_op jit(solution)/shard_map/ppermute | solution.py:211
  41.8 14.5 %collective-permute-start.6 = (bf16[2,8,64,128]{3,2,1,0:T(8,128)(2,1)S(1)}, bf16[2,8,64,128]{3,2,1,0:T(8,128)(2,1)S(1)}, u32[]{:S(2)}, u32[]{:S(2)}) collective-permute-start(bf16[2,8,64,128]{3,2,1,0:T(8,128)(2,1)S(1)} %get-tuple-element.23.x4), channel_id=1, source_target_pairs={{0,504},{1,9},{2,506},{3,11},{4,508},{5,13},{6,510},{7,15},{8,0},{... | collective-permute-start | bytes 786440 | tf_op jit(solution)/shard_map/ppermute | solution.py:211
  43.8 15.4 %collective-permute-start.5 = (bf16[2,8,64,128]{3,2,1,0:T(8,128)(2,1)S(1)}, bf16[2,8,64,128]{3,2,1,0:T(8,128)(2,1)S(1)}, u32[]{:S(2)}, u32[]{:S(2)}) collective-permute-start(bf16[2,8,64,128]{3,2,1,0:T(8,128)(2,1)S(1)} %get-tuple-element.23.x4), channel_id=1, source_target_pairs={{0,16},{1,497},{2,18},{3,499},{4,20},{5,501},{6,22},{7,503},{8,24}... | collective-permute-start | bytes 786440 | tf_op jit(solution)/shard_map/ppermute | solution.py:211
  52.0 13.4 %collective-permute-start.4 = (bf16[2,8,64,128]{3,2,1,0:T(8,128)(2,1)S(1)}, bf16[2,8,64,128]{3,2,1,0:T(8,128)(2,1)S(1)}, u32[]{:S(2)}, u32[]{:S(2)}) collective-permute-start(bf16[2,8,64,128]{3,2,1,0:T(8,128)(2,1)S(1)} %get-tuple-element.23.x4), channel_id=1, source_target_pairs={{0,8},{1,505},{2,10},{3,507},{4,12},{5,509},{6,14},{7,511},{8,16},... | collective-permute-start | bytes 786440 | tf_op jit(solution)/shard_map/ppermute | solution.py:211

commit v4 on v3

--- a/solution.py
+++ b/solution.py
@@ -15,11 +15,10 @@
 TILES = BLK * BLK // 128
 HALF = TILES
 F32, BF16 = jnp.float32, jnp.bfloat16
-PIECES = 2
 VMEM_BYTES = 16 * 1024 * 1024
 
 
-SLICE_BYTES = int(62.5 * 1024 * 1024)
+SLICE_BYTES = int(63.1 * 1024 * 1024)
 
 
 def call(body, name, out_shape, scratch, in_specs, flops, moved, vmem=VMEM_BYTES):
@@ -63,9 +62,7 @@
 def slice_body(ground_hbm, response_hbm, out_ref, held, picked, placed, arrived):
     copies = []
     for m, rows_hbm in enumerate((ground_hbm, response_hbm)):
-        for i in range(PIECES):
-            part = pl.ds(i * (ROWS // PIECES), ROWS // PIECES)
-            copies.append(pltpu.make_async_copy(rows_hbm.at[part], held.at[m, part], arrived.at[m, i]))
+        copies.append(pltpu.make_async_copy(rows_hbm, held.at[m], arrived.at[m]))
     for copy in copies:
         copy.start()
     line = lax.broadcasted_iota(jnp.int32, (1024, 128), 0)
@@ -73,8 +70,7 @@
     col = line % BLK - 8 * lax.axis_index("row")
     pick = jnp.where((col >= 0) & (col < 8) & (lane == line // BLK * 8 + col), 1.0, 0.0).astype(BF16)
     for m in range(2):
-        for copy in copies[m * PIECES : (m + 1) * PIECES]:
-            copy.wait()
+        copies[m].wait()
         flat = held[m].reshape(ROWS * SLOTS, BLK * BLK)
         for n in range(4):
             picked[m, n] = jnp.dot(flat[:, n * 1024 : (n + 1) * 1024], pick, preferred_element_type=F32)
@@ -111,11 +107,13 @@
     i = lax.broadcasted_iota(jnp.int32, (SLOTS, SLOTS), 0)
     j = lax.broadcasted_iota(jnp.int32, (SLOTS, SLOTS), 1)
     swap = jnp.where(i // K8 * K8 + 1 - i % K8 == j, 1.0, 0.0).astype(BF16)
-    crossed = jnp.dot(swap, far.astype(BF16), preferred_element_type=F32)
     spread = jnp.where(pair // 8 == slot % K8 * ROWS + slot // K8, 1.0, 0.0).astype(BF16)
-    for found, out_ref in ((far, same_ref), (crossed, other_ref)):
-        hit = jnp.where((found == near) & (near >= 0.0) & live, 1.0, 0.0).astype(BF16)
-        out_ref[...] = lax.dot_general(hit, spread, (((0,), (0,)), ((), ())), preferred_element_type=F32)
+    facing = jnp.dot(swap, near.astype(BF16), preferred_element_type=F32)
+    for ours, out_ref in ((near, same_ref), (facing, other_ref)):
+        hit = jnp.where((far == ours) & (ours >= 0.0) & live, 1.0, 0.0).astype(BF16)
+        mask = lax.dot_general(hit, spread, (((0,), (0,)), ((), ())), preferred_element_type=F32)
+        for n in range(ROWS * SLOTS):
+            out_ref[n] = jnp.broadcast_to(mask[n : n + 1], (16, WIDE)).astype(BF16)
 
 
 def left_body(groups_ref, ground_ref, response_ref, out_ref, place_ref, same_ref, other_ref, turned):
@@ -143,10 +141,8 @@
 def fill_window(window, pieces):
     for o, piece in enumerate(pieces):
         for m in range(2):
-            flat = piece[m].reshape(ROWS * BLK, 128)
             at = o * ROWS * BLK
-            window[m, at : at + ROWS * BLK, 0:128] = flat
-            window[m, at : at + ROWS * BLK, 128:256] = jnp.concatenate([flat[:, 64:128], flat[:, 0:64]], axis=1)
+            window[m, at : at + ROWS * BLK, :] = piece[m].reshape(ROWS * BLK, WIDE)
 
 
 def rights(window, where_ref, same_ref, other_ref, g):
@@ -154,13 +150,16 @@
     for a in range(SLOTS):
         i = g * SLOTS + a
         at = pl.multiple_of(where_ref[0, i] * BLK, BLK)
-        same = jnp.broadcast_to(same_ref[pl.ds(i, 1), :], (16, 128)).astype(BF16)
-        other = jnp.broadcast_to(other_ref[pl.ds(i, 1), :], (16, 128)).astype(BF16)
-        same, other = jnp.concatenate([same] * 4, axis=0), jnp.concatenate([other] * 4, axis=0)
+        same = jnp.concatenate([same_ref[i]] * 4, axis=0)
+        other = jnp.concatenate([other_ref[i]] * 4, axis=0)
         for m in range(2):
-            both = window[m, pl.ds(at, BLK), :]
-            stacks[m].append(both[:, 0:128] * same + both[:, 128:256] * other)
+            blocks = window[m, pl.ds(at, BLK), :]
+            stacks[m].append(jnp.concatenate([blocks * same, blocks * other], axis=1))
     return [jnp.concatenate(stack, axis=0) for stack in stacks]
+
+
+def settle(product):
+    return product[:, 0:WIDE] + pltpu.roll(product[:, WIDE:], WIDE // 2, 1)
 
 
 def first_body(where_ref, same_ref, other_ref, x0, x1, x2, x3, x4, left_ref, pair_ref, mixed_ref, window):
@@ -168,11 +167,11 @@
 
     def step(g, _):
         ground, response = rights(window, where_ref, same_ref, other_ref, g)
-        both = jnp.concatenate([ground, response], axis=1)
-        product = jnp.dot(left_ref[g], both, preferred_element_type=F32)
-        mixed = product[0:BLK, 0:128] + product[BLK:, 128:256]
+        product = jnp.dot(left_ref[g], ground, preferred_element_type=F32)
+        crossed = jnp.dot(left_ref[g, BLK:], response, preferred_element_type=F32)
+        mixed = settle(product[0:BLK] + crossed)
         mixed_ref[g] = mixed
-        pair_ref[0, g] = product[BLK:, 0:128].astype(BF16)
+        pair_ref[0, g] = settle(product[BLK:]).astype(BF16)
         pair_ref[1, g] = mixed.astype(BF16)
         return 0
 
@@ -185,7 +184,7 @@
     def step(g, _):
         square, mixed = rights(window, where_ref, same_ref, other_ref, g)
         cubic = jnp.dot(left_ref[g, 0:BLK], square, preferred_element_type=F32)
-        cubic = cubic + jnp.dot(left_ref[g, BLK:], mixed, preferred_element_type=F32)
+        cubic = settle(cubic + jnp.dot(left_ref[g, BLK:], mixed, preferred_element_type=F32))
         out_ref[g] = (3.0 * mixed_ref[g] - 2.0 * cubic).astype(BF16)
         return 0
 
@@ -217,10 +216,10 @@
 
 def local(ground, response, pattern):
     rows = jax.ShapeDtypeStruct((2, ROWS, BLK, WIDE), BF16)
-    mask = jax.ShapeDtypeStruct((ROWS * SLOTS, WIDE), F32)
+    mask = jax.ShapeDtypeStruct((ROWS * SLOTS, 16, WIDE), BF16)
     smem = pl.BlockSpec(memory_space=pltpu.SMEM)
     turned = pltpu.VMEM((SLOTS * TILES, 128), F32)
-    window = pltpu.VMEM((2, 5 * ROWS * BLK, 2 * WIDE), BF16)
+    window = pltpu.VMEM((2, 5 * ROWS * BLK, WIDE), BF16)
     cut = call(
         slice_body,
         "slice",
@@ -229,7 +228,7 @@
             pltpu.VMEM((2, ROWS, SLOTS, BLK * BLK), BF16),
             pltpu.VMEM((2, 4, ROWS * SLOTS, 128), F32),
             pltpu.VMEM((2, 2, ROWS * HALF, 128), F32),
-            pltpu.SemaphoreType.DMA((2, PIECES)),
+            pltpu.SemaphoreType.DMA((2,)),
         ],
         [pl.BlockSpec(memory_space=pltpu.HBM)] * 2,
         2 * 1024 * 1024 * 128,

time: 80.3 us -> 79.5 us (0.990)
  local copies, waits for them, and re-layouts: 1.23 us -> 2.45 us
  waiting for transfers between devices: 17.6 us -> 16.4 us
    unnamed x8, local copies, waits for them, and re-layouts: 1.23 us -> 2.45 us
    ppermute x8, waiting for transfers between devices: 17.6 us -> 16.4 us  [from_afar(): return lax.ppermute(block, ('col', 'row'), route)]
where the time goes in v4:
time: 79.5 us; the launch traced here: 79.1 us
  starting transfers between devices  37.6 us (47%)
  waiting for transfers between devices  16.4 us (21%)
  Pallas kernels  11.7 us (15%)
  blocking collectives  10.7 us (13%)
  local copies, waits for them, and re-layouts  2.45 us (3%)
    ppermute x8, starting transfers between devices, from_afar(): return lax.ppermute(block, ('col', 'row'), route)  37.6 us
    ppermute x8, waiting for transfers between devices, from_afar(): return lax.ppermute(block, ('col', 'row'), route)  16.4 us
    all_to_all x1, blocking collectives, local(): part = lax.all_to_all(part, 'row', 0, 0, tiled=True)  10.7 us
    pallas_call x1, Pallas kernels, local(): call(slice_body, 'slice', rows, [pltpu.VMEM((2, ROWS, SLOTS, BLK * BLK),...  3.61 us
    pallas_call x1, Pallas kernels, local(): call(left_body, 'left', (jax.ShapeDtypeStruct((ROWS, 2 * BLK, SLOTS * BLK...  2.46 us
    unnamed x8, local copies, waits for them, and re-layouts  2.45 us
    pallas_call x1, Pallas kernels, local(): call(second_body, 'second', jax.ShapeDtypeStruct((ROWS, BLK, WIDE), BF16)...  2.29 us
    pallas_call x1, Pallas kernels, local(): call(first_body, 'first', (rows, jax.ShapeDtypeStruct((ROWS, BLK, WIDE),...  2.18 us
  transfers between devices with their start and end apart: 8, of which 5 were waited for; matrix products, arithmetic and copies ran while one was open for 0% of the time, Pallas kernels for 3%

profile of v4, /device:TPU:1, one launch (start us, length us, event | category | flops | bytes accessed | tf_op | source)
XLA Modules:
  0.0 79.1 jit_solution(2497131041032822106)
XLA Ops:
  0.0 0.0 copy-start.3
  0.0 3.6 %shard_map.37.x4 = bf16[2,8,64,128]{3,2,1,0:T(8,128)(2,1)} custom-call(bf16[8,16,4096]{2,1,0:T(8,128)(2,1)} %ground_ref, bf16[8,16,4096]{2,1,0:T(8,128)(2,1)} %response_ref), custom_call_target="tpu_custom_call" | custom-call | flops 268435456 | bytes 5242880 | tf_op jit(solution)/shard_map/pallas_call | solution.py:223
  3.6 5.7 %collective-permute-start.3 = (bf16[2,8,64,128]{3,2,1,0:T(8,128)(2,1)}, bf16[2,8,64,128]{3,2,1,0:T(8,128)(2,1)S(1)}, u32[]{:S(2)}, u32[]{:S(2)}) collective-permute-start(bf16[2,8,64,128]{3,2,1,0:T(8,128)(2,1)} %shard_map.37.x4), channel_id=1, source_target_pairs={{0,496},{1,17},{2,498},{3,19},{4,500},{5,21},{6,502},{7,23},{8,504... | collective-permute-start | bytes 786440 | tf_op jit(solution)/shard_map/ppermute | solution.py:210
  9.4 3.5 %collective-permute-start.2 = (bf16[2,8,64,128]{3,2,1,0:T(8,128)(2,1)}, bf16[2,8,64,128]{3,2,1,0:T(8,128)(2,1)S(1)}, u32[]{:S(2)}, u32[]{:S(2)}) collective-permute-start(bf16[2,8,64,128]{3,2,1,0:T(8,128)(2,1)} %shard_map.37.x4), channel_id=1, source_target_pairs={{0,504},{1,9},{2,506},{3,11},{4,508},{5,13},{6,510},{7,15},{8,0},{... | collective-permute-start | bytes 786440 | tf_op jit(solution)/shard_map/ppermute | solution.py:210
  12.9 10.1 %collective-permute-start.1 = (bf16[2,8,64,128]{3,2,1,0:T(8,128)(2,1)}, bf16[2,8,64,128]{3,2,1,0:T(8,128)(2,1)S(1)}, u32[]{:S(2)}, u32[]{:S(2)}) collective-permute-start(bf16[2,8,64,128]{3,2,1,0:T(8,128)(2,1)} %shard_map.37.x4), channel_id=1, source_target_pairs={{0,16},{1,497},{2,18},{3,499},{4,20},{5,501},{6,22},{7,503},{8,24}... | collective-permute-start | bytes 786440 | tf_op jit(solution)/shard_map/ppermute | solution.py:210
  23.1 3.1 %collective-permute-start = (bf16[2,8,64,128]{3,2,1,0:T(8,128)(2,1)}, bf16[2,8,64,128]{3,2,1,0:T(8,128)(2,1)S(1)}, u32[]{:S(2)}, u32[]{:S(2)}) collective-permute-start(bf16[2,8,64,128]{3,2,1,0:T(8,128)(2,1)} %shard_map.37.x4), channel_id=1, source_target_pairs={{0,8},{1,505},{2,10},{3,507},{4,12},{5,509},{6,14},{7,511},{8,16},... | collective-permute-start | bytes 786440 | tf_op jit(solution)/shard_map/ppermute | solution.py:210
  26.2 0.0 copy-done.3
  26.2 0.0 copy-start
  26.2 1.2 %copy-done = bf16[8,16,4096]{2,1,0:T(8,128)(2,1)S(1)} copy-done((bf16[8,16,4096]{2,1,0:T(8,128)(2,1)S(1)}, bf16[8,16,4096]{2,1,0:T(8,128)(2,1)}, u32[]{:S(2)}) %copy-start) | copy-done | bytes 1048600
  27.4 0.0 copy-start.1
  27.4 1.2 %copy-done.1 = bf16[8,16,4096]{2,1,0:T(8,128)(2,1)S(1)} copy-done((bf16[8,16,4096]{2,1,0:T(8,128)(2,1)S(1)}, bf16[8,16,4096]{2,1,0:T(8,128)(2,1)}, u32[]{:S(2)}) %copy-start.1) | copy-done | bytes 1048600
  28.6 0.0 copy-start.2
  28.6 2.5 %shard_map.38 = (bf16[8,128,1024]{2,1,0:T(8,128)(2,1)S(1)}, s32[1,128]{1,0:T(1,128)S(1)}, bf16[128,16,128]{2,1,0:T(8,128)(2,1)S(1)}, bf16[128,16,128]{2,1,0:T(8,128)(2,1)S(1)}) custom-call(s32[16,512]{1,0:T(8,128)S(1)} %fusion.2.groups_ref, bf16[8,16,4096]{2,1,0:T(8,128)(2,1)S(1)} %copy-done, bf16[8,16,4096]{2,1,0:T(8,128)(2,1)S(1)} %copy-done.1), custom_call_target="tpu_custom_call" | custom-call | flops 536870912 | bytes 5242880 | tf_op jit(solution)/shard_map/pallas_call | solution.py:241
  31.1 0.0 collective-permute-done.3.x3
  31.1 0.0 collective-permute-done.2.x2
  31.1 2.5 %collective-permute-done.1.x1 = bf16[2,8,64,128]{3,2,1,0:T(8,128)(2,1)S(1)} collective-permute-done((bf16[2,8,64,128]{3,2,1,0:T(8,128)(2,1)}, bf16[2,8,64,128]{3,2,1,0:T(8,128)(2,1)S(1)}, u32[]{:S(2)}, u32[]{:S(2)}) %collective-permute-start.1) | collective-permute-done | bytes 262176 | tf_op jit(solution)/shard_map/ppermute | solution.py:210
  33.7 3.6 %collective-permute-done.x0 = bf16[2,8,64,128]{3,2,1,0:T(8,128)(2,1)S(1)} collective-permute-done((bf16[2,8,64,128]{3,2,1,0:T(8,128)(2,1)}, bf16[2,8,64,128]{3,2,1,0:T(8,128)(2,1)S(1)}, u32[]{:S(2)}, u32[]{:S(2)}) %collective-permute-start) | collective-permute-done | bytes 262176 | tf_op jit(solution)/shard_map/ppermute | solution.py:210
  37.3 0.0 copy-done.2
  37.3 2.2 %shard_map.39 = (bf16[2,8,64,128]{3,2,1,0:T(8,128)(2,1)S(1)}, f32[8,64,128]{2,1,0:T(8,128)S(1)}) custom-call(s32[1,128]{1,0:T(1,128)S(1)} %get-tuple-element.18.where_ref, bf16[128,16,128]{2,1,0:T(8,128)(2,1)S(1)} %get-tuple-element.19.same_ref, bf16[128,16,128]{2,1,0:T(8,128)(2,1)S(1)} %get-tuple-element.20.other_ref, ...), custom_call_target="tpu_custom_call" | custom-call | flops 402653184 | bytes 5242880 | tf_op jit(solution)/shard_map/pallas_call | solution.py:251
  39.5 1.9 %collective-permute-start.7 = (bf16[2,8,64,128]{3,2,1,0:T(8,128)(2,1)S(1)}, bf16[2,8,64,128]{3,2,1,0:T(8,128)(2,1)S(1)}, u32[]{:S(2)}, u32[]{:S(2)}) collective-permute-start(bf16[2,8,64,128]{3,2,1,0:T(8,128)(2,1)S(1)} %get-tuple-element.23.x4), channel_id=1, source_target_pairs={{0,496},{1,17},{2,498},{3,19},{4,500},{5,21},{6,502},{7,23},{8,504... | collective-permute-start | bytes 786440 | tf_op jit(solution)/shard_map/ppermute | solution.py:210
  41.4 1.9 %collective-permute-start.6 = (bf16[2,8,64,128]{3,2,1,0:T(8,128)(2,1)S(1)}, bf16[2,8,64,128]{3,2,1,0:T(8,128)(2,1)S(1)}, u32[]{:S(2)}, u32[]{:S(2)}) collective-permute-start(bf16[2,8,64,128]{3,2,1,0:T(8,128)(2,1)S(1)} %get-tuple-element.23.x4), channel_id=1, source_target_pairs={{0,504},{1,9},{2,506},{3,11},{4,508},{5,13},{6,510},{7,15},{8,0},{... | collective-permute-start | bytes 786440 | tf_op jit(solution)/shard_map/ppermute | solution.py:210
  43.3 8.2 %collective-permute-start.5 = (bf16[2,8,64,128]{3,2,1,0:T(8,128)(2,1)S(1)}, bf16[2,8,64,128]{3,2,1,0:T(8,128)(2,1)S(1)}, u32[]{:S(2)}, u32[]{:S(2)}) collective-permute-start(bf16[2,8,64,128]{3,2,1,0:T(8,128)(2,1)S(1)} %get-tuple-element.23.x4), channel_id=1, source_target_pairs={{0,16},{1,497},{2,18},{3,499},{4,20},{5,501},{6,22},{7,503},{8,24}... | collective-permute-start | bytes 786440 | tf_op jit(solution)/shard_map/ppermute | solution.py:210
  51.5 3.1 %collective-permute-start.4 = (bf16[2,8,64,128]{3,2,1,0:T(8,128)(2,1)S(1)}, bf16[2,8,64,128]{3,2,1,0:T(8,128)(2,1)S(1)}, u32[]{:S(2)}, u32[]{:S(2)}) collective-permute-start(bf16[2,8,64,128]{3,2,1,0:T(8,128)(2,1)S(1)} %get-tuple-element.23.x4), channel_id=1, source_target_pairs={{0,8},{1,505},{2,10},{3,507},{4,12},{5,509},{6,14},{7,511},{8,16},... | collective-permute-start | bytes 786440 | tf_op jit(solution)/shard_map/ppermute | solution.py:210
  54.6 0.0 collective-permute-done.7.x3
  54.6 1.2 %collective-permute-done.6.x2 = bf16[2,8,64,128]{3,2,1,0:T(8,128)(2,1)S(1)} collective-permute-done((bf16[2,8,64,128]{3,2,1,0:T(8,128)(2,1)S(1)}, bf16[2,8,64,128]{3,2,1,0:T(8,128)(2,1)S(1)}, u32[]{:S(2)}, u32[]{:S(2)}) %collective-permute-start.6) | collective-permute-done | bytes 262176 | tf_op jit(solution)/shard_map/ppermute | solution.py:210
  55.9 2.9 %collective-permute-done.5.x1 = bf16[2,8,64,128]{3,2,1,0:T(8,128)(2,1)S(1)} collective-permute-done((bf16[2,8,64,128]{3,2,1,0:T(8,128)(2,1)S(1)}, bf16[2,8,64,128]{3,2,1,0:T(8,128)(2,1)S(1)}, u32[]{:S(2)}, u32[]{:S(2)}) %collective-permute-start.5) | collective-permute-done | bytes 262176 | tf_op jit(solution)/shard_map/ppermute | solution.py:210
  58.7 6.1 %collective-permute-done.4.x0 = bf16[2,8,64,128]{3,2,1,0:T(8,128)(2,1)S(1)} collective-permute-done((bf16[2,8,64,128]{3,2,1,0:T(8,128)(2,1)S(1)}, bf16[2,8,64,128]{3,2,1,0:T(8,128)(2,1)S(1)}, u32[]{:S(2)}, u32[]{:S(2)}) %collective-permute-start.4) | collective-permute-done | bytes 262176 | tf_op jit(solution)/shard_map/ppermute | solution.py:210
  64.9 2.3 %shard_map.40 = bf16[8,64,128]{2,1,0:T(8,128)(2,1)S(1)} custom-call(s32[1,128]{1,0:T(1,128)S(1)} %get-tuple-element.18.where_ref, bf16[128,16,128]{2,1,0:T(8,128)(2,1)S(1)} %get-tuple-element.19.same_ref, bf16[128,16,128]{2,1,0:T(8,128)(2,1)S(1)} %get-tuple-element.20.other_ref, bf16[2,8,64,128]{3,2,1,0:T(8,128)(2,1)S(1)} %collective-permute-done.4.x0, ...), custom_call_target="tpu_custom_call" | custom-call | flops 268435456 | bytes 5242880 | tf_op jit(solution)/shard_map/pallas_call | solution.py:261
  67.2 10.7 %all_to_all.5.in_ref = bf16[8,64,128]{2,1,0:T(8,128)(2,1)S(1)} all-to-all(bf16[8,64,128]{2,1,0:T(8,128)(2,1)S(1)} %shard_map.40), channel_id=1, replica_groups=mesh['col'=64,'row'=8] {'row'}, dimensions={0} | all-to-all | bytes 262144 | tf_op jit(solution)/shard_map/all_to_all | solution.py:270
  77.9 1.2 %shard_map.41 = bf16[1,16,4096]{2,1,0:T(8,128)(2,1)} custom-call(bf16[8,64,128]{2,1,0:T(8,128)(2,1)S(1)} %all_to_all.5.in_ref), custom_call_target="tpu_custom_call" | custom-call | bytes 262144 | tf_op jit(solution)/shard_map/pallas_call | solution.py:271
  (1 shorter events, 0.0 us)
Async XLA Ops:
  0.0 26.2 %copy-start.3 = (s32[512,16]{0,1:T(8,128)S(1)}, s32[512,16]{0,1:T(8,128)}, u32[]{:S(2)}) copy-start(s32[512,16]{0,1:T(8,128)} %param.5) | copy-start | bytes 98308
  3.6 27.5 %collective-permute-start.3 = (bf16[2,8,64,128]{3,2,1,0:T(8,128)(2,1)}, bf16[2,8,64,128]{3,2,1,0:T(8,128)(2,1)S(1)}, u32[]{:S(2)}, u32[]{:S(2)}) collective-permute-start(bf16[2,8,64,128]{3,2,1,0:T(8,128)(2,1)} %shard_map.37.x4), channel_id=1, source_target_pairs={{0,496},{1,17},{2,498},{3,19},{4,500},{5,21},{6,502},{7,23},{8,504... | collective-permute-start | bytes 786440 | tf_op jit(solution)/shard_map/ppermute | solution.py:210
  9.4 21.8 %collective-permute-start.2 = (bf16[2,8,64,128]{3,2,1,0:T(8,128)(2,1)}, bf16[2,8,64,128]{3,2,1,0:T(8,128)(2,1)S(1)}, u32[]{:S(2)}, u32[]{:S(2)}) collective-permute-start(bf16[2,8,64,128]{3,2,1,0:T(8,128)(2,1)} %shard_map.37.x4), channel_id=1, source_target_pairs={{0,504},{1,9},{2,506},{3,11},{4,508},{5,13},{6,510},{7,15},{8,0},{... | collective-permute-start | bytes 786440 | tf_op jit(solution)/shard_map/ppermute | solution.py:210
  12.9 20.8 %collective-permute-start.1 = (bf16[2,8,64,128]{3,2,1,0:T(8,128)(2,1)}, bf16[2,8,64,128]{3,2,1,0:T(8,128)(2,1)S(1)}, u32[]{:S(2)}, u32[]{:S(2)}) collective-permute-start(bf16[2,8,64,128]{3,2,1,0:T(8,128)(2,1)} %shard_map.37.x4), channel_id=1, source_target_pairs={{0,16},{1,497},{2,18},{3,499},{4,20},{5,501},{6,22},{7,503},{8,24}... | collective-permute-start | bytes 786440 | tf_op jit(solution)/shard_map/ppermute | solution.py:210
  23.1 14.2 %collective-permute-start = (bf16[2,8,64,128]{3,2,1,0:T(8,128)(2,1)}, bf16[2,8,64,128]{3,2,1,0:T(8,128)(2,1)S(1)}, u32[]{:S(2)}, u32[]{:S(2)}) collective-permute-start(bf16[2,8,64,128]{3,2,1,0:T(8,128)(2,1)} %shard_map.37.x4), channel_id=1, source_target_pairs={{0,8},{1,505},{2,10},{3,507},{4,12},{5,509},{6,14},{7,511},{8,16},... | collective-permute-start | bytes 786440 | tf_op jit(solution)/shard_map/ppermute | solution.py:210
  26.2 1.2 %copy-start = (bf16[8,16,4096]{2,1,0:T(8,128)(2,1)S(1)}, bf16[8,16,4096]{2,1,0:T(8,128)(2,1)}, u32[]{:S(2)}) copy-start(bf16[8,16,4096]{2,1,0:T(8,128)(2,1)} %ground_ref) | copy-start | bytes 3145732
  27.4 1.2 %copy-start.1 = (bf16[8,16,4096]{2,1,0:T(8,128)(2,1)S(1)}, bf16[8,16,4096]{2,1,0:T(8,128)(2,1)}, u32[]{:S(2)}) copy-start(bf16[8,16,4096]{2,1,0:T(8,128)(2,1)} %response_ref) | copy-start | bytes 3145732
  28.6 8.6 %copy-start.2 = (bf16[2,8,64,128]{3,2,1,0:T(8,128)(2,1)S(1)}, bf16[2,8,64,128]{3,2,1,0:T(8,128)(2,1)}, u32[]{:S(2)}) copy-start(bf16[2,8,64,128]{3,2,1,0:T(8,128)(2,1)} %shard_map.37.x4) | copy-start | bytes 786436
  39.5 15.2 %collective-permute-start.7 = (bf16[2,8,64,128]{3,2,1,0:T(8,128)(2,1)S(1)}, bf16[2,8,64,128]{3,2,1,0:T(8,128)(2,1)S(1)}, u32[]{:S(2)}, u32[]{:S(2)}) collective-permute-start(bf16[2,8,64,128]{3,2,1,0:T(8,128)(2,1)S(1)} %get-tuple-element.23.x4), channel_id=1, source_target_pairs={{0,496},{1,17},{2,498},{3,19},{4,500},{5,21},{6,502},{7,23},{8,504... | collective-permute-start | bytes 786440 | tf_op jit(solution)/shard_map/ppermute | solution.py:210
  41.4 14.5 %collective-permute-start.6 = (bf16[2,8,64,128]{3,2,1,0:T(8,128)(2,1)S(1)}, bf16[2,8,64,128]{3,2,1,0:T(8,128)(2,1)S(1)}, u32[]{:S(2)}, u32[]{:S(2)}) collective-permute-start(bf16[2,8,64,128]{3,2,1,0:T(8,128)(2,1)S(1)} %get-tuple-element.23.x4), channel_id=1, source_target_pairs={{0,504},{1,9},{2,506},{3,11},{4,508},{5,13},{6,510},{7,15},{8,0},{... | collective-permute-start | bytes 786440 | tf_op jit(solution)/shard_map/ppermute | solution.py:210
  43.3 15.4 %collective-permute-start.5 = (bf16[2,8,64,128]{3,2,1,0:T(8,128)(2,1)S(1)}, bf16[2,8,64,128]{3,2,1,0:T(8,128)(2,1)S(1)}, u32[]{:S(2)}, u32[]{:S(2)}) collective-permute-start(bf16[2,8,64,128]{3,2,1,0:T(8,128)(2,1)S(1)} %get-tuple-element.23.x4), channel_id=1, source_target_pairs={{0,16},{1,497},{2,18},{3,499},{4,20},{5,501},{6,22},{7,503},{8,24}... | collective-permute-start | bytes 786440 | tf_op jit(solution)/shard_map/ppermute | solution.py:210
  51.5 13.4 %collective-permute-start.4 = (bf16[2,8,64,128]{3,2,1,0:T(8,128)(2,1)S(1)}, bf16[2,8,64,128]{3,2,1,0:T(8,128)(2,1)S(1)}, u32[]{:S(2)}, u32[]{:S(2)}) collective-permute-start(bf16[2,8,64,128]{3,2,1,0:T(8,128)(2,1)S(1)} %get-tuple-element.23.x4), channel_id=1, source_target_pairs={{0,8},{1,505},{2,10},{3,507},{4,12},{5,509},{6,14},{7,511},{8,16},... | collective-permute-start | bytes 786440 | tf_op jit(solution)/shard_map/ppermute | solution.py:210

commit v5 on v4

--- a/solution.py
+++ b/solution.py
@@ -11,7 +11,7 @@
 NB = 512
 SLOTS = 16
 ROWS = 8
-WIDE = SLOTS * 8
+WIDE = K8 * BLK
 TILES = BLK * BLK // 128
 HALF = TILES
 F32, BF16 = jnp.float32, jnp.bfloat16
@@ -45,39 +45,29 @@
     return [turned[pl.ds(b, TILES, stride=SLOTS), :].astype(BF16) for b in range(SLOTS)]
 
 
-def exchange(parts):
-    parts = list(parts)
-    chunk = lax.broadcasted_iota(jnp.int32, parts[0].shape, 1) // 8
-    for bit in (1, 2, 4, 8):
-        low = chunk // bit % 2 == 0
-        for i in range(16):
-            if i & bit:
-                continue
-            a, b = parts[i], parts[i | bit]
-            parts[i] = jnp.where(low, a, pltpu.roll(b, 8 * bit, 1))
-            parts[i | bit] = jnp.where(low, pltpu.roll(a, 128 - 8 * bit, 1), b)
-    return parts
-
-
-def slice_body(ground_hbm, response_hbm, out_ref, held, picked, placed, arrived):
+def cross(a, b):
+    low = lax.broadcasted_iota(jnp.int32, a.shape, 1) < BLK
+    return jnp.where(low, a, pltpu.roll(b, BLK, 1)), jnp.where(low, pltpu.roll(a, BLK, 1), b)
+
+
+def slice_body(ground_hbm, response_hbm, out_ref, held, placed, arrived):
     copies = []
     for m, rows_hbm in enumerate((ground_hbm, response_hbm)):
         copies.append(pltpu.make_async_copy(rows_hbm, held.at[m], arrived.at[m]))
     for copy in copies:
         copy.start()
-    line = lax.broadcasted_iota(jnp.int32, (1024, 128), 0)
-    lane = lax.broadcasted_iota(jnp.int32, (1024, 128), 1)
-    col = line % BLK - 8 * lax.axis_index("row")
-    pick = jnp.where((col >= 0) & (col < 8) & (lane == line // BLK * 8 + col), 1.0, 0.0).astype(BF16)
+    line = lax.broadcasted_iota(jnp.int32, (K8 * ROWS, ROWS * SLOTS), 0)
+    slot = lax.broadcasted_iota(jnp.int32, (K8 * ROWS, ROWS * SLOTS), 1)
+    want = line % ROWS * SLOTS + K8 * lax.axis_index("row") + line // ROWS
+    pick = jnp.where(slot == want, 1.0, 0.0).astype(BF16)
     for m in range(2):
         copies[m].wait()
         flat = held[m].reshape(ROWS * SLOTS, BLK * BLK)
-        for n in range(4):
-            picked[m, n] = jnp.dot(flat[:, n * 1024 : (n + 1) * 1024], pick, preferred_element_type=F32)
-            by = [2 * (i % 8) + i // 8 for i in range(16)]
-            parts = exchange(picked[m, n, pl.ds(b, ROWS, stride=SLOTS), :] for b in by)
-            for i, part in enumerate(parts):
-                placed[m, i % 2, pl.ds(n * 8 + i // 2, ROWS, stride=HALF), :] = part
+        mine = jnp.dot(pick, flat, preferred_element_type=F32)
+        for t in range(TILES):
+            part = mine[:, t * 128 : (t + 1) * 128]
+            for half, lines in enumerate(cross(part[0:ROWS], part[ROWS:])):
+                placed[m, half, pl.ds(t, ROWS, stride=HALF), :] = lines
         for half in range(2):
             lines = placed[m, half].astype(BF16).reshape(ROWS, HALF, 128)
             out_ref[m, :, half * HALF : (half + 1) * HALF, :] = lines
@@ -107,7 +97,7 @@
     i = lax.broadcasted_iota(jnp.int32, (SLOTS, SLOTS), 0)
     j = lax.broadcasted_iota(jnp.int32, (SLOTS, SLOTS), 1)
     swap = jnp.where(i // K8 * K8 + 1 - i % K8 == j, 1.0, 0.0).astype(BF16)
-    spread = jnp.where(pair // 8 == slot % K8 * ROWS + slot // K8, 1.0, 0.0).astype(BF16)
+    spread = jnp.where(slot == K8 * lax.axis_index("row") + pair // BLK, 1.0, 0.0).astype(BF16)
     facing = jnp.dot(swap, near.astype(BF16), preferred_element_type=F32)
     for ours, out_ref in ((near, same_ref), (facing, other_ref)):
         hit = jnp.where((far == ours) & (ours >= 0.0) & live, 1.0, 0.0).astype(BF16)
@@ -192,10 +182,10 @@
 
 
 def join_body(in_ref, out_ref, turned):
-    parts = exchange(in_ref[i % 8, (i // 8) * HALF : (i // 8 + 1) * HALF, :].astype(F32) for i in range(16))
-    for i in range(16):
-        j = 2 * (i % 8) + i // 8
-        turned[pl.ds(j * TILES, TILES), :] = parts[i]
+    for r in range(ROWS):
+        first, second = in_ref[r, 0:HALF].astype(F32), in_ref[r, HALF:BLK].astype(F32)
+        for i, lines in enumerate(cross(first, second)):
+            turned[pl.ds((K8 * r + i) * TILES, TILES), :] = lines
     for t in range(TILES):
         out_ref[0, :, t * 128 : (t + 1) * 128] = turned[pl.ds(t, SLOTS, stride=TILES), :].astype(BF16)
 
@@ -226,12 +216,11 @@
         rows,
         [
             pltpu.VMEM((2, ROWS, SLOTS, BLK * BLK), BF16),
-            pltpu.VMEM((2, 4, ROWS * SLOTS, 128), F32),
             pltpu.VMEM((2, 2, ROWS * HALF, 128), F32),
             pltpu.SemaphoreType.DMA((2,)),
         ],
         [pl.BlockSpec(memory_space=pltpu.HBM)] * 2,
-        2 * 1024 * 1024 * 128,
+        2 * 2 * 16 * 128 * 4096,
         5 << 20,
         SLICE_BYTES,
     )(ground, response)

time: 79.5 us -> 78.4 us (0.986)
  Pallas kernels: 11.7 us -> 10.7 us
    pallas_call x1, Pallas kernels: 3.61 us -> 2.79 us  [local(): call(slice_body, 'slice', rows, [pltpu.VMEM((2, ROWS, SLOTS, BLK * BLK),...]
where the time goes in v5:
time: 78.4 us; the launch traced here: 78 us
  starting transfers between devices  37.6 us (48%)
  waiting for transfers between devices  16.4 us (21%)
  Pallas kernels  10.7 us (14%)
  blocking collectives  10.7 us (14%)
  local copies, waits for them, and re-layouts  2.45 us (3%)
    ppermute x8, starting transfers between devices, from_afar(): return lax.ppermute(block, ('col', 'row'), route)  37.6 us
    ppermute x8, waiting for transfers between devices, from_afar(): return lax.ppermute(block, ('col', 'row'), route)  16.4 us
    all_to_all x1, blocking collectives, local(): part = lax.all_to_all(part, 'row', 0, 0, tiled=True)  10.7 us
    pallas_call x1, Pallas kernels, local(): call(slice_body, 'slice', rows, [pltpu.VMEM((2, ROWS, SLOTS, BLK * BLK),...  2.79 us
    pallas_call x1, Pallas kernels, local(): call(left_body, 'left', (jax.ShapeDtypeStruct((ROWS, 2 * BLK, SLOTS * BLK...  2.46 us
    unnamed x8, local copies, waits for them, and re-layouts  2.45 us
    pallas_call x1, Pallas kernels, local(): call(second_body, 'second', jax.ShapeDtypeStruct((ROWS, BLK, WIDE), BF16)...  2.29 us
    pallas_call x1, Pallas kernels, local(): call(first_body, 'first', (rows, jax.ShapeDtypeStruct((ROWS, BLK, WIDE),...  2.2 us
  transfers between devices with their start and end apart: 8, of which 5 were waited for; matrix products, arithmetic and copies ran while one was open for 0% of the time, Pallas kernels for 3%

profile of v5, /device:TPU:1, one launch (start us, length us, event | category | flops | bytes accessed | tf_op | source)
XLA Modules:
  0.0 78.0 jit_solution(12979615727634905346)
XLA Ops:
  0.0 0.0 copy-start.3
  0.0 2.8 %shard_map.37.x4 = bf16[2,8,64,128]{3,2,1,0:T(8,128)(2,1)} custom-call(bf16[8,16,4096]{2,1,0:T(8,128)(2,1)} %ground_ref, bf16[8,16,4096]{2,1,0:T(8,128)(2,1)} %response_ref), custom_call_target="tpu_custom_call" | custom-call | flops 33554432 | bytes 5242880 | tf_op jit(solution)/shard_map/pallas_call | solution.py:213
  2.8 5.7 %collective-permute-start.3 = (bf16[2,8,64,128]{3,2,1,0:T(8,128)(2,1)}, bf16[2,8,64,128]{3,2,1,0:T(8,128)(2,1)S(1)}, u32[]{:S(2)}, u32[]{:S(2)}) collective-permute-start(bf16[2,8,64,128]{3,2,1,0:T(8,128)(2,1)} %shard_map.37.x4), channel_id=1, source_target_pairs={{0,496},{1,17},{2,498},{3,19},{4,500},{5,21},{6,502},{7,23},{8,504... | collective-permute-start | bytes 786440 | tf_op jit(solution)/shard_map/ppermute | solution.py:200
  8.5 3.5 %collective-permute-start.2 = (bf16[2,8,64,128]{3,2,1,0:T(8,128)(2,1)}, bf16[2,8,64,128]{3,2,1,0:T(8,128)(2,1)S(1)}, u32[]{:S(2)}, u32[]{:S(2)}) collective-permute-start(bf16[2,8,64,128]{3,2,1,0:T(8,128)(2,1)} %shard_map.37.x4), channel_id=1, source_target_pairs={{0,504},{1,9},{2,506},{3,11},{4,508},{5,13},{6,510},{7,15},{8,0},{... | collective-permute-start | bytes 786440 | tf_op jit(solution)/shard_map/ppermute | solution.py:200
  12.1 10.1 %collective-permute-start.1 = (bf16[2,8,64,128]{3,2,1,0:T(8,128)(2,1)}, bf16[2,8,64,128]{3,2,1,0:T(8,128)(2,1)S(1)}, u32[]{:S(2)}, u32[]{:S(2)}) collective-permute-start(bf16[2,8,64,128]{3,2,1,0:T(8,128)(2,1)} %shard_map.37.x4), channel_id=1, source_target_pairs={{0,16},{1,497},{2,18},{3,499},{4,20},{5,501},{6,22},{7,503},{8,24}... | collective-permute-start | bytes 786440 | tf_op jit(solution)/shard_map/ppermute | solution.py:200
  22.2 3.1 %collective-permute-start = (bf16[2,8,64,128]{3,2,1,0:T(8,128)(2,1)}, bf16[2,8,64,128]{3,2,1,0:T(8,128)(2,1)S(1)}, u32[]{:S(2)}, u32[]{:S(2)}) collective-permute-start(bf16[2,8,64,128]{3,2,1,0:T(8,128)(2,1)} %shard_map.37.x4), channel_id=1, source_target_pairs={{0,8},{1,505},{2,10},{3,507},{4,12},{5,509},{6,14},{7,511},{8,16},... | collective-permute-start | bytes 786440 | tf_op jit(solution)/shard_map/ppermute | solution.py:200
  25.3 0.0 copy-done.3
  25.4 0.0 copy-start
  25.4 1.2 %copy-done = bf16[8,16,4096]{2,1,0:T(8,128)(2,1)S(1)} copy-done((bf16[8,16,4096]{2,1,0:T(8,128)(2,1)S(1)}, bf16[8,16,4096]{2,1,0:T(8,128)(2,1)}, u32[]{:S(2)}) %copy-start) | copy-done | bytes 1048600
  26.6 0.0 copy-start.1
  26.6 1.2 %copy-done.1 = bf16[8,16,4096]{2,1,0:T(8,128)(2,1)S(1)} copy-done((bf16[8,16,4096]{2,1,0:T(8,128)(2,1)S(1)}, bf16[8,16,4096]{2,1,0:T(8,128)(2,1)}, u32[]{:S(2)}) %copy-start.1) | copy-done | bytes 1048600
  27.8 0.0 copy-start.2
  27.8 2.5 %shard_map.38 = (bf16[8,128,1024]{2,1,0:T(8,128)(2,1)S(1)}, s32[1,128]{1,0:T(1,128)S(1)}, bf16[128,16,128]{2,1,0:T(8,128)(2,1)S(1)}, bf16[128,16,128]{2,1,0:T(8,128)(2,1)S(1)}) custom-call(s32[16,512]{1,0:T(8,128)S(1)} %fusion.2.groups_ref, bf16[8,16,4096]{2,1,0:T(8,128)(2,1)S(1)} %copy-done, bf16[8,16,4096]{2,1,0:T(8,128)(2,1)S(1)} %copy-done.1), custom_call_target="tpu_custom_call" | custom-call | flops 536870912 | bytes 5242880 | tf_op jit(solution)/shard_map/pallas_call | solution.py:230
  30.3 0.0 collective-permute-done.3.x3
  30.3 0.0 collective-permute-done.2.x2
  30.3 2.5 %collective-permute-done.1.x1 = bf16[2,8,64,128]{3,2,1,0:T(8,128)(2,1)S(1)} collective-permute-done((bf16[2,8,64,128]{3,2,1,0:T(8,128)(2,1)}, bf16[2,8,64,128]{3,2,1,0:T(8,128)(2,1)S(1)}, u32[]{:S(2)}, u32[]{:S(2)}) %collective-permute-start.1) | collective-permute-done | bytes 262176 | tf_op jit(solution)/shard_map/ppermute | solution.py:200
  32.8 3.6 %collective-permute-done.x0 = bf16[2,8,64,128]{3,2,1,0:T(8,128)(2,1)S(1)} collective-permute-done((bf16[2,8,64,128]{3,2,1,0:T(8,128)(2,1)}, bf16[2,8,64,128]{3,2,1,0:T(8,128)(2,1)S(1)}, u32[]{:S(2)}, u32[]{:S(2)}) %collective-permute-start) | collective-permute-done | bytes 262176 | tf_op jit(solution)/shard_map/ppermute | solution.py:200
  36.4 0.0 copy-done.2
  36.4 2.2 %shard_map.39 = (bf16[2,8,64,128]{3,2,1,0:T(8,128)(2,1)S(1)}, f32[8,64,128]{2,1,0:T(8,128)S(1)}) custom-call(s32[1,128]{1,0:T(1,128)S(1)} %get-tuple-element.18.where_ref, bf16[128,16,128]{2,1,0:T(8,128)(2,1)S(1)} %get-tuple-element.19.same_ref, bf16[128,16,128]{2,1,0:T(8,128)(2,1)S(1)} %get-tuple-element.20.other_ref, ...), custom_call_target="tpu_custom_call" | custom-call | flops 402653184 | bytes 5242880 | tf_op jit(solution)/shard_map/pallas_call | solution.py:240
  38.7 1.9 %collective-permute-start.7 = (bf16[2,8,64,128]{3,2,1,0:T(8,128)(2,1)S(1)}, bf16[2,8,64,128]{3,2,1,0:T(8,128)(2,1)S(1)}, u32[]{:S(2)}, u32[]{:S(2)}) collective-permute-start(bf16[2,8,64,128]{3,2,1,0:T(8,128)(2,1)S(1)} %get-tuple-element.23.x4), channel_id=1, source_target_pairs={{0,496},{1,17},{2,498},{3,19},{4,500},{5,21},{6,502},{7,23},{8,504... | collective-permute-start | bytes 786440 | tf_op jit(solution)/shard_map/ppermute | solution.py:200
  40.6 1.9 %collective-permute-start.6 = (bf16[2,8,64,128]{3,2,1,0:T(8,128)(2,1)S(1)}, bf16[2,8,64,128]{3,2,1,0:T(8,128)(2,1)S(1)}, u32[]{:S(2)}, u32[]{:S(2)}) collective-permute-start(bf16[2,8,64,128]{3,2,1,0:T(8,128)(2,1)S(1)} %get-tuple-element.23.x4), channel_id=1, source_target_pairs={{0,504},{1,9},{2,506},{3,11},{4,508},{5,13},{6,510},{7,15},{8,0},{... | collective-permute-start | bytes 786440 | tf_op jit(solution)/shard_map/ppermute | solution.py:200
  42.5 8.2 %collective-permute-start.5 = (bf16[2,8,64,128]{3,2,1,0:T(8,128)(2,1)S(1)}, bf16[2,8,64,128]{3,2,1,0:T(8,128)(2,1)S(1)}, u32[]{:S(2)}, u32[]{:S(2)}) collective-permute-start(bf16[2,8,64,128]{3,2,1,0:T(8,128)(2,1)S(1)} %get-tuple-element.23.x4), channel_id=1, source_target_pairs={{0,16},{1,497},{2,18},{3,499},{4,20},{5,501},{6,22},{7,503},{8,24}... | collective-permute-start | bytes 786440 | tf_op jit(solution)/shard_map/ppermute | solution.py:200
  50.7 3.1 %collective-permute-start.4 = (bf16[2,8,64,128]{3,2,1,0:T(8,128)(2,1)S(1)}, bf16[2,8,64,128]{3,2,1,0:T(8,128)(2,1)S(1)}, u32[]{:S(2)}, u32[]{:S(2)}) collective-permute-start(bf16[2,8,64,128]{3,2,1,0:T(8,128)(2,1)S(1)} %get-tuple-element.23.x4), channel_id=1, source_target_pairs={{0,8},{1,505},{2,10},{3,507},{4,12},{5,509},{6,14},{7,511},{8,16},... | collective-permute-start | bytes 786440 | tf_op jit(solution)/shard_map/ppermute | solution.py:200
  53.8 0.0 collective-permute-done.7.x3
  53.8 1.2 %collective-permute-done.6.x2 = bf16[2,8,64,128]{3,2,1,0:T(8,128)(2,1)S(1)} collective-permute-done((bf16[2,8,64,128]{3,2,1,0:T(8,128)(2,1)S(1)}, bf16[2,8,64,128]{3,2,1,0:T(8,128)(2,1)S(1)}, u32[]{:S(2)}, u32[]{:S(2)}) %collective-permute-start.6) | collective-permute-done | bytes 262176 | tf_op jit(solution)/shard_map/ppermute | solution.py:200
  55.0 2.9 %collective-permute-done.5.x1 = bf16[2,8,64,128]{3,2,1,0:T(8,128)(2,1)S(1)} collective-permute-done((bf16[2,8,64,128]{3,2,1,0:T(8,128)(2,1)S(1)}, bf16[2,8,64,128]{3,2,1,0:T(8,128)(2,1)S(1)}, u32[]{:S(2)}, u32[]{:S(2)}) %collective-permute-start.5) | collective-permute-done | bytes 262176 | tf_op jit(solution)/shard_map/ppermute | solution.py:200
  57.9 6.2 %collective-permute-done.4.x0 = bf16[2,8,64,128]{3,2,1,0:T(8,128)(2,1)S(1)} collective-permute-done((bf16[2,8,64,128]{3,2,1,0:T(8,128)(2,1)S(1)}, bf16[2,8,64,128]{3,2,1,0:T(8,128)(2,1)S(1)}, u32[]{:S(2)}, u32[]{:S(2)}) %collective-permute-start.4) | collective-permute-done | bytes 262176 | tf_op jit(solution)/shard_map/ppermute | solution.py:200
  64.1 2.3 %shard_map.40 = bf16[8,64,128]{2,1,0:T(8,128)(2,1)S(1)} custom-call(s32[1,128]{1,0:T(1,128)S(1)} %get-tuple-element.18.where_ref, bf16[128,16,128]{2,1,0:T(8,128)(2,1)S(1)} %get-tuple-element.19.same_ref, bf16[128,16,128]{2,1,0:T(8,128)(2,1)S(1)} %get-tuple-element.20.other_ref, bf16[2,8,64,128]{3,2,1,0:T(8,128)(2,1)S(1)} %collective-permute-done.4.x0, ...), custom_call_target="tpu_custom_call" | custom-call | flops 268435456 | bytes 5242880 | tf_op jit(solution)/shard_map/pallas_call | solution.py:250
  66.4 10.7 %all_to_all.5.in_ref = bf16[8,64,128]{2,1,0:T(8,128)(2,1)S(1)} all-to-all(bf16[8,64,128]{2,1,0:T(8,128)(2,1)S(1)} %shard_map.40), channel_id=1, replica_groups=mesh['col'=64,'row'=8] {'row'}, dimensions={0} | all-to-all | bytes 262144 | tf_op jit(solution)/shard_map/all_to_all | solution.py:259
  77.1 0.9 %shard_map.41 = bf16[1,16,4096]{2,1,0:T(8,128)(2,1)} custom-call(bf16[8,64,128]{2,1,0:T(8,128)(2,1)S(1)} %all_to_all.5.in_ref), custom_call_target="tpu_custom_call" | custom-call | bytes 262144 | tf_op jit(solution)/shard_map/pallas_call | solution.py:260
  (1 shorter events, 0.0 us)
Async XLA Ops:
  0.0 25.3 %copy-start.3 = (s32[512,16]{0,1:T(8,128)S(1)}, s32[512,16]{0,1:T(8,128)}, u32[]{:S(2)}) copy-start(s32[512,16]{0,1:T(8,128)} %param.5) | copy-start | bytes 98308
  2.8 27.5 %collective-permute-start.3 = (bf16[2,8,64,128]{3,2,1,0:T(8,128)(2,1)}, bf16[2,8,64,128]{3,2,1,0:T(8,128)(2,1)S(1)}, u32[]{:S(2)}, u32[]{:S(2)}) collective-permute-start(bf16[2,8,64,128]{3,2,1,0:T(8,128)(2,1)} %shard_map.37.x4), channel_id=1, source_target_pairs={{0,496},{1,17},{2,498},{3,19},{4,500},{5,21},{6,502},{7,23},{8,504... | collective-permute-start | bytes 786440 | tf_op jit(solution)/shard_map/ppermute | solution.py:200
  8.5 21.8 %collective-permute-start.2 = (bf16[2,8,64,128]{3,2,1,0:T(8,128)(2,1)}, bf16[2,8,64,128]{3,2,1,0:T(8,128)(2,1)S(1)}, u32[]{:S(2)}, u32[]{:S(2)}) collective-permute-start(bf16[2,8,64,128]{3,2,1,0:T(8,128)(2,1)} %shard_map.37.x4), channel_id=1, source_target_pairs={{0,504},{1,9},{2,506},{3,11},{4,508},{5,13},{6,510},{7,15},{8,0},{... | collective-permute-start | bytes 786440 | tf_op jit(solution)/shard_map/ppermute | solution.py:200
  12.1 20.8 %collective-permute-start.1 = (bf16[2,8,64,128]{3,2,1,0:T(8,128)(2,1)}, bf16[2,8,64,128]{3,2,1,0:T(8,128)(2,1)S(1)}, u32[]{:S(2)}, u32[]{:S(2)}) collective-permute-start(bf16[2,8,64,128]{3,2,1,0:T(8,128)(2,1)} %shard_map.37.x4), channel_id=1, source_target_pairs={{0,16},{1,497},{2,18},{3,499},{4,20},{5,501},{6,22},{7,503},{8,24}... | collective-permute-start | bytes 786440 | tf_op jit(solution)/shard_map/ppermute | solution.py:200
  22.2 14.2 %collective-permute-start = (bf16[2,8,64,128]{3,2,1,0:T(8,128)(2,1)}, bf16[2,8,64,128]{3,2,1,0:T(8,128)(2,1)S(1)}, u32[]{:S(2)}, u32[]{:S(2)}) collective-permute-start(bf16[2,8,64,128]{3,2,1,0:T(8,128)(2,1)} %shard_map.37.x4), channel_id=1, source_target_pairs={{0,8},{1,505},{2,10},{3,507},{4,12},{5,509},{6,14},{7,511},{8,16},... | collective-permute-start | bytes 786440 | tf_op jit(solution)/shard_map/ppermute | solution.py:200
  25.4 1.2 %copy-start = (bf16[8,16,4096]{2,1,0:T(8,128)(2,1)S(1)}, bf16[8,16,4096]{2,1,0:T(8,128)(2,1)}, u32[]{:S(2)}) copy-start(bf16[8,16,4096]{2,1,0:T(8,128)(2,1)} %ground_ref) | copy-start | bytes 3145732
  26.6 1.2 %copy-start.1 = (bf16[8,16,4096]{2,1,0:T(8,128)(2,1)S(1)}, bf16[8,16,4096]{2,1,0:T(8,128)(2,1)}, u32[]{:S(2)}) copy-start(bf16[8,16,4096]{2,1,0:T(8,128)(2,1)} %response_ref) | copy-start | bytes 3145732
  27.8 8.6 %copy-start.2 = (bf16[2,8,64,128]{3,2,1,0:T(8,128)(2,1)S(1)}, bf16[2,8,64,128]{3,2,1,0:T(8,128)(2,1)}, u32[]{:S(2)}) copy-start(bf16[2,8,64,128]{3,2,1,0:T(8,128)(2,1)} %shard_map.37.x4) | copy-start | bytes 786436
  38.7 15.1 %collective-permute-start.7 = (bf16[2,8,64,128]{3,2,1,0:T(8,128)(2,1)S(1)}, bf16[2,8,64,128]{3,2,1,0:T(8,128)(2,1)S(1)}, u32[]{:S(2)}, u32[]{:S(2)}) collective-permute-start(bf16[2,8,64,128]{3,2,1,0:T(8,128)(2,1)S(1)} %get-tuple-element.23.x4), channel_id=1, source_target_pairs={{0,496},{1,17},{2,498},{3,19},{4,500},{5,21},{6,502},{7,23},{8,504... | collective-permute-start | bytes 786440 | tf_op jit(solution)/shard_map/ppermute | solution.py:200
  40.6 14.5 %collective-permute-start.6 = (bf16[2,8,64,128]{3,2,1,0:T(8,128)(2,1)S(1)}, bf16[2,8,64,128]{3,2,1,0:T(8,128)(2,1)S(1)}, u32[]{:S(2)}, u32[]{:S(2)}) collective-permute-start(bf16[2,8,64,128]{3,2,1,0:T(8,128)(2,1)S(1)} %get-tuple-element.23.x4), channel_id=1, source_target_pairs={{0,504},{1,9},{2,506},{3,11},{4,508},{5,13},{6,510},{7,15},{8,0},{... | collective-permute-start | bytes 786440 | tf_op jit(solution)/shard_map/ppermute | solution.py:200
  42.5 15.4 %collective-permute-start.5 = (bf16[2,8,64,128]{3,2,1,0:T(8,128)(2,1)S(1)}, bf16[2,8,64,128]{3,2,1,0:T(8,128)(2,1)S(1)}, u32[]{:S(2)}, u32[]{:S(2)}) collective-permute-start(bf16[2,8,64,128]{3,2,1,0:T(8,128)(2,1)S(1)} %get-tuple-element.23.x4), channel_id=1, source_target_pairs={{0,16},{1,497},{2,18},{3,499},{4,20},{5,501},{6,22},{7,503},{8,24}... | collective-permute-start | bytes 786440 | tf_op jit(solution)/shard_map/ppermute | solution.py:200
  50.7 13.4 %collective-permute-start.4 = (bf16[2,8,64,128]{3,2,1,0:T(8,128)(2,1)S(1)}, bf16[2,8,64,128]{3,2,1,0:T(8,128)(2,1)S(1)}, u32[]{:S(2)}, u32[]{:S(2)}) collective-permute-start(bf16[2,8,64,128]{3,2,1,0:T(8,128)(2,1)S(1)} %get-tuple-element.23.x4), channel_id=1, source_target_pairs={{0,8},{1,505},{2,10},{3,507},{4,12},{5,509},{6,14},{7,511},{8,16},... | collective-permute-start | bytes 786440 | tf_op jit(solution)/shard_map/ppermute | solution.py:200

commit v6 on v5

--- a/solution.py
+++ b/solution.py
@@ -18,7 +18,7 @@
 VMEM_BYTES = 16 * 1024 * 1024
 
 
-SLICE_BYTES = int(63.1 * 1024 * 1024)
+SLICE_BYTES = int(8 * 1024 * 1024)
 
 
 def call(body, name, out_shape, scratch, in_specs, flops, moved, vmem=VMEM_BYTES):
@@ -50,12 +50,15 @@
     return jnp.where(low, a, pltpu.roll(b, BLK, 1)), jnp.where(low, pltpu.roll(a, BLK, 1), b)
 
 
-def slice_body(ground_hbm, response_hbm, out_ref, held, placed, arrived):
-    copies = []
-    for m, rows_hbm in enumerate((ground_hbm, response_hbm)):
-        copies.append(pltpu.make_async_copy(rows_hbm, held.at[m], arrived.at[m]))
+def fetch(sources, held, arrived):
+    copies = [pltpu.make_async_copy(source, held.at[m], arrived.at[m]) for m, source in enumerate(sources)]
     for copy in copies:
         copy.start()
+    return copies
+
+
+def slice_body(ground_hbm, response_hbm, out_ref, held, placed, arrived):
+    copies = fetch((ground_hbm, response_hbm), held, arrived)
     line = lax.broadcasted_iota(jnp.int32, (K8 * ROWS, ROWS * SLOTS), 0)
     slot = lax.broadcasted_iota(jnp.int32, (K8 * ROWS, ROWS * SLOTS), 1)
     want = line % ROWS * SLOTS + K8 * lax.axis_index("row") + line // ROWS
@@ -106,17 +109,19 @@
             out_ref[n] = jnp.broadcast_to(mask[n : n + 1], (16, WIDE)).astype(BF16)
 
 
-def left_body(groups_ref, ground_ref, response_ref, out_ref, place_ref, same_ref, other_ref, turned):
+def left_body(groups_ref, ground_hbm, response_hbm, out_ref, place_ref, same_ref, other_ref, turned, held, arrived):
+    copies = fetch((response_hbm, ground_hbm), held, arrived)
     lookup(groups_ref, place_ref, same_ref, other_ref)
     src = lax.broadcasted_iota(jnp.int32, (256, 256), 0)
     dst = lax.broadcasted_iota(jnp.int32, (256, 256), 1)
     two, half, col = src // 128, src // BLK % 2, src % BLK
     want = half * 128 + two * BLK + (col % 2) * HALF + col // 2
     turn = jnp.where(dst == want, 1.0, 0.0).astype(BF16)
-    for m, rows_ref in enumerate((response_ref, ground_ref)):
-
-        def step(g, _, m=m, rows_ref=rows_ref):
-            parts = by_slot(rows_ref, g, turned)
+    for m in range(2):
+        copies[m].wait()
+
+        def step(g, _, m=m):
+            parts = by_slot(held.at[m], g, turned)
             pairs = [jnp.concatenate(parts[b : b + 2], axis=1) for b in range(0, SLOTS, 2)]
             both = jnp.dot(jnp.concatenate(pairs, axis=0), turn, preferred_element_type=F32).astype(BF16)
             for i in range(SLOTS // 2):
@@ -209,13 +214,15 @@
     mask = jax.ShapeDtypeStruct((ROWS * SLOTS, 16, WIDE), BF16)
     smem = pl.BlockSpec(memory_space=pltpu.SMEM)
     turned = pltpu.VMEM((SLOTS * TILES, 128), F32)
+    held = pltpu.VMEM((2, ROWS, SLOTS, BLK * BLK), BF16)
     window = pltpu.VMEM((2, 5 * ROWS * BLK, WIDE), BF16)
+    ground, response = (pltpu.with_memory_space_constraint(x, pltpu.HBM) for x in (ground, response))
     cut = call(
         slice_body,
         "slice",
         rows,
         [
-            pltpu.VMEM((2, ROWS, SLOTS, BLK * BLK), BF16),
+            held,
             pltpu.VMEM((2, 2, ROWS * HALF, 128), F32),
             pltpu.SemaphoreType.DMA((2,)),
         ],
@@ -231,8 +238,8 @@
         left_body,
         "left",
         (jax.ShapeDtypeStruct((ROWS, 2 * BLK, SLOTS * BLK), BF16), jax.ShapeDtypeStruct((1, WIDE), jnp.int32), mask, mask),
-        [turned],
-        in_vmem(3),
+        [turned, held, pltpu.SemaphoreType.DMA((2,))],
+        in_vmem(1) + [pl.BlockSpec(memory_space=pltpu.HBM)] * 2,
         2 * 4096 * 256 * 256,
         5 << 20,
     )(groups, ground, response)

time: 78.4 us -> 77.6 us (0.990)
  local copies, waits for them, and re-layouts: 2.45 us -> 0.01 us
  waiting for transfers between devices: 16.4 us -> 17.7 us
    unnamed x8 -> x2, local copies, waits for them, and re-layouts: 2.45 us -> 0.01 us
    ppermute x8, waiting for transfers between devices: 16.4 us -> 17.7 us  [from_afar(): return lax.ppermute(block, ('col', 'row'), route)]
    pallas_call x1, Pallas kernels: 2.46 us -> 3.3 us  [local(): call(left_body, 'left', (jax.ShapeDtypeStruct((ROWS, 2 * BLK, SLOTS * BLK...]
  transfers between devices with their start and end apart: 8 -> 8, of which waited for: 5 -> 5; matrix products, arithmetic and copies ran while one was open for 0% -> 0% of each run, Pallas kernels for 3% -> 4%
where the time goes in v6:
time: 77.6 us; the launch traced here: 77.2 us
  starting transfers between devices  37.7 us (49%)
  waiting for transfers between devices  17.7 us (23%)
  Pallas kernels  10.9 us (14%)
  blocking collectives  10.7 us (14%)
    ppermute x8, starting transfers between devices, from_afar(): return lax.ppermute(block, ('col', 'row'), route)  37.7 us
    ppermute x8, waiting for transfers between devices, from_afar(): return lax.ppermute(block, ('col', 'row'), route)  17.7 us
    all_to_all x1, blocking collectives, local(): part = lax.all_to_all(part, 'row', 0, 0, tiled=True)  10.7 us
    pallas_call x1, Pallas kernels, local(): call(left_body, 'left', (jax.ShapeDtypeStruct((ROWS, 2 * BLK, SLOTS * BLK...  3.3 us
    pallas_call x1, Pallas kernels, local(): call(second_body, 'second', jax.ShapeDtypeStruct((ROWS, BLK, WIDE), BF16)...  2.34 us
    pallas_call x1, Pallas kernels, local(): call(first_body, 'first', (rows, jax.ShapeDtypeStruct((ROWS, BLK, WIDE),...  2.24 us
    pallas_call x1, Pallas kernels, local(): call(slice_body, 'slice', rows, [held, pltpu.VMEM((2, 2, ROWS * HALF, 128...  2.09 us
  transfers between devices with their start and end apart: 8, of which 5 were waited for; matrix products, arithmetic and copies ran while one was open for 0% of the time, Pallas kernels for 4%

profile of v6, /device:TPU:1, one launch (start us, length us, event | category | flops | bytes accessed | tf_op | source)
XLA Modules:
  0.0 77.2 jit_solution(16815872150618939965)
XLA Ops:
  0.0 0.0 copy-start
  0.0 2.1 %shard_map.37.x4 = bf16[2,8,64,128]{3,2,1,0:T(8,128)(2,1)S(1)} custom-call(bf16[8,16,4096]{2,1,0:T(8,128)(2,1)} %ground_hbm.2, bf16[8,16,4096]{2,1,0:T(8,128)(2,1)} %response_hbm.2), custom_call_target="tpu_custom_call" | custom-call | flops 33554432 | bytes 5242880 | tf_op jit(solution)/shard_map/pallas_call | solution.py:220
  2.1 5.7 %collective-permute-start.3 = (bf16[2,8,64,128]{3,2,1,0:T(8,128)(2,1)S(1)}, bf16[2,8,64,128]{3,2,1,0:T(8,128)(2,1)S(1)}, u32[]{:S(2)}, u32[]{:S(2)}) collective-permute-start(bf16[2,8,64,128]{3,2,1,0:T(8,128)(2,1)S(1)} %shard_map.37.x4), channel_id=1, source_target_pairs={{0,496},{1,17},{2,498},{3,19},{4,500},{5,21},{6,502},{7,23},{8,504... | collective-permute-start | bytes 786440 | tf_op jit(solution)/shard_map/ppermute | solution.py:205
  7.8 3.5 %collective-permute-start.2 = (bf16[2,8,64,128]{3,2,1,0:T(8,128)(2,1)S(1)}, bf16[2,8,64,128]{3,2,1,0:T(8,128)(2,1)S(1)}, u32[]{:S(2)}, u32[]{:S(2)}) collective-permute-start(bf16[2,8,64,128]{3,2,1,0:T(8,128)(2,1)S(1)} %shard_map.37.x4), channel_id=1, source_target_pairs={{0,504},{1,9},{2,506},{3,11},{4,508},{5,13},{6,510},{7,15},{8,0},{... | collective-permute-start | bytes 786440 | tf_op jit(solution)/shard_map/ppermute | solution.py:205
  11.4 10.1 %collective-permute-start.1 = (bf16[2,8,64,128]{3,2,1,0:T(8,128)(2,1)S(1)}, bf16[2,8,64,128]{3,2,1,0:T(8,128)(2,1)S(1)}, u32[]{:S(2)}, u32[]{:S(2)}) collective-permute-start(bf16[2,8,64,128]{3,2,1,0:T(8,128)(2,1)S(1)} %shard_map.37.x4), channel_id=1, source_target_pairs={{0,16},{1,497},{2,18},{3,499},{4,20},{5,501},{6,22},{7,503},{8,24}... | collective-permute-start | bytes 786440 | tf_op jit(solution)/shard_map/ppermute | solution.py:205
  21.5 3.1 %collective-permute-start = (bf16[2,8,64,128]{3,2,1,0:T(8,128)(2,1)S(1)}, bf16[2,8,64,128]{3,2,1,0:T(8,128)(2,1)S(1)}, u32[]{:S(2)}, u32[]{:S(2)}) collective-permute-start(bf16[2,8,64,128]{3,2,1,0:T(8,128)(2,1)S(1)} %shard_map.37.x4), channel_id=1, source_target_pairs={{0,8},{1,505},{2,10},{3,507},{4,12},{5,509},{6,14},{7,511},{8,16},... | collective-permute-start | bytes 786440 | tf_op jit(solution)/shard_map/ppermute | solution.py:205
  24.6 0.0 copy-done
  24.7 3.3 %shard_map.38 = (bf16[8,128,1024]{2,1,0:T(8,128)(2,1)S(1)}, s32[1,128]{1,0:T(1,128)S(1)}, bf16[128,16,128]{2,1,0:T(8,128)(2,1)S(1)}, bf16[128,16,128]{2,1,0:T(8,128)(2,1)S(1)}) custom-call(s32[16,512]{1,0:T(8,128)S(1)} %fusion.2.groups_ref, bf16[8,16,4096]{2,1,0:T(8,128)(2,1)} %ground_hbm.2, bf16[8,16,4096]{2,1,0:T(8,128)(2,1)} %response_hbm.2), custom_call_target="tpu_custom_call" | custom-call | flops 536870912 | bytes 5242880 | tf_op jit(solution)/shard_map/pallas_call | solution.py:237
  28.0 0.0 collective-permute-done.3.x3
  28.0 0.0 collective-permute-done.2.x2
  28.0 3.8 %collective-permute-done.1.x1 = bf16[2,8,64,128]{3,2,1,0:T(8,128)(2,1)S(1)} collective-permute-done((bf16[2,8,64,128]{3,2,1,0:T(8,128)(2,1)S(1)}, bf16[2,8,64,128]{3,2,1,0:T(8,128)(2,1)S(1)}, u32[]{:S(2)}, u32[]{:S(2)}) %collective-permute-start.1) | collective-permute-done | bytes 262176 | tf_op jit(solution)/shard_map/ppermute | solution.py:205
  31.8 3.6 %collective-permute-done.x0 = bf16[2,8,64,128]{3,2,1,0:T(8,128)(2,1)S(1)} collective-permute-done((bf16[2,8,64,128]{3,2,1,0:T(8,128)(2,1)S(1)}, bf16[2,8,64,128]{3,2,1,0:T(8,128)(2,1)S(1)}, u32[]{:S(2)}, u32[]{:S(2)}) %collective-permute-start) | collective-permute-done | bytes 262176 | tf_op jit(solution)/shard_map/ppermute | solution.py:205
  35.4 2.2 %shard_map.39 = (bf16[2,8,64,128]{3,2,1,0:T(8,128)(2,1)S(1)}, f32[8,64,128]{2,1,0:T(8,128)S(1)}) custom-call(s32[1,128]{1,0:T(1,128)S(1)} %get-tuple-element.18.where_ref, bf16[128,16,128]{2,1,0:T(8,128)(2,1)S(1)} %get-tuple-element.19.same_ref, bf16[128,16,128]{2,1,0:T(8,128)(2,1)S(1)} %get-tuple-element.20.other_ref, ...), custom_call_target="tpu_custom_call" | custom-call | flops 402653184 | bytes 5242880 | tf_op jit(solution)/shard_map/pallas_call | solution.py:247
  37.7 1.9 %collective-permute-start.7 = (bf16[2,8,64,128]{3,2,1,0:T(8,128)(2,1)S(1)}, bf16[2,8,64,128]{3,2,1,0:T(8,128)(2,1)S(1)}, u32[]{:S(2)}, u32[]{:S(2)}) collective-permute-start(bf16[2,8,64,128]{3,2,1,0:T(8,128)(2,1)S(1)} %get-tuple-element.23.x4), channel_id=1, source_target_pairs={{0,496},{1,17},{2,498},{3,19},{4,500},{5,21},{6,502},{7,23},{8,504... | collective-permute-start | bytes 786440 | tf_op jit(solution)/shard_map/ppermute | solution.py:205
  39.6 1.9 %collective-permute-start.6 = (bf16[2,8,64,128]{3,2,1,0:T(8,128)(2,1)S(1)}, bf16[2,8,64,128]{3,2,1,0:T(8,128)(2,1)S(1)}, u32[]{:S(2)}, u32[]{:S(2)}) collective-permute-start(bf16[2,8,64,128]{3,2,1,0:T(8,128)(2,1)S(1)} %get-tuple-element.23.x4), channel_id=1, source_target_pairs={{0,504},{1,9},{2,506},{3,11},{4,508},{5,13},{6,510},{7,15},{8,0},{... | collective-permute-start | bytes 786440 | tf_op jit(solution)/shard_map/ppermute | solution.py:205
  41.5 8.3 %collective-permute-start.5 = (bf16[2,8,64,128]{3,2,1,0:T(8,128)(2,1)S(1)}, bf16[2,8,64,128]{3,2,1,0:T(8,128)(2,1)S(1)}, u32[]{:S(2)}, u32[]{:S(2)}) collective-permute-start(bf16[2,8,64,128]{3,2,1,0:T(8,128)(2,1)S(1)} %get-tuple-element.23.x4), channel_id=1, source_target_pairs={{0,16},{1,497},{2,18},{3,499},{4,20},{5,501},{6,22},{7,503},{8,24}... | collective-permute-start | bytes 786440 | tf_op jit(solution)/shard_map/ppermute | solution.py:205
  49.9 3.1 %collective-permute-start.4 = (bf16[2,8,64,128]{3,2,1,0:T(8,128)(2,1)S(1)}, bf16[2,8,64,128]{3,2,1,0:T(8,128)(2,1)S(1)}, u32[]{:S(2)}, u32[]{:S(2)}) collective-permute-start(bf16[2,8,64,128]{3,2,1,0:T(8,128)(2,1)S(1)} %get-tuple-element.23.x4), channel_id=1, source_target_pairs={{0,8},{1,505},{2,10},{3,507},{4,12},{5,509},{6,14},{7,511},{8,16},... | collective-permute-start | bytes 786440 | tf_op jit(solution)/shard_map/ppermute | solution.py:205
  53.0 0.0 collective-permute-done.7.x3
  53.0 1.2 %collective-permute-done.6.x2 = bf16[2,8,64,128]{3,2,1,0:T(8,128)(2,1)S(1)} collective-permute-done((bf16[2,8,64,128]{3,2,1,0:T(8,128)(2,1)S(1)}, bf16[2,8,64,128]{3,2,1,0:T(8,128)(2,1)S(1)}, u32[]{:S(2)}, u32[]{:S(2)}) %collective-permute-start.6) | collective-permute-done | bytes 262176 | tf_op jit(solution)/shard_map/ppermute | solution.py:205
  54.2 2.9 %collective-permute-done.5.x1 = bf16[2,8,64,128]{3,2,1,0:T(8,128)(2,1)S(1)} collective-permute-done((bf16[2,8,64,128]{3,2,1,0:T(8,128)(2,1)S(1)}, bf16[2,8,64,128]{3,2,1,0:T(8,128)(2,1)S(1)}, u32[]{:S(2)}, u32[]{:S(2)}) %collective-permute-start.5) | collective-permute-done | bytes 262176 | tf_op jit(solution)/shard_map/ppermute | solution.py:205
  57.0 6.2 %collective-permute-done.4.x0 = bf16[2,8,64,128]{3,2,1,0:T(8,128)(2,1)S(1)} collective-permute-done((bf16[2,8,64,128]{3,2,1,0:T(8,128)(2,1)S(1)}, bf16[2,8,64,128]{3,2,1,0:T(8,128)(2,1)S(1)}, u32[]{:S(2)}, u32[]{:S(2)}) %collective-permute-start.4) | collective-permute-done | bytes 262176 | tf_op jit(solution)/shard_map/ppermute | solution.py:205
  63.2 2.3 %shard_map.40 = bf16[8,64,128]{2,1,0:T(8,128)(2,1)S(1)} custom-call(s32[1,128]{1,0:T(1,128)S(1)} %get-tuple-element.18.where_ref, bf16[128,16,128]{2,1,0:T(8,128)(2,1)S(1)} %get-tuple-element.19.same_ref, bf16[128,16,128]{2,1,0:T(8,128)(2,1)S(1)} %get-tuple-element.20.other_ref, bf16[2,8,64,128]{3,2,1,0:T(8,128)(2,1)S(1)} %collective-permute-done.4.x0, ...), custom_call_target="tpu_custom_call" | custom-call | flops 268435456 | bytes 5242880 | tf_op jit(solution)/shard_map/pallas_call | solution.py:257
  65.6 10.7 %all_to_all.5.in_ref = bf16[8,64,128]{2,1,0:T(8,128)(2,1)S(1)} all-to-all(bf16[8,64,128]{2,1,0:T(8,128)(2,1)S(1)} %shard_map.40), channel_id=1, replica_groups=mesh['col'=64,'row'=8] {'row'}, dimensions={0} | all-to-all | bytes 262144 | tf_op jit(solution)/shard_map/all_to_all | solution.py:266
  76.3 0.9 %shard_map.41 = bf16[1,16,4096]{2,1,0:T(8,128)(2,1)} custom-call(bf16[8,64,128]{2,1,0:T(8,128)(2,1)S(1)} %all_to_all.5.in_ref), custom_call_target="tpu_custom_call" | custom-call | bytes 262144 | tf_op jit(solution)/shard_map/pallas_call | solution.py:267
  (1 shorter events, 0.0 us)
Async XLA Ops:
  0.0 24.6 %copy-start = (s32[512,16]{0,1:T(8,128)S(1)}, s32[512,16]{0,1:T(8,128)}, u32[]{:S(2)}) copy-start(s32[512,16]{0,1:T(8,128)} %param.5) | copy-start | bytes 98308
  2.1 25.9 %collective-permute-start.3 = (bf16[2,8,64,128]{3,2,1,0:T(8,128)(2,1)S(1)}, bf16[2,8,64,128]{3,2,1,0:T(8,128)(2,1)S(1)}, u32[]{:S(2)}, u32[]{:S(2)}) collective-permute-start(bf16[2,8,64,128]{3,2,1,0:T(8,128)(2,1)S(1)} %shard_map.37.x4), channel_id=1, source_target_pairs={{0,496},{1,17},{2,498},{3,19},{4,500},{5,21},{6,502},{7,23},{8,504... | collective-permute-start | bytes 786440 | tf_op jit(solution)/shard_map/ppermute | solution.py:205
  7.8 20.2 %collective-permute-start.2 = (bf16[2,8,64,128]{3,2,1,0:T(8,128)(2,1)S(1)}, bf16[2,8,64,128]{3,2,1,0:T(8,128)(2,1)S(1)}, u32[]{:S(2)}, u32[]{:S(2)}) collective-permute-start(bf16[2,8,64,128]{3,2,1,0:T(8,128)(2,1)S(1)} %shard_map.37.x4), channel_id=1, source_target_pairs={{0,504},{1,9},{2,506},{3,11},{4,508},{5,13},{6,510},{7,15},{8,0},{... | collective-permute-start | bytes 786440 | tf_op jit(solution)/shard_map/ppermute | solution.py:205
  11.4 20.4 %collective-permute-start.1 = (bf16[2,8,64,128]{3,2,1,0:T(8,128)(2,1)S(1)}, bf16[2,8,64,128]{3,2,1,0:T(8,128)(2,1)S(1)}, u32[]{:S(2)}, u32[]{:S(2)}) collective-permute-start(bf16[2,8,64,128]{3,2,1,0:T(8,128)(2,1)S(1)} %shard_map.37.x4), channel_id=1, source_target_pairs={{0,16},{1,497},{2,18},{3,499},{4,20},{5,501},{6,22},{7,503},{8,24}... | collective-permute-start | bytes 786440 | tf_op jit(solution)/shard_map/ppermute | solution.py:205
  21.5 13.9 %collective-permute-start = (bf16[2,8,64,128]{3,2,1,0:T(8,128)(2,1)S(1)}, bf16[2,8,64,128]{3,2,1,0:T(8,128)(2,1)S(1)}, u32[]{:S(2)}, u32[]{:S(2)}) collective-permute-start(bf16[2,8,64,128]{3,2,1,0:T(8,128)(2,1)S(1)} %shard_map.37.x4), channel_id=1, source_target_pairs={{0,8},{1,505},{2,10},{3,507},{4,12},{5,509},{6,14},{7,511},{8,16},... | collective-permute-start | bytes 786440 | tf_op jit(solution)/shard_map/ppermute | solution.py:205
  37.7 15.3 %collective-permute-start.7 = (bf16[2,8,64,128]{3,2,1,0:T(8,128)(2,1)S(1)}, bf16[2,8,64,128]{3,2,1,0:T(8,128)(2,1)S(1)}, u32[]{:S(2)}, u32[]{:S(2)}) collective-permute-start(bf16[2,8,64,128]{3,2,1,0:T(8,128)(2,1)S(1)} %get-tuple-element.23.x4), channel_id=1, source_target_pairs={{0,496},{1,17},{2,498},{3,19},{4,500},{5,21},{6,502},{7,23},{8,504... | collective-permute-start | bytes 786440 | tf_op jit(solution)/shard_map/ppermute | solution.py:205
  39.6 14.6 %collective-permute-start.6 = (bf16[2,8,64,128]{3,2,1,0:T(8,128)(2,1)S(1)}, bf16[2,8,64,128]{3,2,1,0:T(8,128)(2,1)S(1)}, u32[]{:S(2)}, u32[]{:S(2)}) collective-permute-start(bf16[2,8,64,128]{3,2,1,0:T(8,128)(2,1)S(1)} %get-tuple-element.23.x4), channel_id=1, source_target_pairs={{0,504},{1,9},{2,506},{3,11},{4,508},{5,13},{6,510},{7,15},{8,0},{... | collective-permute-start | bytes 786440 | tf_op jit(solution)/shard_map/ppermute | solution.py:205
  41.5 15.5 %collective-permute-start.5 = (bf16[2,8,64,128]{3,2,1,0:T(8,128)(2,1)S(1)}, bf16[2,8,64,128]{3,2,1,0:T(8,128)(2,1)S(1)}, u32[]{:S(2)}, u32[]{:S(2)}) collective-permute-start(bf16[2,8,64,128]{3,2,1,0:T(8,128)(2,1)S(1)} %get-tuple-element.23.x4), channel_id=1, source_target_pairs={{0,16},{1,497},{2,18},{3,499},{4,20},{5,501},{6,22},{7,503},{8,24}... | collective-permute-start | bytes 786440 | tf_op jit(solution)/shard_map/ppermute | solution.py:205
  49.9 13.4 %collective-permute-start.4 = (bf16[2,8,64,128]{3,2,1,0:T(8,128)(2,1)S(1)}, bf16[2,8,64,128]{3,2,1,0:T(8,128)(2,1)S(1)}, u32[]{:S(2)}, u32[]{:S(2)}) collective-permute-start(bf16[2,8,64,128]{3,2,1,0:T(8,128)(2,1)S(1)} %get-tuple-element.23.x4), channel_id=1, source_target_pairs={{0,8},{1,505},{2,10},{3,507},{4,12},{5,509},{6,14},{7,511},{8,16},... | collective-permute-start | bytes 786440 | tf_op jit(solution)/shard_map/ppermute | solution.py:205

commit v7 on v6

--- a/solution.py
+++ b/solution.py
@@ -18,7 +18,7 @@
 VMEM_BYTES = 16 * 1024 * 1024
 
 
-SLICE_BYTES = int(8 * 1024 * 1024)
+SLICE_BYTES = 8 * 1024 * 1024
 
 
 def call(body, name, out_shape, scratch, in_specs, flops, moved, vmem=VMEM_BYTES):
@@ -92,8 +92,11 @@
     behind = column - group
     size = NB // ROWS
     behind = jnp.where(behind > REACH, behind - size, jnp.where(behind < -REACH, behind + size, behind))
-    behind = jnp.where(odd == 1, -behind, behind)
-    piece = jnp.where(behind > 0, behind - 1, jnp.where(behind < 0, 1 - behind, 4))
+    ahead = jnp.where(behind < 0, 1, 0)
+    twice = jnp.where(behind > 1, 1, jnp.where(behind < -1, 1, 0))
+    low = twice * (1 - column % 4 // 2) + (1 - twice) * (1 - column % 2)
+    plain = 1 - jnp.abs(ahead - low)
+    piece = jnp.where(behind == 0, 4, 2 * twice + plain + odd * (1 - 2 * plain))
     place_ref[...] = jnp.where(live, piece, 4) * ROWS + kind
     theirs = jnp.where(line == group * ROWS + kind, 1.0, 0.0).astype(BF16)
     far = jnp.dot(groups, theirs, preferred_element_type=F32)
@@ -195,18 +198,23 @@
         out_ref[0, :, t * 128 : (t + 1) * 128] = turned[pl.ds(t, SLOTS, stride=TILES), :].astype(BF16)
 
 
-def from_afar(block, distance):
+def partner(column, distance, shifted):
+    size = NB // ROWS
+    back = distance if shifted else 0
+    return (((column - back) % size ^ distance) + back) % size
+
+
+def trade(block, distance, shifted):
     columns, rows = lax.axis_size("col"), lax.axis_size("row")
     route = []
     for c in range(columns):
         for r in range(rows):
-            to = (c + (distance if r % 2 == 0 else -distance)) % columns
-            route.append((c * rows + r, to * rows + r))
+            route.append((c * rows + r, partner(c, distance, shifted != (r % 2 == 1)) * rows + r))
     return lax.ppermute(block, ("col", "row"), route)
 
 
 def surround(block):
-    return [from_afar(block, distance) for distance in (1, 2, -1, -2)] + [block]
+    return [trade(block, distance, shifted) for distance in (1, 2) for shifted in (True, False)] + [block]
 
 
 def local(ground, response, pattern):

time: 77.6 us -> 74.7 us (0.963)
  waiting for transfers between devices: 17.7 us -> 13.6 us
  blocking collectives: 10.7 us -> 11.5 us
    ppermute x8, waiting for transfers between devices: 17.7 us -> 13.6 us  [trade(): return lax.ppermute(block, ('col', 'row'), route)]
    all_to_all x1, blocking collectives: 10.7 us -> 11.5 us  [local(): part = lax.all_to_all(part, 'row', 0, 0, tiled=True)]
  transfers between devices with their start and end apart: 8 -> 8, of which waited for: 5 -> 5; matrix products, arithmetic and copies ran while one was open for 0% -> 0% of each run, Pallas kernels for 4% -> 5%
where the time goes in v7:
time: 74.7 us; the launch traced here: 74.3 us
  starting transfers between devices  37.9 us (51%)
  waiting for transfers between devices  13.6 us (18%)
  blocking collectives  11.5 us (15%)
  Pallas kernels  11.1 us (15%)
    ppermute x8, starting transfers between devices, trade(): return lax.ppermute(block, ('col', 'row'), route)  37.9 us
    ppermute x8, waiting for transfers between devices, trade(): return lax.ppermute(block, ('col', 'row'), route)  13.6 us
    all_to_all x1, blocking collectives, local(): part = lax.all_to_all(part, 'row', 0, 0, tiled=True)  11.5 us
    pallas_call x1, Pallas kernels, local(): call(left_body, 'left', (jax.ShapeDtypeStruct((ROWS, 2 * BLK, SLOTS * BLK...  3.55 us
    pallas_call x1, Pallas kernels, local(): call(second_body, 'second', jax.ShapeDtypeStruct((ROWS, BLK, WIDE), BF16)...  2.34 us
    pallas_call x1, Pallas kernels, local(): call(first_body, 'first', (rows, jax.ShapeDtypeStruct((ROWS, BLK, WIDE),...  2.24 us
    pallas_call x1, Pallas kernels, local(): call(slice_body, 'slice', rows, [held, pltpu.VMEM((2, 2, ROWS * HALF, 128...  2.09 us
  transfers between devices with their start and end apart: 8, of which 5 were waited for; matrix products, arithmetic and copies ran while one was open for 0% of the time, Pallas kernels for 5%

profile of v7, /device:TPU:1, one launch (start us, length us, event | category | flops | bytes accessed | tf_op | source)
XLA Modules:
  0.0 74.3 jit_solution(12820355591563394107)
XLA Ops:
  0.0 0.0 copy-start
  0.0 2.1 %shard_map.37.x4 = bf16[2,8,64,128]{3,2,1,0:T(8,128)(2,1)S(1)} custom-call(bf16[8,16,4096]{2,1,0:T(8,128)(2,1)} %ground_hbm.2, bf16[8,16,4096]{2,1,0:T(8,128)(2,1)} %response_hbm.2), custom_call_target="tpu_custom_call" | custom-call | flops 33554432 | bytes 5242880 | tf_op jit(solution)/shard_map/pallas_call | solution.py:228
  2.1 14.8 %collective-permute-start.3 = (bf16[2,8,64,128]{3,2,1,0:T(8,128)(2,1)S(1)}, bf16[2,8,64,128]{3,2,1,0:T(8,128)(2,1)S(1)}, u32[]{:S(2)}, u32[]{:S(2)}) collective-permute-start(bf16[2,8,64,128]{3,2,1,0:T(8,128)(2,1)S(1)} %shard_map.37.x4), channel_id=1, source_target_pairs={{0,16},{1,497},{2,18},{3,499},{4,20},{5,501},{6,22},{7,503},{8,24}... | collective-permute-start | bytes 786440 | tf_op jit(solution)/shard_map/ppermute | solution.py:213
  17.0 1.9 %collective-permute-start.2 = (bf16[2,8,64,128]{3,2,1,0:T(8,128)(2,1)S(1)}, bf16[2,8,64,128]{3,2,1,0:T(8,128)(2,1)S(1)}, u32[]{:S(2)}, u32[]{:S(2)}) collective-permute-start(bf16[2,8,64,128]{3,2,1,0:T(8,128)(2,1)S(1)} %shard_map.37.x4), channel_id=1, source_target_pairs={{0,496},{1,17},{2,498},{3,19},{4,500},{5,21},{6,502},{7,23},{8,504... | collective-permute-start | bytes 786440 | tf_op jit(solution)/shard_map/ppermute | solution.py:213
  18.9 5.0 %collective-permute-start.1 = (bf16[2,8,64,128]{3,2,1,0:T(8,128)(2,1)S(1)}, bf16[2,8,64,128]{3,2,1,0:T(8,128)(2,1)S(1)}, u32[]{:S(2)}, u32[]{:S(2)}) collective-permute-start(bf16[2,8,64,128]{3,2,1,0:T(8,128)(2,1)S(1)} %shard_map.37.x4), channel_id=1, source_target_pairs={{0,8},{1,505},{2,10},{3,507},{4,12},{5,509},{6,14},{7,511},{8,0},{... | collective-permute-start | bytes 786440 | tf_op jit(solution)/shard_map/ppermute | solution.py:213
  23.9 1.9 %collective-permute-start = (bf16[2,8,64,128]{3,2,1,0:T(8,128)(2,1)S(1)}, bf16[2,8,64,128]{3,2,1,0:T(8,128)(2,1)S(1)}, u32[]{:S(2)}, u32[]{:S(2)}) collective-permute-start(bf16[2,8,64,128]{3,2,1,0:T(8,128)(2,1)S(1)} %shard_map.37.x4), channel_id=1, source_target_pairs={{0,504},{1,9},{2,506},{3,11},{4,508},{5,13},{6,510},{7,15},{8,16},... | collective-permute-start | bytes 786440 | tf_op jit(solution)/shard_map/ppermute | solution.py:213
  25.8 0.0 copy-done
  25.9 3.5 %shard_map.38 = (bf16[8,128,1024]{2,1,0:T(8,128)(2,1)S(1)}, s32[1,128]{1,0:T(1,128)S(1)}, bf16[128,16,128]{2,1,0:T(8,128)(2,1)S(1)}, bf16[128,16,128]{2,1,0:T(8,128)(2,1)S(1)}) custom-call(s32[16,512]{1,0:T(8,128)S(1)} %fusion.2.groups_ref, bf16[8,16,4096]{2,1,0:T(8,128)(2,1)} %ground_hbm.2, bf16[8,16,4096]{2,1,0:T(8,128)(2,1)} %response_hbm.2), custom_call_target="tpu_custom_call" | custom-call | flops 536870912 | bytes 5242880 | tf_op jit(solution)/shard_map/pallas_call | solution.py:245
  29.4 0.0 collective-permute-done.3.x3
  29.4 0.0 collective-permute-done.2.x2
  29.4 3.2 %collective-permute-done.1.x1 = bf16[2,8,64,128]{3,2,1,0:T(8,128)(2,1)S(1)} collective-permute-done((bf16[2,8,64,128]{3,2,1,0:T(8,128)(2,1)S(1)}, bf16[2,8,64,128]{3,2,1,0:T(8,128)(2,1)S(1)}, u32[]{:S(2)}, u32[]{:S(2)}) %collective-permute-start.1) | collective-permute-done | bytes 262176 | tf_op jit(solution)/shard_map/ppermute | solution.py:213
  32.6 1.3 %collective-permute-done.x0 = bf16[2,8,64,128]{3,2,1,0:T(8,128)(2,1)S(1)} collective-permute-done((bf16[2,8,64,128]{3,2,1,0:T(8,128)(2,1)S(1)}, bf16[2,8,64,128]{3,2,1,0:T(8,128)(2,1)S(1)}, u32[]{:S(2)}, u32[]{:S(2)}) %collective-permute-start) | collective-permute-done | bytes 262176 | tf_op jit(solution)/shard_map/ppermute | solution.py:213
  33.9 2.2 %shard_map.39 = (bf16[2,8,64,128]{3,2,1,0:T(8,128)(2,1)S(1)}, f32[8,64,128]{2,1,0:T(8,128)S(1)}) custom-call(s32[1,128]{1,0:T(1,128)S(1)} %get-tuple-element.18.where_ref, bf16[128,16,128]{2,1,0:T(8,128)(2,1)S(1)} %get-tuple-element.19.same_ref, bf16[128,16,128]{2,1,0:T(8,128)(2,1)S(1)} %get-tuple-element.20.other_ref, ...), custom_call_target="tpu_custom_call" | custom-call | flops 402653184 | bytes 5242880 | tf_op jit(solution)/shard_map/pallas_call | solution.py:255
  36.2 5.8 %collective-permute-start.7 = (bf16[2,8,64,128]{3,2,1,0:T(8,128)(2,1)S(1)}, bf16[2,8,64,128]{3,2,1,0:T(8,128)(2,1)S(1)}, u32[]{:S(2)}, u32[]{:S(2)}) collective-permute-start(bf16[2,8,64,128]{3,2,1,0:T(8,128)(2,1)S(1)} %get-tuple-element.23.x4), channel_id=1, source_target_pairs={{0,16},{1,497},{2,18},{3,499},{4,20},{5,501},{6,22},{7,503},{8,24}... | collective-permute-start | bytes 786440 | tf_op jit(solution)/shard_map/ppermute | solution.py:213
  42.0 1.9 %collective-permute-start.6 = (bf16[2,8,64,128]{3,2,1,0:T(8,128)(2,1)S(1)}, bf16[2,8,64,128]{3,2,1,0:T(8,128)(2,1)S(1)}, u32[]{:S(2)}, u32[]{:S(2)}) collective-permute-start(bf16[2,8,64,128]{3,2,1,0:T(8,128)(2,1)S(1)} %get-tuple-element.23.x4), channel_id=1, source_target_pairs={{0,496},{1,17},{2,498},{3,19},{4,500},{5,21},{6,502},{7,23},{8,504... | collective-permute-start | bytes 786440 | tf_op jit(solution)/shard_map/ppermute | solution.py:213
  43.9 3.8 %collective-permute-start.5 = (bf16[2,8,64,128]{3,2,1,0:T(8,128)(2,1)S(1)}, bf16[2,8,64,128]{3,2,1,0:T(8,128)(2,1)S(1)}, u32[]{:S(2)}, u32[]{:S(2)}) collective-permute-start(bf16[2,8,64,128]{3,2,1,0:T(8,128)(2,1)S(1)} %get-tuple-element.23.x4), channel_id=1, source_target_pairs={{0,8},{1,505},{2,10},{3,507},{4,12},{5,509},{6,14},{7,511},{8,0},{... | collective-permute-start | bytes 786440 | tf_op jit(solution)/shard_map/ppermute | solution.py:213
  47.8 2.6 %collective-permute-start.4 = (bf16[2,8,64,128]{3,2,1,0:T(8,128)(2,1)S(1)}, bf16[2,8,64,128]{3,2,1,0:T(8,128)(2,1)S(1)}, u32[]{:S(2)}, u32[]{:S(2)}) collective-permute-start(bf16[2,8,64,128]{3,2,1,0:T(8,128)(2,1)S(1)} %get-tuple-element.23.x4), channel_id=1, source_target_pairs={{0,504},{1,9},{2,506},{3,11},{4,508},{5,13},{6,510},{7,15},{8,16},... | collective-permute-start | bytes 786440 | tf_op jit(solution)/shard_map/ppermute | solution.py:213
  50.4 0.0 collective-permute-done.7.x3
  50.4 3.1 %collective-permute-done.6.x2 = bf16[2,8,64,128]{3,2,1,0:T(8,128)(2,1)S(1)} collective-permute-done((bf16[2,8,64,128]{3,2,1,0:T(8,128)(2,1)S(1)}, bf16[2,8,64,128]{3,2,1,0:T(8,128)(2,1)S(1)}, u32[]{:S(2)}, u32[]{:S(2)}) %collective-permute-start.6) | collective-permute-done | bytes 262176 | tf_op jit(solution)/shard_map/ppermute | solution.py:213
  53.5 4.0 %collective-permute-done.5.x1 = bf16[2,8,64,128]{3,2,1,0:T(8,128)(2,1)S(1)} collective-permute-done((bf16[2,8,64,128]{3,2,1,0:T(8,128)(2,1)S(1)}, bf16[2,8,64,128]{3,2,1,0:T(8,128)(2,1)S(1)}, u32[]{:S(2)}, u32[]{:S(2)}) %collective-permute-start.5) | collective-permute-done | bytes 262176 | tf_op jit(solution)/shard_map/ppermute | solution.py:213
  57.6 1.9 %collective-permute-done.4.x0 = bf16[2,8,64,128]{3,2,1,0:T(8,128)(2,1)S(1)} collective-permute-done((bf16[2,8,64,128]{3,2,1,0:T(8,128)(2,1)S(1)}, bf16[2,8,64,128]{3,2,1,0:T(8,128)(2,1)S(1)}, u32[]{:S(2)}, u32[]{:S(2)}) %collective-permute-start.4) | collective-permute-done | bytes 262176 | tf_op jit(solution)/shard_map/ppermute | solution.py:213
  59.5 2.3 %shard_map.40 = bf16[8,64,128]{2,1,0:T(8,128)(2,1)S(1)} custom-call(s32[1,128]{1,0:T(1,128)S(1)} %get-tuple-element.18.where_ref, bf16[128,16,128]{2,1,0:T(8,128)(2,1)S(1)} %get-tuple-element.19.same_ref, bf16[128,16,128]{2,1,0:T(8,128)(2,1)S(1)} %get-tuple-element.20.other_ref, bf16[2,8,64,128]{3,2,1,0:T(8,128)(2,1)S(1)} %collective-permute-done.4.x0, ...), custom_call_target="tpu_custom_call" | custom-call | flops 268435456 | bytes 5242880 | tf_op jit(solution)/shard_map/pallas_call | solution.py:265
  61.8 11.5 %all_to_all.5.in_ref = bf16[8,64,128]{2,1,0:T(8,128)(2,1)S(1)} all-to-all(bf16[8,64,128]{2,1,0:T(8,128)(2,1)S(1)} %shard_map.40), channel_id=1, replica_groups=mesh['col'=64,'row'=8] {'row'}, dimensions={0} | all-to-all | bytes 262144 | tf_op jit(solution)/shard_map/all_to_all | solution.py:274
  73.3 0.9 %shard_map.41 = bf16[1,16,4096]{2,1,0:T(8,128)(2,1)} custom-call(bf16[8,64,128]{2,1,0:T(8,128)(2,1)S(1)} %all_to_all.5.in_ref), custom_call_target="tpu_custom_call" | custom-call | bytes 262144 | tf_op jit(solution)/shard_map/pallas_call | solution.py:275
  (1 shorter events, 0.0 us)
Async XLA Ops:
  0.0 25.8 %copy-start = (s32[512,16]{0,1:T(8,128)S(1)}, s32[512,16]{0,1:T(8,128)}, u32[]{:S(2)}) copy-start(s32[512,16]{0,1:T(8,128)} %param.5) | copy-start | bytes 98308
  2.1 27.3 %collective-permute-start.3 = (bf16[2,8,64,128]{3,2,1,0:T(8,128)(2,1)S(1)}, bf16[2,8,64,128]{3,2,1,0:T(8,128)(2,1)S(1)}, u32[]{:S(2)}, u32[]{:S(2)}) collective-permute-start(bf16[2,8,64,128]{3,2,1,0:T(8,128)(2,1)S(1)} %shard_map.37.x4), channel_id=1, source_target_pairs={{0,16},{1,497},{2,18},{3,499},{4,20},{5,501},{6,22},{7,503},{8,24}... | collective-permute-start | bytes 786440 | tf_op jit(solution)/shard_map/ppermute | solution.py:213
  17.0 12.5 %collective-permute-start.2 = (bf16[2,8,64,128]{3,2,1,0:T(8,128)(2,1)S(1)}, bf16[2,8,64,128]{3,2,1,0:T(8,128)(2,1)S(1)}, u32[]{:S(2)}, u32[]{:S(2)}) collective-permute-start(bf16[2,8,64,128]{3,2,1,0:T(8,128)(2,1)S(1)} %shard_map.37.x4), channel_id=1, source_target_pairs={{0,496},{1,17},{2,498},{3,19},{4,500},{5,21},{6,502},{7,23},{8,504... | collective-permute-start | bytes 786440 | tf_op jit(solution)/shard_map/ppermute | solution.py:213
  18.9 13.7 %collective-permute-start.1 = (bf16[2,8,64,128]{3,2,1,0:T(8,128)(2,1)S(1)}, bf16[2,8,64,128]{3,2,1,0:T(8,128)(2,1)S(1)}, u32[]{:S(2)}, u32[]{:S(2)}) collective-permute-start(bf16[2,8,64,128]{3,2,1,0:T(8,128)(2,1)S(1)} %shard_map.37.x4), channel_id=1, source_target_pairs={{0,8},{1,505},{2,10},{3,507},{4,12},{5,509},{6,14},{7,511},{8,0},{... | collective-permute-start | bytes 786440 | tf_op jit(solution)/shard_map/ppermute | solution.py:213
  23.9 10.0 %collective-permute-start = (bf16[2,8,64,128]{3,2,1,0:T(8,128)(2,1)S(1)}, bf16[2,8,64,128]{3,2,1,0:T(8,128)(2,1)S(1)}, u32[]{:S(2)}, u32[]{:S(2)}) collective-permute-start(bf16[2,8,64,128]{3,2,1,0:T(8,128)(2,1)S(1)} %shard_map.37.x4), channel_id=1, source_target_pairs={{0,504},{1,9},{2,506},{3,11},{4,508},{5,13},{6,510},{7,15},{8,16},... | collective-permute-start | bytes 786440 | tf_op jit(solution)/shard_map/ppermute | solution.py:213
  36.2 14.2 %collective-permute-start.7 = (bf16[2,8,64,128]{3,2,1,0:T(8,128)(2,1)S(1)}, bf16[2,8,64,128]{3,2,1,0:T(8,128)(2,1)S(1)}, u32[]{:S(2)}, u32[]{:S(2)}) collective-permute-start(bf16[2,8,64,128]{3,2,1,0:T(8,128)(2,1)S(1)} %get-tuple-element.23.x4), channel_id=1, source_target_pairs={{0,16},{1,497},{2,18},{3,499},{4,20},{5,501},{6,22},{7,503},{8,24}... | collective-permute-start | bytes 786440 | tf_op jit(solution)/shard_map/ppermute | solution.py:213
  42.0 11.5 %collective-permute-start.6 = (bf16[2,8,64,128]{3,2,1,0:T(8,128)(2,1)S(1)}, bf16[2,8,64,128]{3,2,1,0:T(8,128)(2,1)S(1)}, u32[]{:S(2)}, u32[]{:S(2)}) collective-permute-start(bf16[2,8,64,128]{3,2,1,0:T(8,128)(2,1)S(1)} %get-tuple-element.23.x4), channel_id=1, source_target_pairs={{0,496},{1,17},{2,498},{3,19},{4,500},{5,21},{6,502},{7,23},{8,504... | collective-permute-start | bytes 786440 | tf_op jit(solution)/shard_map/ppermute | solution.py:213
  43.9 13.6 %collective-permute-start.5 = (bf16[2,8,64,128]{3,2,1,0:T(8,128)(2,1)S(1)}, bf16[2,8,64,128]{3,2,1,0:T(8,128)(2,1)S(1)}, u32[]{:S(2)}, u32[]{:S(2)}) collective-permute-start(bf16[2,8,64,128]{3,2,1,0:T(8,128)(2,1)S(1)} %get-tuple-element.23.x4), channel_id=1, source_target_pairs={{0,8},{1,505},{2,10},{3,507},{4,12},{5,509},{6,14},{7,511},{8,0},{... | collective-permute-start | bytes 786440 | tf_op jit(solution)/shard_map/ppermute | solution.py:213
  47.8 11.7 %collective-permute-start.4 = (bf16[2,8,64,128]{3,2,1,0:T(8,128)(2,1)S(1)}, bf16[2,8,64,128]{3,2,1,0:T(8,128)(2,1)S(1)}, u32[]{:S(2)}, u32[]{:S(2)}) collective-permute-start(bf16[2,8,64,128]{3,2,1,0:T(8,128)(2,1)S(1)} %get-tuple-element.23.x4), channel_id=1, source_target_pairs={{0,504},{1,9},{2,506},{3,11},{4,508},{5,13},{6,510},{7,15},{8,16},... | collective-permute-start | bytes 786440 | tf_op jit(solution)/shard_map/ppermute | solution.py:213

commit v8 on v7

--- a/solution.py
+++ b/solution.py
@@ -96,7 +96,8 @@
     twice = jnp.where(behind > 1, 1, jnp.where(behind < -1, 1, 0))
     low = twice * (1 - column % 4 // 2) + (1 - twice) * (1 - column % 2)
     plain = 1 - jnp.abs(ahead - low)
-    piece = jnp.where(behind == 0, 4, 2 * twice + plain + odd * (1 - 2 * plain))
+    plain = plain + odd * (1 - 2 * plain)
+    piece = jnp.where(behind == 0, 4, jnp.where(twice == 1, 2 + plain, 1 - plain))
     place_ref[...] = jnp.where(live, piece, 4) * ROWS + kind
     theirs = jnp.where(line == group * ROWS + kind, 1.0, 0.0).astype(BF16)
     far = jnp.dot(groups, theirs, preferred_element_type=F32)
@@ -214,7 +215,8 @@
 
 
 def surround(block):
-    return [trade(block, distance, shifted) for distance in (1, 2) for shifted in (True, False)] + [block]
+    turns = ((1, False), (1, True), (2, True), (2, False))
+    return [trade(block, distance, shifted) for distance, shifted in turns] + [block]
 
 
 def local(ground, response, pattern):

time: 74.7 us -> 75.4 us (level)
  blocking collectives: 11.5 us -> 9.48 us
  waiting for transfers between devices: 13.6 us -> 15.4 us
  starting transfers between devices: 37.9 us -> 38.8 us
    all_to_all x1, blocking collectives: 11.5 us -> 9.48 us  [local(): part = lax.all_to_all(part, 'row', 0, 0, tiled=True)]
    ppermute x8, waiting for transfers between devices: 13.6 us -> 15.4 us  [trade(): return lax.ppermute(block, ('col', 'row'), route)]
    ppermute x8, starting transfers between devices: 37.9 us -> 38.8 us  [trade(): return lax.ppermute(block, ('col', 'row'), route)]
where the time goes in v8:
time: 75.4 us; the launch traced here: 75 us
  starting transfers between devices  38.8 us (51%)
  waiting for transfers between devices  15.4 us (20%)
  Pallas kernels  11.2 us (15%)
  blocking collectives  9.48 us (13%)
    ppermute x8, starting transfers between devices, trade(): return lax.ppermute(block, ('col', 'row'), route)  38.8 us
    ppermute x8, waiting for transfers between devices, trade(): return lax.ppermute(block, ('col', 'row'), route)  15.4 us
    all_to_all x1, blocking collectives, local(): part = lax.all_to_all(part, 'row', 0, 0, tiled=True)  9.48 us
    pallas_call x1, Pallas kernels, local(): call(left_body, 'left', (jax.ShapeDtypeStruct((ROWS, 2 * BLK, SLOTS * BLK...  3.55 us
    pallas_call x1, Pallas kernels, local(): call(second_body, 'second', jax.ShapeDtypeStruct((ROWS, BLK, WIDE), BF16)...  2.34 us
    pallas_call x1, Pallas kernels, local(): call(first_body, 'first', (rows, jax.ShapeDtypeStruct((ROWS, BLK, WIDE),...  2.25 us
    pallas_call x1, Pallas kernels, local(): call(slice_body, 'slice', rows, [held, pltpu.VMEM((2, 2, ROWS * HALF, 128...  2.09 us
  transfers between devices with their start and end apart: 8, of which 5 were waited for; matrix products, arithmetic and copies ran while one was open for 0% of the time, Pallas kernels for 5%

profile of v8, /device:TPU:1, one launch (start us, length us, event | category | flops | bytes accessed | tf_op | source)
XLA Modules:
  0.0 75.0 jit_solution(4126628695018379004)
XLA Ops:
  0.0 0.0 copy-start
  0.0 2.1 %shard_map.37.x4 = bf16[2,8,64,128]{3,2,1,0:T(8,128)(2,1)S(1)} custom-call(bf16[8,16,4096]{2,1,0:T(8,128)(2,1)} %ground_hbm.2, bf16[8,16,4096]{2,1,0:T(8,128)(2,1)} %response_hbm.2), custom_call_target="tpu_custom_call" | custom-call | flops 33554432 | bytes 5242880 | tf_op jit(solution)/shard_map/pallas_call | solution.py:230
  2.1 14.8 %collective-permute-start.3 = (bf16[2,8,64,128]{3,2,1,0:T(8,128)(2,1)S(1)}, bf16[2,8,64,128]{3,2,1,0:T(8,128)(2,1)S(1)}, u32[]{:S(2)}, u32[]{:S(2)}) collective-permute-start(bf16[2,8,64,128]{3,2,1,0:T(8,128)(2,1)S(1)} %shard_map.37.x4), channel_id=1, source_target_pairs={{0,16},{1,497},{2,18},{3,499},{4,20},{5,501},{6,22},{7,503},{8,24}... | collective-permute-start | bytes 786440 | tf_op jit(solution)/shard_map/ppermute | solution.py:214
  17.0 1.9 %collective-permute-start.2 = (bf16[2,8,64,128]{3,2,1,0:T(8,128)(2,1)S(1)}, bf16[2,8,64,128]{3,2,1,0:T(8,128)(2,1)S(1)}, u32[]{:S(2)}, u32[]{:S(2)}) collective-permute-start(bf16[2,8,64,128]{3,2,1,0:T(8,128)(2,1)S(1)} %shard_map.37.x4), channel_id=1, source_target_pairs={{0,496},{1,17},{2,498},{3,19},{4,500},{5,21},{6,502},{7,23},{8,504... | collective-permute-start | bytes 786440 | tf_op jit(solution)/shard_map/ppermute | solution.py:214
  18.9 2.6 %collective-permute-start.1 = (bf16[2,8,64,128]{3,2,1,0:T(8,128)(2,1)S(1)}, bf16[2,8,64,128]{3,2,1,0:T(8,128)(2,1)S(1)}, u32[]{:S(2)}, u32[]{:S(2)}) collective-permute-start(bf16[2,8,64,128]{3,2,1,0:T(8,128)(2,1)S(1)} %shard_map.37.x4), channel_id=1, source_target_pairs={{0,504},{1,9},{2,506},{3,11},{4,508},{5,13},{6,510},{7,15},{8,16},... | collective-permute-start | bytes 786440 | tf_op jit(solution)/shard_map/ppermute | solution.py:214
  21.5 5.0 %collective-permute-start = (bf16[2,8,64,128]{3,2,1,0:T(8,128)(2,1)S(1)}, bf16[2,8,64,128]{3,2,1,0:T(8,128)(2,1)S(1)}, u32[]{:S(2)}, u32[]{:S(2)}) collective-permute-start(bf16[2,8,64,128]{3,2,1,0:T(8,128)(2,1)S(1)} %shard_map.37.x4), channel_id=1, source_target_pairs={{0,8},{1,505},{2,10},{3,507},{4,12},{5,509},{6,14},{7,511},{8,0},{... | collective-permute-start | bytes 786440 | tf_op jit(solution)/shard_map/ppermute | solution.py:214
  26.5 0.0 copy-done
  26.6 3.5 %shard_map.38 = (bf16[8,128,1024]{2,1,0:T(8,128)(2,1)S(1)}, s32[1,128]{1,0:T(1,128)S(1)}, bf16[128,16,128]{2,1,0:T(8,128)(2,1)S(1)}, bf16[128,16,128]{2,1,0:T(8,128)(2,1)S(1)}) custom-call(s32[16,512]{1,0:T(8,128)S(1)} %fusion.2.groups_ref, bf16[8,16,4096]{2,1,0:T(8,128)(2,1)} %ground_hbm.2, bf16[8,16,4096]{2,1,0:T(8,128)(2,1)} %response_hbm.2), custom_call_target="tpu_custom_call" | custom-call | flops 536870912 | bytes 5242880 | tf_op jit(solution)/shard_map/pallas_call | solution.py:247
  30.1 0.0 collective-permute-done.3.x3
  30.2 0.0 collective-permute-done.2.x2
  30.2 1.1 %collective-permute-done.1.x1 = bf16[2,8,64,128]{3,2,1,0:T(8,128)(2,1)S(1)} collective-permute-done((bf16[2,8,64,128]{3,2,1,0:T(8,128)(2,1)S(1)}, bf16[2,8,64,128]{3,2,1,0:T(8,128)(2,1)S(1)}, u32[]{:S(2)}, u32[]{:S(2)}) %collective-permute-start.1) | collective-permute-done | bytes 262176 | tf_op jit(solution)/shard_map/ppermute | solution.py:214
  31.3 3.6 %collective-permute-done.x0 = bf16[2,8,64,128]{3,2,1,0:T(8,128)(2,1)S(1)} collective-permute-done((bf16[2,8,64,128]{3,2,1,0:T(8,128)(2,1)S(1)}, bf16[2,8,64,128]{3,2,1,0:T(8,128)(2,1)S(1)}, u32[]{:S(2)}, u32[]{:S(2)}) %collective-permute-start) | collective-permute-done | bytes 262176 | tf_op jit(solution)/shard_map/ppermute | solution.py:214
  34.9 2.2 %shard_map.39 = (bf16[2,8,64,128]{3,2,1,0:T(8,128)(2,1)S(1)}, f32[8,64,128]{2,1,0:T(8,128)S(1)}) custom-call(s32[1,128]{1,0:T(1,128)S(1)} %get-tuple-element.18.where_ref, bf16[128,16,128]{2,1,0:T(8,128)(2,1)S(1)} %get-tuple-element.19.same_ref, bf16[128,16,128]{2,1,0:T(8,128)(2,1)S(1)} %get-tuple-element.20.other_ref, ...), custom_call_target="tpu_custom_call" | custom-call | flops 402653184 | bytes 5242880 | tf_op jit(solution)/shard_map/pallas_call | solution.py:257
  37.1 5.1 %collective-permute-start.7 = (bf16[2,8,64,128]{3,2,1,0:T(8,128)(2,1)S(1)}, bf16[2,8,64,128]{3,2,1,0:T(8,128)(2,1)S(1)}, u32[]{:S(2)}, u32[]{:S(2)}) collective-permute-start(bf16[2,8,64,128]{3,2,1,0:T(8,128)(2,1)S(1)} %get-tuple-element.23.x4), channel_id=1, source_target_pairs={{0,16},{1,497},{2,18},{3,499},{4,20},{5,501},{6,22},{7,503},{8,24}... | collective-permute-start | bytes 786440 | tf_op jit(solution)/shard_map/ppermute | solution.py:214
  42.3 1.9 %collective-permute-start.6 = (bf16[2,8,64,128]{3,2,1,0:T(8,128)(2,1)S(1)}, bf16[2,8,64,128]{3,2,1,0:T(8,128)(2,1)S(1)}, u32[]{:S(2)}, u32[]{:S(2)}) collective-permute-start(bf16[2,8,64,128]{3,2,1,0:T(8,128)(2,1)S(1)} %get-tuple-element.23.x4), channel_id=1, source_target_pairs={{0,496},{1,17},{2,498},{3,19},{4,500},{5,21},{6,502},{7,23},{8,504... | collective-permute-start | bytes 786440 | tf_op jit(solution)/shard_map/ppermute | solution.py:214
  44.2 4.7 %collective-permute-start.5 = (bf16[2,8,64,128]{3,2,1,0:T(8,128)(2,1)S(1)}, bf16[2,8,64,128]{3,2,1,0:T(8,128)(2,1)S(1)}, u32[]{:S(2)}, u32[]{:S(2)}) collective-permute-start(bf16[2,8,64,128]{3,2,1,0:T(8,128)(2,1)S(1)} %get-tuple-element.23.x4), channel_id=1, source_target_pairs={{0,504},{1,9},{2,506},{3,11},{4,508},{5,13},{6,510},{7,15},{8,16},... | collective-permute-start | bytes 786440 | tf_op jit(solution)/shard_map/ppermute | solution.py:214
  48.9 2.7 %collective-permute-start.4 = (bf16[2,8,64,128]{3,2,1,0:T(8,128)(2,1)S(1)}, bf16[2,8,64,128]{3,2,1,0:T(8,128)(2,1)S(1)}, u32[]{:S(2)}, u32[]{:S(2)}) collective-permute-start(bf16[2,8,64,128]{3,2,1,0:T(8,128)(2,1)S(1)} %get-tuple-element.23.x4), channel_id=1, source_target_pairs={{0,8},{1,505},{2,10},{3,507},{4,12},{5,509},{6,14},{7,511},{8,0},{... | collective-permute-start | bytes 786440 | tf_op jit(solution)/shard_map/ppermute | solution.py:214
  51.6 0.0 collective-permute-done.7.x3
  51.6 1.4 %collective-permute-done.6.x2 = bf16[2,8,64,128]{3,2,1,0:T(8,128)(2,1)S(1)} collective-permute-done((bf16[2,8,64,128]{3,2,1,0:T(8,128)(2,1)S(1)}, bf16[2,8,64,128]{3,2,1,0:T(8,128)(2,1)S(1)}, u32[]{:S(2)}, u32[]{:S(2)}) %collective-permute-start.6) | collective-permute-done | bytes 262176 | tf_op jit(solution)/shard_map/ppermute | solution.py:214
  53.0 8.8 %collective-permute-done.5.x1 = bf16[2,8,64,128]{3,2,1,0:T(8,128)(2,1)S(1)} collective-permute-done((bf16[2,8,64,128]{3,2,1,0:T(8,128)(2,1)S(1)}, bf16[2,8,64,128]{3,2,1,0:T(8,128)(2,1)S(1)}, u32[]{:S(2)}, u32[]{:S(2)}) %collective-permute-start.5) | collective-permute-done | bytes 262176 | tf_op jit(solution)/shard_map/ppermute | solution.py:214
  61.8 0.5 collective-permute-done.4.x0
  62.3 2.3 %shard_map.40 = bf16[8,64,128]{2,1,0:T(8,128)(2,1)S(1)} custom-call(s32[1,128]{1,0:T(1,128)S(1)} %get-tuple-element.18.where_ref, bf16[128,16,128]{2,1,0:T(8,128)(2,1)S(1)} %get-tuple-element.19.same_ref, bf16[128,16,128]{2,1,0:T(8,128)(2,1)S(1)} %get-tuple-element.20.other_ref, bf16[2,8,64,128]{3,2,1,0:T(8,128)(2,1)S(1)} %collective-permute-done.4.x0, ...), custom_call_target="tpu_custom_call" | custom-call | flops 268435456 | bytes 5242880 | tf_op jit(solution)/shard_map/pallas_call | solution.py:267
  64.6 9.5 %all_to_all.5.in_ref = bf16[8,64,128]{2,1,0:T(8,128)(2,1)S(1)} all-to-all(bf16[8,64,128]{2,1,0:T(8,128)(2,1)S(1)} %shard_map.40), channel_id=1, replica_groups=mesh['col'=64,'row'=8] {'row'}, dimensions={0} | all-to-all | bytes 262144 | tf_op jit(solution)/shard_map/all_to_all | solution.py:276
  74.1 0.9 %shard_map.41 = bf16[1,16,4096]{2,1,0:T(8,128)(2,1)} custom-call(bf16[8,64,128]{2,1,0:T(8,128)(2,1)S(1)} %all_to_all.5.in_ref), custom_call_target="tpu_custom_call" | custom-call | bytes 262144 | tf_op jit(solution)/shard_map/pallas_call | solution.py:277
  (1 shorter events, 0.0 us)
Async XLA Ops:
  0.0 26.5 %copy-start = (s32[512,16]{0,1:T(8,128)S(1)}, s32[512,16]{0,1:T(8,128)}, u32[]{:S(2)}) copy-start(s32[512,16]{0,1:T(8,128)} %param.5) | copy-start | bytes 98308
  2.1 28.0 %collective-permute-start.3 = (bf16[2,8,64,128]{3,2,1,0:T(8,128)(2,1)S(1)}, bf16[2,8,64,128]{3,2,1,0:T(8,128)(2,1)S(1)}, u32[]{:S(2)}, u32[]{:S(2)}) collective-permute-start(bf16[2,8,64,128]{3,2,1,0:T(8,128)(2,1)S(1)} %shard_map.37.x4), channel_id=1, source_target_pairs={{0,16},{1,497},{2,18},{3,499},{4,20},{5,501},{6,22},{7,503},{8,24}... | collective-permute-start | bytes 786440 | tf_op jit(solution)/shard_map/ppermute | solution.py:214
  17.0 13.2 %collective-permute-start.2 = (bf16[2,8,64,128]{3,2,1,0:T(8,128)(2,1)S(1)}, bf16[2,8,64,128]{3,2,1,0:T(8,128)(2,1)S(1)}, u32[]{:S(2)}, u32[]{:S(2)}) collective-permute-start(bf16[2,8,64,128]{3,2,1,0:T(8,128)(2,1)S(1)} %shard_map.37.x4), channel_id=1, source_target_pairs={{0,496},{1,17},{2,498},{3,19},{4,500},{5,21},{6,502},{7,23},{8,504... | collective-permute-start | bytes 786440 | tf_op jit(solution)/shard_map/ppermute | solution.py:214
  18.9 12.4 %collective-permute-start.1 = (bf16[2,8,64,128]{3,2,1,0:T(8,128)(2,1)S(1)}, bf16[2,8,64,128]{3,2,1,0:T(8,128)(2,1)S(1)}, u32[]{:S(2)}, u32[]{:S(2)}) collective-permute-start(bf16[2,8,64,128]{3,2,1,0:T(8,128)(2,1)S(1)} %shard_map.37.x4), channel_id=1, source_target_pairs={{0,504},{1,9},{2,506},{3,11},{4,508},{5,13},{6,510},{7,15},{8,16},... | collective-permute-start | bytes 786440 | tf_op jit(solution)/shard_map/ppermute | solution.py:214
  21.5 13.3 %collective-permute-start = (bf16[2,8,64,128]{3,2,1,0:T(8,128)(2,1)S(1)}, bf16[2,8,64,128]{3,2,1,0:T(8,128)(2,1)S(1)}, u32[]{:S(2)}, u32[]{:S(2)}) collective-permute-start(bf16[2,8,64,128]{3,2,1,0:T(8,128)(2,1)S(1)} %shard_map.37.x4), channel_id=1, source_target_pairs={{0,8},{1,505},{2,10},{3,507},{4,12},{5,509},{6,14},{7,511},{8,0},{... | collective-permute-start | bytes 786440 | tf_op jit(solution)/shard_map/ppermute | solution.py:214
  37.1 14.5 %collective-permute-start.7 = (bf16[2,8,64,128]{3,2,1,0:T(8,128)(2,1)S(1)}, bf16[2,8,64,128]{3,2,1,0:T(8,128)(2,1)S(1)}, u32[]{:S(2)}, u32[]{:S(2)}) collective-permute-start(bf16[2,8,64,128]{3,2,1,0:T(8,128)(2,1)S(1)} %get-tuple-element.23.x4), channel_id=1, source_target_pairs={{0,16},{1,497},{2,18},{3,499},{4,20},{5,501},{6,22},{7,503},{8,24}... | collective-permute-start | bytes 786440 | tf_op jit(solution)/shard_map/ppermute | solution.py:214
  42.3 10.7 %collective-permute-start.6 = (bf16[2,8,64,128]{3,2,1,0:T(8,128)(2,1)S(1)}, bf16[2,8,64,128]{3,2,1,0:T(8,128)(2,1)S(1)}, u32[]{:S(2)}, u32[]{:S(2)}) collective-permute-start(bf16[2,8,64,128]{3,2,1,0:T(8,128)(2,1)S(1)} %get-tuple-element.23.x4), channel_id=1, source_target_pairs={{0,496},{1,17},{2,498},{3,19},{4,500},{5,21},{6,502},{7,23},{8,504... | collective-permute-start | bytes 786440 | tf_op jit(solution)/shard_map/ppermute | solution.py:214
  44.2 17.6 %collective-permute-start.5 = (bf16[2,8,64,128]{3,2,1,0:T(8,128)(2,1)S(1)}, bf16[2,8,64,128]{3,2,1,0:T(8,128)(2,1)S(1)}, u32[]{:S(2)}, u32[]{:S(2)}) collective-permute-start(bf16[2,8,64,128]{3,2,1,0:T(8,128)(2,1)S(1)} %get-tuple-element.23.x4), channel_id=1, source_target_pairs={{0,504},{1,9},{2,506},{3,11},{4,508},{5,13},{6,510},{7,15},{8,16},... | collective-permute-start | bytes 786440 | tf_op jit(solution)/shard_map/ppermute | solution.py:214
  48.9 13.3 %collective-permute-start.4 = (bf16[2,8,64,128]{3,2,1,0:T(8,128)(2,1)S(1)}, bf16[2,8,64,128]{3,2,1,0:T(8,128)(2,1)S(1)}, u32[]{:S(2)}, u32[]{:S(2)}) collective-permute-start(bf16[2,8,64,128]{3,2,1,0:T(8,128)(2,1)S(1)} %get-tuple-element.23.x4), channel_id=1, source_target_pairs={{0,8},{1,505},{2,10},{3,507},{4,12},{5,509},{6,14},{7,511},{8,0},{... | collective-permute-start | bytes 786440 | tf_op jit(solution)/shard_map/ppermute | solution.py:214

commit v9 on v7

--- a/solution.py
+++ b/solution.py
@@ -96,7 +96,7 @@
     twice = jnp.where(behind > 1, 1, jnp.where(behind < -1, 1, 0))
     low = twice * (1 - column % 4 // 2) + (1 - twice) * (1 - column % 2)
     plain = 1 - jnp.abs(ahead - low)
-    piece = jnp.where(behind == 0, 4, 2 * twice + plain + odd * (1 - 2 * plain))
+    piece = jnp.where(behind == 0, 4, twice + 2 * (plain + odd * (1 - 2 * plain)))
     place_ref[...] = jnp.where(live, piece, 4) * ROWS + kind
     theirs = jnp.where(line == group * ROWS + kind, 1.0, 0.0).astype(BF16)
     far = jnp.dot(groups, theirs, preferred_element_type=F32)
@@ -214,7 +214,7 @@
 
 
 def surround(block):
-    return [trade(block, distance, shifted) for distance in (1, 2) for shifted in (True, False)] + [block]
+    return [trade(block, distance, shifted) for shifted in (True, False) for distance in (1, 2)] + [block]
 
 
 def local(ground, response, pattern):

time: 74.7 us -> 75.4 us (level)
  waiting for transfers between devices: 13.6 us -> 16.5 us
  blocking collectives: 11.5 us -> 10.3 us
  starting transfers between devices: 37.9 us -> 36.9 us
    ppermute x8, waiting for transfers between devices: 13.6 us -> 16.5 us  [trade(): return lax.ppermute(block, ('col', 'row'), route)]
    all_to_all x1, blocking collectives: 11.5 us -> 10.3 us  [local(): part = lax.all_to_all(part, 'row', 0, 0, tiled=True)]
    ppermute x8, starting transfers between devices: 37.9 us -> 36.9 us  [trade(): return lax.ppermute(block, ('col', 'row'), route)]
where the time goes in v9:
time: 75.4 us; the launch traced here: 75 us
  starting transfers between devices  36.9 us (49%)
  waiting for transfers between devices  16.5 us (22%)
  Pallas kernels  11.1 us (15%)
  blocking collectives  10.3 us (14%)
    ppermute x8, starting transfers between devices, trade(): return lax.ppermute(block, ('col', 'row'), route)  36.9 us
    ppermute x8, waiting for transfers between devices, trade(): return lax.ppermute(block, ('col', 'row'), route)  16.5 us
    all_to_all x1, blocking collectives, local(): part = lax.all_to_all(part, 'row', 0, 0, tiled=True)  10.3 us
    pallas_call x1, Pallas kernels, local(): call(left_body, 'left', (jax.ShapeDtypeStruct((ROWS, 2 * BLK, SLOTS * BLK...  3.55 us
    pallas_call x1, Pallas kernels, local(): call(second_body, 'second', jax.ShapeDtypeStruct((ROWS, BLK, WIDE), BF16)...  2.34 us
    pallas_call x1, Pallas kernels, local(): call(first_body, 'first', (rows, jax.ShapeDtypeStruct((ROWS, BLK, WIDE),...  2.24 us
    pallas_call x1, Pallas kernels, local(): call(slice_body, 'slice', rows, [held, pltpu.VMEM((2, 2, ROWS * HALF, 128...  2.09 us
  transfers between devices with their start and end apart: 8, of which 5 were waited for; matrix products, arithmetic and copies ran while one was open for 0% of the time, Pallas kernels for 5%

profile of v9, /device:TPU:1, one launch (start us, length us, event | category | flops | bytes accessed | tf_op | source)
XLA Modules:
  0.0 75.0 jit_solution(14921923414093101460)
XLA Ops:
  0.0 0.0 copy-start
  0.0 2.1 %shard_map.37.x4 = bf16[2,8,64,128]{3,2,1,0:T(8,128)(2,1)S(1)} custom-call(bf16[8,16,4096]{2,1,0:T(8,128)(2,1)} %ground_hbm.2, bf16[8,16,4096]{2,1,0:T(8,128)(2,1)} %response_hbm.2), custom_call_target="tpu_custom_call" | custom-call | flops 33554432 | bytes 5242880 | tf_op jit(solution)/shard_map/pallas_call | solution.py:228
  2.1 14.8 %collective-permute-start.3 = (bf16[2,8,64,128]{3,2,1,0:T(8,128)(2,1)S(1)}, bf16[2,8,64,128]{3,2,1,0:T(8,128)(2,1)S(1)}, u32[]{:S(2)}, u32[]{:S(2)}) collective-permute-start(bf16[2,8,64,128]{3,2,1,0:T(8,128)(2,1)S(1)} %shard_map.37.x4), channel_id=1, source_target_pairs={{0,16},{1,497},{2,18},{3,499},{4,20},{5,501},{6,22},{7,503},{8,24}... | collective-permute-start | bytes 786440 | tf_op jit(solution)/shard_map/ppermute | solution.py:213
  17.0 1.9 %collective-permute-start.2 = (bf16[2,8,64,128]{3,2,1,0:T(8,128)(2,1)S(1)}, bf16[2,8,64,128]{3,2,1,0:T(8,128)(2,1)S(1)}, u32[]{:S(2)}, u32[]{:S(2)}) collective-permute-start(bf16[2,8,64,128]{3,2,1,0:T(8,128)(2,1)S(1)} %shard_map.37.x4), channel_id=1, source_target_pairs={{0,8},{1,505},{2,10},{3,507},{4,12},{5,509},{6,14},{7,511},{8,0},{... | collective-permute-start | bytes 786440 | tf_op jit(solution)/shard_map/ppermute | solution.py:213
  18.9 3.8 %collective-permute-start.1 = (bf16[2,8,64,128]{3,2,1,0:T(8,128)(2,1)S(1)}, bf16[2,8,64,128]{3,2,1,0:T(8,128)(2,1)S(1)}, u32[]{:S(2)}, u32[]{:S(2)}) collective-permute-start(bf16[2,8,64,128]{3,2,1,0:T(8,128)(2,1)S(1)} %shard_map.37.x4), channel_id=1, source_target_pairs={{0,496},{1,17},{2,498},{3,19},{4,500},{5,21},{6,502},{7,23},{8,504... | collective-permute-start | bytes 786440 | tf_op jit(solution)/shard_map/ppermute | solution.py:213
  22.7 1.9 %collective-permute-start = (bf16[2,8,64,128]{3,2,1,0:T(8,128)(2,1)S(1)}, bf16[2,8,64,128]{3,2,1,0:T(8,128)(2,1)S(1)}, u32[]{:S(2)}, u32[]{:S(2)}) collective-permute-start(bf16[2,8,64,128]{3,2,1,0:T(8,128)(2,1)S(1)} %shard_map.37.x4), channel_id=1, source_target_pairs={{0,504},{1,9},{2,506},{3,11},{4,508},{5,13},{6,510},{7,15},{8,16},... | collective-permute-start | bytes 786440 | tf_op jit(solution)/shard_map/ppermute | solution.py:213
  24.6 0.0 copy-done
  24.7 3.5 %shard_map.38 = (bf16[8,128,1024]{2,1,0:T(8,128)(2,1)S(1)}, s32[1,128]{1,0:T(1,128)S(1)}, bf16[128,16,128]{2,1,0:T(8,128)(2,1)S(1)}, bf16[128,16,128]{2,1,0:T(8,128)(2,1)S(1)}) custom-call(s32[16,512]{1,0:T(8,128)S(1)} %fusion.2.groups_ref, bf16[8,16,4096]{2,1,0:T(8,128)(2,1)} %ground_hbm.2, bf16[8,16,4096]{2,1,0:T(8,128)(2,1)} %response_hbm.2), custom_call_target="tpu_custom_call" | custom-call | flops 536870912 | bytes 5242880 | tf_op jit(solution)/shard_map/pallas_call | solution.py:245
  28.2 0.0 collective-permute-done.3.x3
  28.2 4.7 %collective-permute-done.2.x2 = bf16[2,8,64,128]{3,2,1,0:T(8,128)(2,1)S(1)} collective-permute-done((bf16[2,8,64,128]{3,2,1,0:T(8,128)(2,1)S(1)}, bf16[2,8,64,128]{3,2,1,0:T(8,128)(2,1)S(1)}, u32[]{:S(2)}, u32[]{:S(2)}) %collective-permute-start.2) | collective-permute-done | bytes 262176 | tf_op jit(solution)/shard_map/ppermute | solution.py:213
  33.0 0.0 collective-permute-done.1.x1
  33.0 0.7 collective-permute-done.x0
  33.7 2.2 %shard_map.39 = (bf16[2,8,64,128]{3,2,1,0:T(8,128)(2,1)S(1)}, f32[8,64,128]{2,1,0:T(8,128)S(1)}) custom-call(s32[1,128]{1,0:T(1,128)S(1)} %get-tuple-element.18.where_ref, bf16[128,16,128]{2,1,0:T(8,128)(2,1)S(1)} %get-tuple-element.19.same_ref, bf16[128,16,128]{2,1,0:T(8,128)(2,1)S(1)} %get-tuple-element.20.other_ref, ...), custom_call_target="tpu_custom_call" | custom-call | flops 402653184 | bytes 5242880 | tf_op jit(solution)/shard_map/pallas_call | solution.py:255
  35.9 6.2 %collective-permute-start.7 = (bf16[2,8,64,128]{3,2,1,0:T(8,128)(2,1)S(1)}, bf16[2,8,64,128]{3,2,1,0:T(8,128)(2,1)S(1)}, u32[]{:S(2)}, u32[]{:S(2)}) collective-permute-start(bf16[2,8,64,128]{3,2,1,0:T(8,128)(2,1)S(1)} %get-tuple-element.23.x4), channel_id=1, source_target_pairs={{0,16},{1,497},{2,18},{3,499},{4,20},{5,501},{6,22},{7,503},{8,24}... | collective-permute-start | bytes 786440 | tf_op jit(solution)/shard_map/ppermute | solution.py:213
  42.1 2.0 %collective-permute-start.6 = (bf16[2,8,64,128]{3,2,1,0:T(8,128)(2,1)S(1)}, bf16[2,8,64,128]{3,2,1,0:T(8,128)(2,1)S(1)}, u32[]{:S(2)}, u32[]{:S(2)}) collective-permute-start(bf16[2,8,64,128]{3,2,1,0:T(8,128)(2,1)S(1)} %get-tuple-element.23.x4), channel_id=1, source_target_pairs={{0,8},{1,505},{2,10},{3,507},{4,12},{5,509},{6,14},{7,511},{8,0},{... | collective-permute-start | bytes 786440 | tf_op jit(solution)/shard_map/ppermute | solution.py:213
  44.2 4.3 %collective-permute-start.5 = (bf16[2,8,64,128]{3,2,1,0:T(8,128)(2,1)S(1)}, bf16[2,8,64,128]{3,2,1,0:T(8,128)(2,1)S(1)}, u32[]{:S(2)}, u32[]{:S(2)}) collective-permute-start(bf16[2,8,64,128]{3,2,1,0:T(8,128)(2,1)S(1)} %get-tuple-element.23.x4), channel_id=1, source_target_pairs={{0,496},{1,17},{2,498},{3,19},{4,500},{5,21},{6,502},{7,23},{8,504... | collective-permute-start | bytes 786440 | tf_op jit(solution)/shard_map/ppermute | solution.py:213
  48.5 1.9 %collective-permute-start.4 = (bf16[2,8,64,128]{3,2,1,0:T(8,128)(2,1)S(1)}, bf16[2,8,64,128]{3,2,1,0:T(8,128)(2,1)S(1)}, u32[]{:S(2)}, u32[]{:S(2)}) collective-permute-start(bf16[2,8,64,128]{3,2,1,0:T(8,128)(2,1)S(1)} %get-tuple-element.23.x4), channel_id=1, source_target_pairs={{0,504},{1,9},{2,506},{3,11},{4,508},{5,13},{6,510},{7,15},{8,16},... | collective-permute-start | bytes 786440 | tf_op jit(solution)/shard_map/ppermute | solution.py:213
  50.4 0.0 collective-permute-done.7.x3
  50.4 2.5 %collective-permute-done.6.x2 = bf16[2,8,64,128]{3,2,1,0:T(8,128)(2,1)S(1)} collective-permute-done((bf16[2,8,64,128]{3,2,1,0:T(8,128)(2,1)S(1)}, bf16[2,8,64,128]{3,2,1,0:T(8,128)(2,1)S(1)}, u32[]{:S(2)}, u32[]{:S(2)}) %collective-permute-start.6) | collective-permute-done | bytes 262176 | tf_op jit(solution)/shard_map/ppermute | solution.py:213
  52.9 5.5 %collective-permute-done.5.x1 = bf16[2,8,64,128]{3,2,1,0:T(8,128)(2,1)S(1)} collective-permute-done((bf16[2,8,64,128]{3,2,1,0:T(8,128)(2,1)S(1)}, bf16[2,8,64,128]{3,2,1,0:T(8,128)(2,1)S(1)}, u32[]{:S(2)}, u32[]{:S(2)}) %collective-permute-start.5) | collective-permute-done | bytes 262176 | tf_op jit(solution)/shard_map/ppermute | solution.py:213
  58.4 3.0 %collective-permute-done.4.x0 = bf16[2,8,64,128]{3,2,1,0:T(8,128)(2,1)S(1)} collective-permute-done((bf16[2,8,64,128]{3,2,1,0:T(8,128)(2,1)S(1)}, bf16[2,8,64,128]{3,2,1,0:T(8,128)(2,1)S(1)}, u32[]{:S(2)}, u32[]{:S(2)}) %collective-permute-start.4) | collective-permute-done | bytes 262176 | tf_op jit(solution)/shard_map/ppermute | solution.py:213
  61.4 2.3 %shard_map.40 = bf16[8,64,128]{2,1,0:T(8,128)(2,1)S(1)} custom-call(s32[1,128]{1,0:T(1,128)S(1)} %get-tuple-element.18.where_ref, bf16[128,16,128]{2,1,0:T(8,128)(2,1)S(1)} %get-tuple-element.19.same_ref, bf16[128,16,128]{2,1,0:T(8,128)(2,1)S(1)} %get-tuple-element.20.other_ref, bf16[2,8,64,128]{3,2,1,0:T(8,128)(2,1)S(1)} %collective-permute-done.4.x0, ...), custom_call_target="tpu_custom_call" | custom-call | flops 268435456 | bytes 5242880 | tf_op jit(solution)/shard_map/pallas_call | solution.py:265
  63.8 10.3 %all_to_all.5.in_ref = bf16[8,64,128]{2,1,0:T(8,128)(2,1)S(1)} all-to-all(bf16[8,64,128]{2,1,0:T(8,128)(2,1)S(1)} %shard_map.40), channel_id=1, replica_groups=mesh['col'=64,'row'=8] {'row'}, dimensions={0} | all-to-all | bytes 262144 | tf_op jit(solution)/shard_map/all_to_all | solution.py:274
  74.1 0.9 %shard_map.41 = bf16[1,16,4096]{2,1,0:T(8,128)(2,1)} custom-call(bf16[8,64,128]{2,1,0:T(8,128)(2,1)S(1)} %all_to_all.5.in_ref), custom_call_target="tpu_custom_call" | custom-call | bytes 262144 | tf_op jit(solution)/shard_map/pallas_call | solution.py:275
  (1 shorter events, 0.0 us)
Async XLA Ops:
  0.0 24.6 %copy-start = (s32[512,16]{0,1:T(8,128)S(1)}, s32[512,16]{0,1:T(8,128)}, u32[]{:S(2)}) copy-start(s32[512,16]{0,1:T(8,128)} %param.5) | copy-start | bytes 98308
  2.1 26.1 %collective-permute-start.3 = (bf16[2,8,64,128]{3,2,1,0:T(8,128)(2,1)S(1)}, bf16[2,8,64,128]{3,2,1,0:T(8,128)(2,1)S(1)}, u32[]{:S(2)}, u32[]{:S(2)}) collective-permute-start(bf16[2,8,64,128]{3,2,1,0:T(8,128)(2,1)S(1)} %shard_map.37.x4), channel_id=1, source_target_pairs={{0,16},{1,497},{2,18},{3,499},{4,20},{5,501},{6,22},{7,503},{8,24}... | collective-permute-start | bytes 786440 | tf_op jit(solution)/shard_map/ppermute | solution.py:213
  17.0 16.0 %collective-permute-start.2 = (bf16[2,8,64,128]{3,2,1,0:T(8,128)(2,1)S(1)}, bf16[2,8,64,128]{3,2,1,0:T(8,128)(2,1)S(1)}, u32[]{:S(2)}, u32[]{:S(2)}) collective-permute-start(bf16[2,8,64,128]{3,2,1,0:T(8,128)(2,1)S(1)} %shard_map.37.x4), channel_id=1, source_target_pairs={{0,8},{1,505},{2,10},{3,507},{4,12},{5,509},{6,14},{7,511},{8,0},{... | collective-permute-start | bytes 786440 | tf_op jit(solution)/shard_map/ppermute | solution.py:213
  18.9 14.1 %collective-permute-start.1 = (bf16[2,8,64,128]{3,2,1,0:T(8,128)(2,1)S(1)}, bf16[2,8,64,128]{3,2,1,0:T(8,128)(2,1)S(1)}, u32[]{:S(2)}, u32[]{:S(2)}) collective-permute-start(bf16[2,8,64,128]{3,2,1,0:T(8,128)(2,1)S(1)} %shard_map.37.x4), channel_id=1, source_target_pairs={{0,496},{1,17},{2,498},{3,19},{4,500},{5,21},{6,502},{7,23},{8,504... | collective-permute-start | bytes 786440 | tf_op jit(solution)/shard_map/ppermute | solution.py:213
  22.7 11.0 %collective-permute-start = (bf16[2,8,64,128]{3,2,1,0:T(8,128)(2,1)S(1)}, bf16[2,8,64,128]{3,2,1,0:T(8,128)(2,1)S(1)}, u32[]{:S(2)}, u32[]{:S(2)}) collective-permute-start(bf16[2,8,64,128]{3,2,1,0:T(8,128)(2,1)S(1)} %shard_map.37.x4), channel_id=1, source_target_pairs={{0,504},{1,9},{2,506},{3,11},{4,508},{5,13},{6,510},{7,15},{8,16},... | collective-permute-start | bytes 786440 | tf_op jit(solution)/shard_map/ppermute | solution.py:213
  35.9 14.4 %collective-permute-start.7 = (bf16[2,8,64,128]{3,2,1,0:T(8,128)(2,1)S(1)}, bf16[2,8,64,128]{3,2,1,0:T(8,128)(2,1)S(1)}, u32[]{:S(2)}, u32[]{:S(2)}) collective-permute-start(bf16[2,8,64,128]{3,2,1,0:T(8,128)(2,1)S(1)} %get-tuple-element.23.x4), channel_id=1, source_target_pairs={{0,16},{1,497},{2,18},{3,499},{4,20},{5,501},{6,22},{7,503},{8,24}... | collective-permute-start | bytes 786440 | tf_op jit(solution)/shard_map/ppermute | solution.py:213
  42.1 10.8 %collective-permute-start.6 = (bf16[2,8,64,128]{3,2,1,0:T(8,128)(2,1)S(1)}, bf16[2,8,64,128]{3,2,1,0:T(8,128)(2,1)S(1)}, u32[]{:S(2)}, u32[]{:S(2)}) collective-permute-start(bf16[2,8,64,128]{3,2,1,0:T(8,128)(2,1)S(1)} %get-tuple-element.23.x4), channel_id=1, source_target_pairs={{0,8},{1,505},{2,10},{3,507},{4,12},{5,509},{6,14},{7,511},{8,0},{... | collective-permute-start | bytes 786440 | tf_op jit(solution)/shard_map/ppermute | solution.py:213
  44.2 14.2 %collective-permute-start.5 = (bf16[2,8,64,128]{3,2,1,0:T(8,128)(2,1)S(1)}, bf16[2,8,64,128]{3,2,1,0:T(8,128)(2,1)S(1)}, u32[]{:S(2)}, u32[]{:S(2)}) collective-permute-start(bf16[2,8,64,128]{3,2,1,0:T(8,128)(2,1)S(1)} %get-tuple-element.23.x4), channel_id=1, source_target_pairs={{0,496},{1,17},{2,498},{3,19},{4,500},{5,21},{6,502},{7,23},{8,504... | collective-permute-start | bytes 786440 | tf_op jit(solution)/shard_map/ppermute | solution.py:213
  48.5 13.0 %collective-permute-start.4 = (bf16[2,8,64,128]{3,2,1,0:T(8,128)(2,1)S(1)}, bf16[2,8,64,128]{3,2,1,0:T(8,128)(2,1)S(1)}, u32[]{:S(2)}, u32[]{:S(2)}) collective-permute-start(bf16[2,8,64,128]{3,2,1,0:T(8,128)(2,1)S(1)} %get-tuple-element.23.x4), channel_id=1, source_target_pairs={{0,504},{1,9},{2,506},{3,11},{4,508},{5,13},{6,510},{7,15},{8,16},... | collective-permute-start | bytes 786440 | tf_op jit(solution)/shard_map/ppermute | solution.py:213
